TPU v7x, 256 devices: a whole 4x4x8 slice. The times are simulated.
256 devices in a mesh: chan: 16 (over x, y), tm: 16 (over z, core).
Axes of the slice: x: 4, y: 4, z: 8, core: 2. Of those that a mesh axis runs over, the one named last changes fastest.
Arguments:
- raw_strain: bfloat16 [256, 262144], P('chan', 'tm'), may hold values from -60 to 60
- fir_taps: bfloat16 [8, 128], replicated, may hold values from -0.5 to 0.5
- start_basis: float32 [8, 256, 32], replicated, may hold values from -6 to 6
Outputs:
- denoised: float32 [8, 256, 65536], P(None, 'chan', 'tm')
All inputs are finite; a program needn't handle non-finite values.
Results may differ from a plain program's by a relative error of at most 0.0003.
Values may be sent and summed in bfloat16 or wider, within the bound.
No kernel may reach another device: no remote copies, remote signals or barrier semaphores. Data moves between devices by JAX's collectives and lax.ppermute only.
A program may use at most 192 MiB of HBM per device.

v0:
```python
import jax
import jax.numpy as jnp
from jax import lax
from jax.sharding import PartitionSpec as P

ITERS = 3


def shifted(block, axis, distance):
    devices = range(lax.axis_size(axis))
    route = [(i - distance, i) for i in devices if i - distance in devices]
    return lax.ppermute(block, axis, route)


def toeplitz(fir_taps, window):
    band_count, tap_count = fir_taps.shape
    padded_taps = jnp.concatenate(
        [
            jnp.zeros((band_count, 4), fir_taps.dtype),
            fir_taps,
            jnp.zeros((band_count, window - tap_count), fir_taps.dtype),
        ],
        axis=1,
    )
    tiled_rows = jnp.tile(padded_taps, (1, 128))[:, : 128 * window].reshape(band_count, 128, window)
    return jnp.transpose(tiled_rows, (2, 0, 1)).reshape(window, band_count * 128)


def decimate(raw_strain, before, fir_taps):
    channels, samples = raw_strain.shape
    band_count, tap_count = fir_taps.shape
    blocks = samples // 512
    toeplitz_table = toeplitz(fir_taps, 512 + tap_count)
    extended = jnp.concatenate([before, raw_strain], axis=1)
    leading = extended[:, :samples].reshape(channels, blocks, 512)
    trailing = raw_strain.reshape(channels, blocks, 512)[:, :, 512 - tap_count :]
    filtered = jnp.dot(leading, toeplitz_table[:512], preferred_element_type=jnp.float32)
    filtered = filtered + jnp.dot(
        trailing, toeplitz_table[512:], preferred_element_type=jnp.float32
    )
    filtered = filtered.reshape(channels, blocks, band_count, 128)
    return jnp.transpose(filtered, (2, 0, 1, 3)).reshape(band_count, channels, blocks * 128)


def orthonormal(image):
    compact = jnp.einsum("bik,bil->bkl", image, image, precision=lax.Precision.HIGHEST)
    lower_small = jnp.linalg.cholesky(compact)
    return lax.linalg.triangular_solve(
        lower_small, image, left_side=False, lower=True, transpose_a=True
    )


def refine(gram_matrix, subspace):
    for number in range(ITERS):
        image = jnp.einsum("bij,bjk->bik", gram_matrix, subspace, precision=lax.Precision.HIGHEST)
        subspace = orthonormal(image)
    return subspace


def shards(raw_strain, fir_taps, start_basis):
    rim_piece = raw_strain[:, raw_strain.shape[1] - fir_taps.shape[1] :]
    before = shifted(rim_piece, "tm", 1)
    own_count = raw_strain.shape[0]
    offset = lax.axis_index("chan") * own_count
    decimated = decimate(raw_strain, before, fir_taps)
    gathered = lax.all_gather(decimated, "chan", axis=1, tiled=True)
    local_gram = jnp.einsum("bct,bdt->bcd", gathered, gathered, precision=lax.Precision.HIGHEST)
    total_gram = lax.psum(local_gram, "tm")
    subspace = refine(total_gram, start_basis)
    own_basis = lax.dynamic_slice_in_dim(subspace, offset, own_count, 1)
    projected = jnp.einsum("bck,bct->bkt", subspace, gathered, precision=lax.Precision.HIGHEST)
    return jnp.einsum("bck,bkt->bct", own_basis, projected, precision=lax.Precision.HIGHEST)


def solution(mesh):
    placed = (P("chan", "tm"), P(), P())
    return jax.shard_map(
        shards, mesh=mesh, in_specs=placed, out_specs=P(None, "chan", "tm"), check_vma=False
    )
```

profile of v0, /device:TPU:1, one launch (start us, length us, event | category | flops | bytes accessed | tf_op | source)
XLA Modules:
  0.0 557.3 jit_solution(4502102348403562086)
XLA Ops:
  6.5 0.7 slice.30
  7.3 4.9 collective-permute-start
  12.3 0.8 maximum_maximum_fusion
  13.1 0.1 tile.4
  13.2 2.8 reshape.51
  15.9 1.4 tile.10
  17.4 0.1 slice.38
  17.5 0.2 copy.39
  17.7 0.8 copy-done.2
  18.5 0.2 copy.36
  18.7 0.4 fusion
  19.1 0.1 slice.39
  19.3 0.2 copy.34
  19.4 0.7 bitcast_add_fusion
  20.2 0.5 copy.37
  20.6 0.2 bitcast_bitcast_fusion
  20.8 0.4 copy.20
  21.3 1.5 reshape.38
  22.8 0.2 all-reduce.2.cloned.1.call-start
  23.0 203.6 %all-gather.2.cloned.1.call-done = f32[8,256,4096]{2,1,0:T(8,128)} async-done(((f32[8,16,4096]{2,1,0:T(8,128)}), f32[8,256,4096]{2,1,0:T(8,128)}) %all-gather.2.cloned.1.call-update) | async-done | bytes 33554448 | tf_op jit(solution)/shard_map/all_gather | solution.py:66
  226.6 36.9 %fusion.11 = f32[8,256,256]{2,1,0:T(8,128)} fusion(f32[8,256,4096]{2,1,0:T(8,128)} %all-gather.2.cloned.1.call-done), kind=kOutput, calls=%fused_computation.33 | convolution fusion | flops 25769803776 | bytes 35651584 | tf_op jit(solution)/shard_map/bct,bdt->bcd/dot_general | solution.py:67
  263.5 114.6 %all-reduce.2.cloned.1.call-done = f32[8,256,256]{2,1,0:T(8,128)} async-done(((f32[8,256,256]{2,1,0:T(8,128)}), f32[8,256,256]{2,1,0:T(8,128)}) %all-reduce.2.cloned.1.call-update) | async-done | bytes 2097168 | tf_op jit(solution)/shard_map/psum | solution.py:68
  378.1 3.8 fusion.12
  381.9 0.3 fusion.13
  382.2 0.1 copy.21
  382.3 23.4 %custom-call.10 = f32[8,32,32]{2,1,0:T(8,128)S(1)} custom-call(f32[8,32,32]{2,1,0:T(8,128)S(1)} %fusion.7), custom_call_target="Cholesky" | custom-call | tf_op jit(solution)/shard_map/jit(cholesky)/cholesky | solution.py:47
  405.8 0.1 compare_reduce_fusion.2
  405.9 0.1 select_bitcast_fusion.2
  406.0 19.7 %custom-call.11 = f32[8,1,32,32]{2,3,1,0:T(8,128)S(1)} custom-call(f32[8,1,32,32]{3,2,1,0:T(8,128)S(1)} %select_bitcast_fusion.2), custom_call_target="InvertDiagBlocksLowerTriangular" | custom-call | tf_op jit(solution)/shard_map/triangular_solve/custom-call.0 | solution.py:48
  425.7 0.4 convolution_bitcast_fusion.2
  426.2 2.0 fusion.14
  428.2 0.3 fusion.15
  428.6 0.1 copy.23
  428.7 23.4 %custom-call.12 = f32[8,32,32]{2,1,0:T(8,128)S(1)} custom-call(f32[8,32,32]{2,1,0:T(8,128)S(1)} %fusion.5), custom_call_target="Cholesky" | custom-call | tf_op jit(solution)/shard_map/jit(cholesky)/cholesky | solution.py:47
  452.2 0.1 compare_reduce_fusion.1
  452.3 0.1 select_bitcast_fusion.1
  452.4 19.9 %custom-call.13 = f32[8,1,32,32]{2,3,1,0:T(8,128)S(1)} custom-call(f32[8,1,32,32]{3,2,1,0:T(8,128)S(1)} %select_bitcast_fusion.1), custom_call_target="InvertDiagBlocksLowerTriangular" | custom-call | tf_op jit(solution)/shard_map/triangular_solve/custom-call.0 | solution.py:48
  472.3 0.4 convolution_bitcast_fusion.1
  472.8 2.0 fusion.16
  474.8 0.3 fusion.17
  475.2 0.1 copy.25
  475.3 23.4 %custom-call.14 = f32[8,32,32]{2,1,0:T(8,128)S(1)} custom-call(f32[8,32,32]{2,1,0:T(8,128)S(1)} %fusion.3), custom_call_target="Cholesky" | custom-call | tf_op jit(solution)/shard_map/jit(cholesky)/cholesky | solution.py:47
  498.8 0.1 compare_reduce_fusion
  498.9 0.1 select_bitcast_fusion
  499.0 19.7 %custom-call.15 = f32[8,1,32,32]{2,3,1,0:T(8,128)S(1)} custom-call(f32[8,1,32,32]{3,2,1,0:T(8,128)S(1)} %select_bitcast_fusion), custom_call_target="InvertDiagBlocksLowerTriangular" | custom-call | tf_op jit(solution)/shard_map/triangular_solve/custom-call.0 | solution.py:48
  518.7 0.4 convolution_bitcast_fusion
  519.1 26.3 %fusion.18 = f32[8,32,4096]{2,1,0:T(8,128)} fusion(f32[8,256,32]{1,2,0:T(8,128)S(1)} %convolution_bitcast_fusion, f32[8,256,4096]{2,1,0:T(8,128)} %all-gather.2.cloned.1.call-done), kind=kOutput, calls=%fused_computation.40 | convolution fusion | flops 3221225472 | bytes 38010880 | tf_op jit(solution)/shard_map/bck,bct->bkt/dot_general | solution.py:71
  545.5 5.0 fusion.8
  (23 shorter events, 0.4 us)
Async XLA Ops:
  6.5 371.6 %copy-start = (f32[8,256,32]{1,2,0:T(8,128)S(1)}, f32[8,256,32]{1,2,0:T(8,128)}, u32[]{:S(2)}) copy-start(f32[8,256,32]{1,2,0:T(8,128)} %param.8) | copy-start | bytes 786436
  6.5 220.1 %all-gather.2.cloned.1.call-start = ((), (), s32[]{:S(2)}) async-start(), calls=%async_computation | async-start | bytes 35651584 | tf_op jit(solution)/shard_map/all_gather | solution.py:66
  7.3 11.9 %collective-permute-start = (bf16[16,128]{1,0:T(8,128)(2,1)S(1)}, bf16[16,128]{1,0:T(8,128)(2,1)S(1)}, u32[]{:S(2)}, u32[]{:S(2)}) collective-permute-start(bf16[16,128]{1,0:T(8,128)(2,1)S(1)} %slice.30), channel_id=1, source_target_pairs={{0,1},{1,2},{2,3},{3,4},{4,5},{5,6},{6,7},{7,8},{8,9},{9,10},{10,1... | collective-permute-start | bytes 12296 | tf_op jit(solution)/shard_map/ppermute | solution.py:12
  17.5 1.0 copy-start.2
  22.8 355.3 %all-reduce.2.cloned.1.call-start = ((), (), s32[]{:S(2)}) async-start(), calls=%async_computation.1 | async-start | bytes 4194304 | tf_op jit(solution)/shard_map/psum | solution.py:68
  378.1 48.1 %copy-start.1 = (f32[8,256,256]{2,1,0:T(8,128)S(1)}, f32[8,256,256]{2,1,0:T(8,128)}, u32[]{:S(2)}) copy-start(f32[8,256,256]{2,1,0:T(8,128)} %all-reduce.2.cloned.1.call-done) | copy-start | bytes 6291460
Sparse Core Ops, SparseCore 0:
  22.9 203.6 all-gather.1
  263.6 114.4 all-reduce.1
where the time goes:
time: 557 us
  waiting for transfers between devices  318 us (57%)
  other arithmetic  131 us (24%)
  matrix products  79.5 us (14%)
  between operations  13.7 us (2%)
  local copies, waits for them, and re-layouts  9.5 us (2%)
    all_gather x1, waiting for transfers between devices, shards(): gathered = lax.all_gather(decimated, 'chan', axis=1, tiled=True)  204 us
    psum x1, waiting for transfers between devices, shards(): total_gram = lax.psum(local_gram, 'tm')  115 us
    another operation x10, other arithmetic, orthonormal(): lower_small = jnp.linalg.cholesky(compact)  70.8 us
    another operation x7, other arithmetic, orthonormal(): lax.linalg.triangular_solve(lower_small, image, left_side=False, lower=Tr...  59.6 us
    dot_general x1, matrix products, shards(): jnp.einsum('bct,bdt->bcd', gathered, gathered, precision=lax.Precision.HI...  36.9 us
    dot_general x1, matrix products, shards(): jnp.einsum('bck,bct->bkt', subspace, gathered, precision=lax.Precision.HI...  26.3 us
  transfers between devices with their start and end apart: 3, of which 2 were waited for; matrix products, arithmetic and copies ran while one was open for 1% of the time, Pallas kernels for 0%

commit v1 on v0

v1 whole, which is shorter than its diff:
```python
import jax
import jax.numpy as jnp
from jax import lax
from jax.experimental import pallas as pl
from jax.experimental.pallas import tpu as pltpu
from jax.sharding import PartitionSpec as P

ITERS = 3
RIM = 128
STEP = 512
WINDOW = STEP + RIM
HIGHEST = lax.Precision.HIGHEST
VMEM_LIMIT = 40 * 1024 * 1024


def swapped(block, axis, distance):
    route = [(i, i ^ distance) for i in range(lax.axis_size(axis))]
    return lax.ppermute(block, axis, route)


def dot_nt(a, b, precision=None):
    return lax.dot_general(
        a, b, (((1,), (1,)), ((), ())), precision=precision, preferred_element_type=jnp.float32
    )


def halves(value):
    high = value.astype(jnp.bfloat16)
    return high, (value - high.astype(jnp.float32)).astype(jnp.bfloat16)


def gram_kernel(x_ref, taps_ref, gram_ref, table_ref):
    taps = taps_ref[0].astype(jnp.float32)
    row = jnp.concatenate([taps, jnp.zeros((1, STEP), jnp.float32)], axis=1)
    table = pltpu.roll(jnp.broadcast_to(row, (128, WINDOW)), 4, 1, stride=4, stride_axis=0)
    table = table.astype(jnp.bfloat16)
    table_ref[0] = table
    pieces = [
        dot_nt(x_ref[:, first : first + WINDOW], table)
        for first in range(0, x_ref.shape[1] - RIM, STEP)
    ]
    high, low = halves(jnp.concatenate(pieces, axis=1))
    gram_ref[0] = dot_nt(high, high) + dot_nt(high, low) + dot_nt(low, high)


def decimated_gram(windows, fir_taps):
    channels, samples = windows.shape
    bands = fir_taps.shape[0]
    return pl.pallas_call(
        gram_kernel,
        grid=(bands,),
        in_specs=[
            pl.BlockSpec((channels, samples), lambda b: (0, 0)),
            pl.BlockSpec((1, 1, RIM), lambda b: (b, 0, 0)),
        ],
        out_specs=[
            pl.BlockSpec((1, channels, channels), lambda b: (b, 0, 0)),
            pl.BlockSpec((1, 128, WINDOW), lambda b: (b, 0, 0)),
        ],
        out_shape=[
            jax.ShapeDtypeStruct((bands, channels, channels), jnp.float32),
            jax.ShapeDtypeStruct((bands, 128, WINDOW), jnp.bfloat16),
        ],
        compiler_params=pltpu.CompilerParams(vmem_limit_bytes=VMEM_LIMIT),
        name="decimated_gram",
    )(windows, fir_taps[:, None, :])


def inverse_cholesky(compact):
    rank = compact.shape[0]
    rows = lax.broadcasted_iota(jnp.int32, (rank, rank), 0)
    columns = lax.broadcasted_iota(jnp.int32, (rank, rank), 1)
    unit = (rows == columns).astype(jnp.float32)
    both = jnp.concatenate([compact, unit], axis=1)
    below = lax.broadcasted_iota(jnp.int32, (rank, 1), 0)
    for j in range(rank - 1):
        factor = jnp.where(below > j, both[:, j : j + 1], 0.0) / both[j : j + 1, j : j + 1]
        both = both - factor * both[j : j + 1, :]
    pivots = jnp.sum(unit * both[:, :rank], axis=1, keepdims=True)
    return both[:, rank:] / jnp.sqrt(pivots)


def refine_kernel(half_ref, gram_ref, start_ref, out_ref, basis_ref):
    basis = start_ref[...]
    for _ in range(ITERS):
        image = jnp.dot(gram_ref[...], basis, precision=HIGHEST, preferred_element_type=jnp.float32)
        compact = lax.dot_general(
            image,
            image,
            (((0,), (0,)), ((), ())),
            precision=HIGHEST,
            preferred_element_type=jnp.float32,
        )
        basis = dot_nt(image, inverse_cholesky(compact), HIGHEST)
    basis_ref[...] = basis
    count = out_ref.shape[1]
    part = basis_ref[pl.ds(pl.multiple_of(half_ref[0] * count, count), count), :]
    out_ref[...] = dot_nt(basis, part, HIGHEST)


def projector_half(half, gram_matrix, start):
    channels = gram_matrix.shape[0]
    return pl.pallas_call(
        refine_kernel,
        in_specs=[
            pl.BlockSpec(memory_space=pltpu.SMEM),
            pl.BlockSpec(memory_space=pltpu.VMEM),
            pl.BlockSpec(memory_space=pltpu.VMEM),
        ],
        out_specs=pl.BlockSpec(memory_space=pltpu.VMEM),
        out_shape=jax.ShapeDtypeStruct((channels, channels // 2), jnp.float32),
        scratch_shapes=[pltpu.VMEM(start.shape, jnp.float32)],
        compiler_params=pltpu.CompilerParams(vmem_limit_bytes=VMEM_LIMIT),
        name="projector_half",
    )(half.reshape(1), gram_matrix, start)


def denoise_kernel(x_ref, rim_ref, projector_ref, table_ref, out_ref, mixed_ref):
    bands, own, count = out_ref.shape
    sources, _, samples = x_ref.shape
    rows = bands * own
    projector = jnp.concatenate(
        [
            jnp.concatenate([projector_ref[2 * b], projector_ref[2 * b + 1]], axis=1)
            for b in range(bands)
        ],
        axis=0,
    )
    stacked = jnp.concatenate(halves(projector), axis=0)

    def mix(x, first):
        both = jnp.dot(stacked, x, preferred_element_type=jnp.float32)
        high, low = halves(both[:rows] + both[rows:])
        mixed_ref[:rows, first : first + x.shape[1]] = high
        mixed_ref[rows:, first : first + x.shape[1]] = low

    for first in range(0, samples, STEP):
        mix(x_ref[:, :, first : first + STEP].reshape(sources * own, STEP), first)
    mix(rim_ref[...].reshape(sources * own, RIM), samples)
    blocks = count // 128
    for b in range(bands):
        windows = [
            mixed_ref[part + b * own : part + (b + 1) * own, STEP * m : STEP * m + WINDOW]
            for part in (0, rows)
            for m in range(blocks)
        ]
        both = dot_nt(jnp.concatenate(windows, axis=0), table_ref[b])
        result = both[: blocks * own] + both[blocks * own :]
        for m in range(blocks):
            out_ref[b, :, 128 * m : 128 * m + 128] = result[m * own : (m + 1) * own]


def denoise(gathered, projector, table):
    sources, own, extended = gathered.shape
    bands = table.shape[0]
    samples = 4096
    steps = (extended - RIM) // samples
    return pl.pallas_call(
        denoise_kernel,
        grid=(steps,),
        in_specs=[
            pl.BlockSpec((sources, own, samples), lambda i: (0, 0, i)),
            pl.BlockSpec((sources, own, RIM), lambda i: (0, 0, (i + 1) * (samples // RIM))),
            pl.BlockSpec(projector.shape, lambda i: (0, 0, 0)),
            pl.BlockSpec(table.shape, lambda i: (0, 0, 0)),
        ],
        out_specs=pl.BlockSpec((bands, own, samples // 4), lambda i: (0, 0, i)),
        out_shape=jax.ShapeDtypeStruct((bands, own, steps * samples // 4), jnp.float32),
        scratch_shapes=[pltpu.VMEM((2 * bands * own, samples + RIM), jnp.bfloat16)],
        compiler_params=pltpu.CompilerParams(vmem_limit_bytes=VMEM_LIMIT),
        name="denoise",
    )(gathered, gathered, projector, table)


def shards(raw_strain, fir_taps, start_basis):
    own, samples = raw_strain.shape
    bands = fir_taps.shape[0]
    chan_count, tm_count = lax.axis_size("chan"), lax.axis_size("tm")
    channels = own * chan_count
    place, core = lax.axis_index("chan"), lax.axis_index("tm") % 2
    rim_piece = raw_strain[:, samples - RIM :]
    before = lax.ppermute(rim_piece, "tm", [(i, i + 1) for i in range(tm_count - 1)])
    extended = jnp.concatenate([before, raw_strain], axis=1)
    gathered = lax.all_gather(extended, "chan", axis=0)

    part = samples // chan_count
    windows = jnp.stack(
        [extended[:, part * i : part * i + part + RIM] for i in range(chan_count)], axis=0
    )
    windows = lax.all_to_all(windows, "chan", 0, 0, tiled=True)
    local_gram, table = decimated_gram(windows.reshape(channels, part + RIM), fir_taps)

    local_gram = local_gram.reshape(bands, 2, channels // 2, channels)
    sent = swapped(lax.dynamic_index_in_dim(local_gram, 1 - core, 1, False), "tm", 1)
    summed = lax.dynamic_index_in_dim(local_gram, core, 1, False) + sent
    quarters = summed.reshape(chan_count, channels // 4, channels)
    quarter = jnp.sum(lax.all_to_all(quarters, "chan", 0, 0, tiled=True), axis=0)
    distance = 2
    while distance < tm_count:
        quarter = quarter + swapped(quarter, "tm", distance)
        distance *= 2

    other = swapped(quarter, "tm", 1)
    pair = jnp.where(core == 0, jnp.stack([quarter, other]), jnp.stack([other, quarter]))
    other = swapped(pair, "chan", 1)
    half = place % 2
    four = jnp.where(half == 0, jnp.stack([pair, other], 1), jnp.stack([other, pair], 1))
    start = lax.dynamic_index_in_dim(start_basis, place // 2, 0, False)
    projector = projector_half(half, four.reshape(channels, channels), start)

    projector = projector.reshape(chan_count, own, channels // 2)
    projector = lax.all_to_all(projector, "chan", 0, 0, tiled=True)
    return denoise(gathered, projector, table)


def solution(mesh):
    placed = (P("chan", "tm"), P(), P())
    return jax.shard_map(
        shards, mesh=mesh, in_specs=placed, out_specs=P(None, "chan", "tm"), check_vma=False
    )
```

time: 557 us -> 166 us (0.30)
  waiting for transfers between devices: 318 us -> 29.5 us
  other arithmetic: 131 us -> 1.5 us
  matrix products: 79.5 us -> 0 us
  blocking collectives: 0 us -> 42.1 us
  Pallas kernels: 0 us -> 26.3 us
  starting transfers between devices: 5.15 us -> 28.3 us
  local copies, waits for them, and re-layouts: 9.5 us -> 23.7 us
    all_gather x1, waiting for transfers between devices: 204 us -> 0.01 us  [shards(): gathered = lax.all_gather(extended, 'chan', axis=0)]
    another operation x17 -> x0, other arithmetic: 130 us -> none  [the longest x10 70.8 us: orthonormal(): lower_small = jnp.linalg.cholesky(compact)]
    psum x1 -> x0, waiting for transfers between devices: 115 us -> none  [shards(): total_gram = lax.psum(local_gram, 'tm')]
    dot_general x11 -> x0, matrix products: 78.2 us -> none  [the longest x1 36.9 us: shards(): jnp.einsum('bct,bdt->bcd', gathered, gathered, precision=lax.Precision.HI...]
    all_to_all x0 -> x2, blocking collectives: none -> 42.1 us  [the longest x1 30.2 us: shards(): lax.all_to_all(quarters, 'chan', 0, 0, tiled=True)]
    pallas_call x0 -> x3, Pallas kernels: none -> 26.3 us  [the longest x1 11.6 us: projector_half(): pl.pallas_call(refine_kernel, in_specs=[pl.BlockSpec(memory_space=pltpu.S...]
    ppermute x1 -> x7, starting transfers between devices: 4.92 us -> 21.6 us  [the longest x6 16.7 us: swapped(): return lax.ppermute(block, axis, route)]
    unnamed x11 -> x30, local copies, waits for them, and re-layouts: 4.52 us -> 19.9 us
  transfers between devices with their start and end apart: 3 -> 9, of which waited for: 2 -> 8; matrix products, arithmetic and copies ran while one was open for 1% -> 11% of each run, Pallas kernels for 0% -> 11%
where the time goes in v1:
time: 166 us; the launch traced here: 165 us
  blocking collectives  42.1 us (25%)
  waiting for transfers between devices  29.5 us (18%)
  starting transfers between devices  28.3 us (17%)
  Pallas kernels  26.3 us (16%)
  local copies, waits for them, and re-layouts  23.7 us (14%)
  between operations  13.5 us (8%)
    all_to_all x1, blocking collectives, shards(): lax.all_to_all(quarters, 'chan', 0, 0, tiled=True)  30.2 us
    unnamed x30, local copies, waits for them, and re-layouts  19.9 us
    ppermute x6, starting transfers between devices, swapped(): return lax.ppermute(block, axis, route)  16.7 us
    all_to_all x1, waiting for transfers between devices, shards(): windows = lax.all_to_all(windows, 'chan', 0, 0, tiled=True)  14.7 us
    ppermute x6, waiting for transfers between devices, swapped(): return lax.ppermute(block, axis, route)  14 us
    all_to_all x1, blocking collectives, shards(): projector = lax.all_to_all(projector, 'chan', 0, 0, tiled=True)  11.9 us
    pallas_call x1, Pallas kernels, projector_half(): pl.pallas_call(refine_kernel, in_specs=[pl.BlockSpec(memory_space=pltpu.S...  11.6 us
    pallas_call x1, Pallas kernels, denoise(): pl.pallas_call(denoise_kernel, grid=(steps,), in_specs=[pl.BlockSpec((sou...  7.78 us
  transfers between devices with their start and end apart: 9, of which 8 were waited for; matrix products, arithmetic and copies ran while one was open for 11% of the time, Pallas kernels for 11%

profile of v1, /device:TPU:1, one launch (start us, length us, event | category | flops | bytes accessed | tf_op | source)
XLA Modules:
  0.0 164.9 jit_solution(12292754748790913065)
XLA Ops:
  6.5 0.8 slice.51
  7.3 4.9 %collective-permute-start = (bf16[16,128]{1,0:T(8,128)(2,1)S(1)}, bf16[16,128]{1,0:T(8,128)(2,1)S(1)}, u32[]{:S(2)}, u32[]{:S(2)}) collective-permute-start(bf16[16,128]{1,0:T(8,128)(2,1)S(1)} %slice.51), channel_id=1, source_target_pairs={{0,1},{1,2},{2,3},{3,4},{4,5},{5,6},{6,7},{7,8},{8,9},{9,10},{10,1... | collective-permute-start | bytes 12296 | tf_op jit(solution)/shard_map/ppermute | solution.py:182
  12.2 0.7 collective-permute-done
  13.0 1.1 constant_dynamic-update-slice_fusion
  14.1 0.8 copy-done.5
  14.9 0.0 all-gather.3.cloned.1.call-update
  14.9 1.4 constant_dynamic-update-slice_fusion.17
  16.3 1.4 constant_dynamic-update-slice_fusion.16
  17.7 1.4 constant_dynamic-update-slice_fusion.15
  19.0 1.4 constant_dynamic-update-slice_fusion.14
  20.4 1.4 constant_dynamic-update-slice_fusion.13
  21.8 1.4 constant_dynamic-update-slice_fusion.12
  23.2 1.4 constant_dynamic-update-slice_fusion.11
  24.6 0.6 constant_dynamic-update-slice_fusion.10
  25.2 0.6 constant_dynamic-update-slice_fusion.9
  25.8 0.6 constant_dynamic-update-slice_fusion.8
  26.4 0.6 constant_dynamic-update-slice_fusion.7
  27.1 0.6 constant_dynamic-update-slice_fusion.6
  27.7 0.6 constant_dynamic-update-slice_fusion.5
  28.3 0.6 constant_dynamic-update-slice_fusion.4
  28.9 0.6 constant_dynamic-update-slice_fusion.3
  29.5 0.6 constant_dynamic-update-slice_fusion.2
  30.2 6.8 %all-to-all-start = ((bf16[16,16,1152]{2,1,0:T(8,128)(2,1)}), bf16[16,16,1152]{2,1,0:T(8,128)(2,1)S(1)}, u32[]{:S(2)}, u32[]{:S(2)}) async-start(bf16[16,16,1152]{2,1,0:T(8,128)(2,1)} %constant_dynamic-update-slice_fusion.2), calls=%async_computation | async-start | bytes 1179648 | tf_op jit(solution)/shard_map/all_to_all | solution.py:190
  37.0 14.7 %all-to-all-done = bf16[16,16,1152]{2,1,0:T(8,128)(2,1)S(1)} async-done(((bf16[16,16,1152]{2,1,0:T(8,128)(2,1)}), bf16[16,16,1152]{2,1,0:T(8,128)(2,1)S(1)}, u32[]{:S(2)}, u32[]{:S(2)}) %all-to-all-start) | async-done | bytes 589856 | tf_op jit(solution)/shard_map/all_to_all | solution.py:190
  51.7 6.9 %decimated_gram.1 = (f32[8,256,256]{2,1,0:T(8,128)S(1)}, bf16[8,128,640]{2,1,0:T(8,128)(2,1)S(1)}) custom-call(bf16[256,1152]{1,0:T(8,128)(2,1)S(1)} %bitcast.54, bf16[8,1,128]{2,1,0:T(2,128)(2,1)S(1)} %copy.5.taps_ref), custom_call_target="tpu_custom_call" | custom-call | tf_op jit(solution)/shard_map/decimated_gram/pallas_call | solution.py:49
  58.6 0.0 copy-start.2
  58.7 1.0 copy-done.2
  59.7 1.2 dynamic-slice_bitcast_fusion
  60.9 0.1 collective-permute-start.1
  61.0 2.9 %collective-permute-done.1 = f32[8,128,256]{2,1,0:T(8,128)} collective-permute-done((f32[8,128,256]{2,1,0:T(8,128)}, f32[8,128,256]{2,1,0:T(8,128)}, u32[]{:S(2)}, u32[]{:S(2)}) %collective-permute-start.1) | collective-permute-done | bytes 1048608 | tf_op jit(solution)/shard_map/ppermute | solution.py:18
  63.9 1.4 bitcast_add_fusion
  65.2 30.2 %all_to_all.15 = f32[16,64,256]{2,1,0:T(8,128)S(1)} all-to-all(f32[16,64,256]{2,1,0:T(8,128)S(1)} %bitcast.60), channel_id=1, replica_groups=mesh['chan'=16,'tm'=16] {'chan'}, dimensions={0} | all-to-all | bytes 2097152 | tf_op jit(solution)/shard_map/all_to_all | solution.py:197
  95.4 0.1 reduce_sum.9
  95.5 2.9 %collective-permute-start.2 = (f32[64,256]{1,0:T(8,128)S(1)}, f32[64,256]{1,0:T(8,128)S(1)}, u32[]{:S(2)}, u32[]{:S(2)}) collective-permute-start(f32[64,256]{1,0:T(8,128)S(1)} %reduce_sum.9), channel_id=1, source_target_pairs={{0,2},{1,3},{2,0},{3,1},{4,6},{5,7},{6,4},{7,5},{8,10},{9,11},{10,... | collective-permute-start | bytes 196616 | tf_op jit(solution)/shard_map/ppermute | solution.py:18
  98.4 2.1 %collective-permute-done.2 = f32[64,256]{1,0:T(8,128)S(1)} collective-permute-done((f32[64,256]{1,0:T(8,128)S(1)}, f32[64,256]{1,0:T(8,128)S(1)}, u32[]{:S(2)}, u32[]{:S(2)}) %collective-permute-start.2) | collective-permute-done | bytes 65568 | tf_op jit(solution)/shard_map/ppermute | solution.py:18
  100.5 2.7 %collective-permute-start.3 = (f32[64,256]{1,0:T(8,128)S(1)}, f32[64,256]{1,0:T(8,128)S(1)}, u32[]{:S(2)}, u32[]{:S(2)}) collective-permute-start(f32[64,256]{1,0:T(8,128)S(1)} %add.37), channel_id=1, source_target_pairs={{0,4},{1,5},{2,6},{3,7},{4,0},{5,1},{6,2},{7,3},{8,12},{9,13},{10,... | collective-permute-start | bytes 196616 | tf_op jit(solution)/shard_map/ppermute | solution.py:18
  103.1 2.1 %collective-permute-done.3 = f32[64,256]{1,0:T(8,128)S(1)} collective-permute-done((f32[64,256]{1,0:T(8,128)S(1)}, f32[64,256]{1,0:T(8,128)S(1)}, u32[]{:S(2)}, u32[]{:S(2)}) %collective-permute-start.3) | collective-permute-done | bytes 65568 | tf_op jit(solution)/shard_map/ppermute | solution.py:18
  105.2 6.2 %collective-permute-start.4 = (f32[64,256]{1,0:T(8,128)S(1)}, f32[64,256]{1,0:T(8,128)S(1)}, u32[]{:S(2)}, u32[]{:S(2)}) collective-permute-start(f32[64,256]{1,0:T(8,128)S(1)} %add.38), channel_id=1, source_target_pairs={{0,8},{1,9},{2,10},{3,11},{4,12},{5,13},{6,14},{7,15},{8,0},{9,1},... | collective-permute-start | bytes 196616 | tf_op jit(solution)/shard_map/ppermute | solution.py:18
  111.4 1.8 %collective-permute-done.4 = f32[64,256]{1,0:T(8,128)S(1)} collective-permute-done((f32[64,256]{1,0:T(8,128)S(1)}, f32[64,256]{1,0:T(8,128)S(1)}, u32[]{:S(2)}, u32[]{:S(2)}) %collective-permute-start.4) | collective-permute-done | bytes 65568 | tf_op jit(solution)/shard_map/ppermute | solution.py:18
  113.2 4.4 %collective-permute-start.5 = (f32[64,256]{1,0:T(8,128)S(1)}, f32[64,256]{1,0:T(8,128)S(1)}, u32[]{:S(2)}, u32[]{:S(2)}) collective-permute-start(f32[64,256]{1,0:T(8,128)S(1)} %add.39), channel_id=1, source_target_pairs={{0,1},{1,0},{2,3},{3,2},{4,5},{5,4},{6,7},{7,6},{8,9},{9,8},{10,11... | collective-permute-start | bytes 196616 | tf_op jit(solution)/shard_map/ppermute | solution.py:18
  117.6 0.9 collective-permute-done.5
  118.5 0.4 collective-permute-start.6
  118.9 0.1 copy.6
  119.0 4.3 %collective-permute-done.6 = f32[2,64,256]{2,1,0:T(8,128)S(1)} collective-permute-done((f32[2,64,256]{2,1,0:T(8,128)S(1)}, f32[2,64,256]{2,1,0:T(8,128)S(1)}, u32[]{:S(2)}, u32[]{:S(2)}) %collective-permute-start.6) | collective-permute-done | bytes 131104 | tf_op jit(solution)/shard_map/ppermute | solution.py:18
  123.3 11.6 %projector_half.1 = f32[256,128]{1,0:T(8,128)S(1)} custom-call(s32[1]{0:T(128)} %bitcast.1.half_ref, f32[256,256]{1,0:T(8,128)S(1)} %bitcast.57, f32[256,32]{1,0:T(8,128)S(1)} %bitcast.58), custom_call_target="tpu_custom_call" | custom-call | tf_op jit(solution)/shard_map/projector_half/pallas_call | solution.py:103
  134.9 11.9 %all_to_all.16.projector_ref = f32[16,16,128]{2,1,0:T(8,128)S(1)} all-to-all(f32[16,16,128]{2,1,0:T(8,128)S(1)} %bitcast.59), channel_id=1, replica_groups=mesh['chan'=16,'tm'=16] {'chan'}, dimensions={0} | all-to-all | bytes 262144 | tf_op jit(solution)/shard_map/all_to_all | solution.py:212
  146.9 3.4 %copy-done.1 = bf16[256,16512]{1,0:T(8,128)(2,1)S(1)} copy-done((bf16[256,16512]{1,0:T(8,128)(2,1)S(1)}, bf16[256,16512]{1,0:T(8,128)(2,1)}, u32[]{:S(2)}) %copy-start.1) | copy-done | bytes 8454168
  150.3 7.8 %denoise.1 = f32[8,16,4096]{2,1,0:T(8,128)} custom-call(bf16[16,16,16512]{2,1,0:T(8,128)(2,1)S(1)} %bitcast.52, bf16[16,16,16512]{2,1,0:T(8,128)(2,1)S(1)} %bitcast.53, f32[16,16,128]{2,1,0:T(8,128)S(1)} %all_to_all.16.projector_ref, bf16[8,128,640]{2,1,0:T(8,128)(2,1)S(1)} %copy-done.3), custom_call_target="tpu_custom_call" | custom-call | tf_op jit(solution)/shard_map/denoise/pallas_call | solution.py:158
  (21 shorter events, 0.1 us)
Async XLA Ops:
  6.5 112.3 %copy-start = (f32[8,256,32]{1,2,0:T(8,128)S(1)}, f32[8,256,32]{1,2,0:T(8,128)}, u32[]{:S(2)}) copy-start(f32[8,256,32]{1,2,0:T(8,128)} %param.5) | copy-start | bytes 786436
  6.5 18.1 %copy-start.4 = (bf16[16,16384]{1,0:T(8,128)(2,1)S(1)}, bf16[16,16384]{1,0:T(8,128)(2,1)}, u32[]{:S(2)}) copy-start(bf16[16,16384]{1,0:T(8,128)(2,1)} %param.3) | copy-start | bytes 1572868
  6.5 30.4 %copy-start.6 = (bf16[8,128]{1,0:T(8,128)(2,1)S(1)}, bf16[8,128]{1,0:T(8,128)(2,1)}, u32[]{:S(2)}) copy-start(bf16[8,128]{1,0:T(8,128)(2,1)} %param.4) | copy-start | bytes 6148
  6.5 140.3 %all-gather.3.cloned.1.call-start = ((), (), s32[]{:S(2)}) async-start(), calls=%async_computation.3 | async-start | bytes 8982528 | tf_op jit(solution)/shard_map/all_gather | solution.py:184
  7.3 5.7 %collective-permute-start = (bf16[16,128]{1,0:T(8,128)(2,1)S(1)}, bf16[16,128]{1,0:T(8,128)(2,1)S(1)}, u32[]{:S(2)}, u32[]{:S(2)}) collective-permute-start(bf16[16,128]{1,0:T(8,128)(2,1)S(1)} %slice.51), channel_id=1, source_target_pairs={{0,1},{1,2},{2,3},{3,4},{4,5},{5,6},{6,7},{7,8},{8,9},{9,10},{10,1... | collective-permute-start | bytes 12296 | tf_op jit(solution)/shard_map/ppermute | solution.py:182
  14.1 0.8 copy-start.5
  30.2 21.5 %all-to-all-start = ((bf16[16,16,1152]{2,1,0:T(8,128)(2,1)}), bf16[16,16,1152]{2,1,0:T(8,128)(2,1)S(1)}, u32[]{:S(2)}, u32[]{:S(2)}) async-start(bf16[16,16,1152]{2,1,0:T(8,128)(2,1)} %constant_dynamic-update-slice_fusion.2), calls=%async_computation | async-start | bytes 1179648 | tf_op jit(solution)/shard_map/all_to_all | solution.py:190
  58.6 1.1 copy-start.2
  60.9 3.0 %collective-permute-start.1 = (f32[8,128,256]{2,1,0:T(8,128)}, f32[8,128,256]{2,1,0:T(8,128)}, u32[]{:S(2)}, u32[]{:S(2)}) collective-permute-start(f32[8,128,256]{2,1,0:T(8,128)} %dynamic-slice_bitcast_fusion), channel_id=1, source_target_pairs={{0,1},{1,0},{2,3},{3,2},{4,5},{5,4},{6,7},{7,6},{8,9},{9,8},{10,11... | collective-permute-start | bytes 3145736 | tf_op jit(solution)/shard_map/ppermute | solution.py:18
  95.4 51.4 %copy-start.3 = (bf16[8,128,640]{2,1,0:T(8,128)(2,1)S(1)}, bf16[8,128,640]{2,1,0:T(8,128)(2,1)}, u32[]{:S(2)}) copy-start(bf16[8,128,640]{2,1,0:T(8,128)(2,1)} %copy-done.2) | copy-start | bytes 3932164
  95.5 5.0 %collective-permute-start.2 = (f32[64,256]{1,0:T(8,128)S(1)}, f32[64,256]{1,0:T(8,128)S(1)}, u32[]{:S(2)}, u32[]{:S(2)}) collective-permute-start(f32[64,256]{1,0:T(8,128)S(1)} %reduce_sum.9), channel_id=1, source_target_pairs={{0,2},{1,3},{2,0},{3,1},{4,6},{5,7},{6,4},{7,5},{8,10},{9,11},{10,... | collective-permute-start | bytes 196616 | tf_op jit(solution)/shard_map/ppermute | solution.py:18
  100.5 4.7 %collective-permute-start.3 = (f32[64,256]{1,0:T(8,128)S(1)}, f32[64,256]{1,0:T(8,128)S(1)}, u32[]{:S(2)}, u32[]{:S(2)}) collective-permute-start(f32[64,256]{1,0:T(8,128)S(1)} %add.37), channel_id=1, source_target_pairs={{0,4},{1,5},{2,6},{3,7},{4,0},{5,1},{6,2},{7,3},{8,12},{9,13},{10,... | collective-permute-start | bytes 196616 | tf_op jit(solution)/shard_map/ppermute | solution.py:18
  105.2 8.0 %collective-permute-start.4 = (f32[64,256]{1,0:T(8,128)S(1)}, f32[64,256]{1,0:T(8,128)S(1)}, u32[]{:S(2)}, u32[]{:S(2)}) collective-permute-start(f32[64,256]{1,0:T(8,128)S(1)} %add.38), channel_id=1, source_target_pairs={{0,8},{1,9},{2,10},{3,11},{4,12},{5,13},{6,14},{7,15},{8,0},{9,1},... | collective-permute-start | bytes 196616 | tf_op jit(solution)/shard_map/ppermute | solution.py:18
  113.2 5.3 %collective-permute-start.5 = (f32[64,256]{1,0:T(8,128)S(1)}, f32[64,256]{1,0:T(8,128)S(1)}, u32[]{:S(2)}, u32[]{:S(2)}) collective-permute-start(f32[64,256]{1,0:T(8,128)S(1)} %add.39), channel_id=1, source_target_pairs={{0,1},{1,0},{2,3},{3,2},{4,5},{5,4},{6,7},{7,6},{8,9},{9,8},{10,11... | collective-permute-start | bytes 196616 | tf_op jit(solution)/shard_map/ppermute | solution.py:18
  118.5 4.8 %collective-permute-start.6 = (f32[2,64,256]{2,1,0:T(8,128)S(1)}, f32[2,64,256]{2,1,0:T(8,128)S(1)}, u32[]{:S(2)}, u32[]{:S(2)}) collective-permute-start(f32[2,64,256]{2,1,0:T(8,128)S(1)} %maximum_select_fusion.2), channel_id=1, source_target_pairs={{0,16},{16,0},{32,48},{48,32},{64,80},{80,64},{96,112},{112,96},{1... | collective-permute-start | bytes 393224 | tf_op jit(solution)/shard_map/ppermute | solution.py:18
  146.9 3.4 %copy-start.1 = (bf16[256,16512]{1,0:T(8,128)(2,1)S(1)}, bf16[256,16512]{1,0:T(8,128)(2,1)}, u32[]{:S(2)}) copy-start(bf16[256,16512]{1,0:T(8,128)(2,1)} %all-gather.3.cloned.1.call-done) | copy-start | bytes 25362436
Sparse Core Ops, SparseCore 0:
  15.0 96.2 all-gather.2

commit v2 on v1

v2 whole, which is shorter than its diff:
```python
import jax
import jax.numpy as jnp
from jax import lax
from jax.experimental import pallas as pl
from jax.experimental.pallas import tpu as pltpu
from jax.sharding import PartitionSpec as P

ITERS = 3
RIM = 128
STEP = 512
WINDOW = STEP + RIM
HIGHEST = lax.Precision.HIGHEST
VMEM_LIMIT = 40 * 1024 * 1024


def swapped(block, axis, distance):
    route = [(i, i ^ distance) for i in range(lax.axis_size(axis))]
    return lax.ppermute(block, axis, route)


def dot_nt(a, b, precision=None):
    return lax.dot_general(
        a, b, (((1,), (1,)), ((), ())), precision=precision, preferred_element_type=jnp.float32
    )


def halves(value):
    high = value.astype(jnp.bfloat16)
    return high, (value - high.astype(jnp.float32)).astype(jnp.bfloat16)


def windows_kernel(raw_ref, before_ref, extended_ref, windows_ref):
    count, _, width = windows_ref.shape
    part = width - RIM
    extended_ref[:, :RIM] = before_ref[...]
    extended_ref[:, RIM:] = raw_ref[...]
    for i in range(count):
        first = i * part - RIM
        if i:
            windows_ref[i] = raw_ref[:, first : first + width]
        else:
            windows_ref[i, :, :RIM] = before_ref[...]
            windows_ref[i, :, RIM:] = raw_ref[:, :part]


def overlapping(raw_strain, before, count):
    own, samples = raw_strain.shape
    return pl.pallas_call(
        windows_kernel,
        out_shape=[
            jax.ShapeDtypeStruct((own, samples + RIM), raw_strain.dtype),
            jax.ShapeDtypeStruct((count, own, samples // count + RIM), raw_strain.dtype),
        ],
        compiler_params=pltpu.CompilerParams(vmem_limit_bytes=16 * 1024 * 1024),
        name="overlapping",
    )(raw_strain, before)


def table_kernel(taps_ref, table_ref):
    for b in range(taps_ref.shape[0]):
        row = jnp.concatenate(
            [taps_ref[b].astype(jnp.float32), jnp.zeros((1, STEP), jnp.float32)], axis=1
        )
        table = pltpu.roll(jnp.broadcast_to(row, (128, WINDOW)), 4, 1, stride=4, stride_axis=0)
        table_ref[128 * b : 128 * b + 128, :] = table.astype(table_ref.dtype)


def filter_table(fir_taps):
    return pl.pallas_call(
        table_kernel,
        out_shape=jax.ShapeDtypeStruct((128 * fir_taps.shape[0], WINDOW), fir_taps.dtype),
        compiler_params=pltpu.CompilerParams(vmem_limit_bytes=16 * 1024 * 1024),
        name="filter_table",
    )(fir_taps[:, None, :])


def gram_kernel(core_ref, x_ref, table_ref, kept_ref, sent_ref, packed_ref):
    core = core_ref[0]
    count = packed_ref.shape[0] // 2
    lanes = lax.broadcasted_iota(jnp.int32, (64, 128), 1)
    pieces = [
        dot_nt(x_ref[:, first : first + WINDOW], table_ref[...])
        for first in range(0, x_ref.shape[1] - RIM, STEP)
    ]
    for b in range(kept_ref.shape[0]):
        decimated = jnp.concatenate([p[:, 128 * b : 128 * b + 128] for p in pieces], axis=1)
        high, low = halves(decimated)
        gram = dot_nt(high, high) + dot_nt(high, low) + dot_nt(low, high)
        packed_ref[0:64, :] = gram[0:64, 0:128]
        packed_ref[64:128, :] = gram[0:64, 128:256]
        packed_ref[128:192, :] = gram[64:128, 128:256]
        packed_ref[192:256, :] = gram[128:192, 128:256]
        last = pltpu.roll(gram[192:256, 128:256], 64, 1)
        packed_ref[256:320, :] = jnp.where(lanes < 64, last, gram[64:128, 0:128])
        kept_ref[b] = packed_ref[pl.ds(pl.multiple_of(core * count, 8), count), :]
        sent_ref[b] = packed_ref[pl.ds(pl.multiple_of((1 - core) * count, 8), count), :]


def unpacked(packed):
    first, corner = packed[0:64], packed[256:320]
    upper = jnp.concatenate(
        [first, jnp.concatenate([first.T[64:128], corner[:, 64:128]], axis=1)], axis=0
    )
    third = packed[192:256]
    lower = jnp.concatenate(
        [third, jnp.concatenate([third.T[64:128], corner[:, 0:64]], axis=1)], axis=0
    )
    across = packed[64:192]
    return jnp.concatenate(
        [
            jnp.concatenate([upper, across], axis=1),
            jnp.concatenate([across.T, lower], axis=1),
        ],
        axis=0,
    )


def decimated_gram(core, windows, table):
    channels, samples = windows.shape
    bands = table.shape[0] // 128
    half = jax.ShapeDtypeStruct((bands, 160, 128), jnp.float32)
    half_spec = pl.BlockSpec((2, 160, 128), lambda b: (b, 0, 0))
    return pl.pallas_call(
        gram_kernel,
        grid=(bands // 2,),
        in_specs=[
            pl.BlockSpec(memory_space=pltpu.SMEM),
            pl.BlockSpec((channels, samples), lambda b: (0, 0)),
            pl.BlockSpec((256, WINDOW), lambda b: (b, 0)),
        ],
        out_specs=[half_spec, half_spec],
        out_shape=[half, half],
        scratch_shapes=[pltpu.VMEM((320, 128), jnp.float32)],
        compiler_params=pltpu.CompilerParams(vmem_limit_bytes=VMEM_LIMIT),
        name="decimated_gram",
    )(core.reshape(1), windows, table)


def inverse_cholesky(compact):
    rank = compact.shape[0]
    rows = lax.broadcasted_iota(jnp.int32, (rank, rank), 0)
    columns = lax.broadcasted_iota(jnp.int32, (rank, rank), 1)
    unit = (rows == columns).astype(jnp.float32)
    both = jnp.concatenate([compact, unit], axis=1)
    below = lax.broadcasted_iota(jnp.int32, both.shape, 0)
    for block in range(0, rank, 8):
        spread = [
            jnp.broadcast_to(both[:, block + p : block + p + 1], both.shape) for p in range(8)
        ]
        for p in range(8):
            j = block + p
            column = spread[p]
            factor = jnp.where(below > j, column * (1.0 / column[j : j + 1, :]), 0.0)
            both = both - factor * both[j : j + 1, :]
            for q in range(p + 1, 8):
                spread[q] = spread[q] - factor * spread[q][j : j + 1, :]
    pivots = jnp.sum(unit * both[:, :rank], axis=1, keepdims=True)
    return both[:, rank:] / jnp.sqrt(pivots)


def refine_kernel(
    place_ref, mine_ref, core_ref, chan_ref, both_ref, start_ref, out_ref, gram_ref, basis_ref
):
    core, half = place_ref[0], place_ref[1]
    near = jnp.where(core == 0, mine_ref[...], core_ref[...])
    near_next = jnp.where(core == 0, core_ref[...], mine_ref[...])
    far = jnp.where(core == 0, chan_ref[...], both_ref[...])
    far_next = jnp.where(core == 0, both_ref[...], chan_ref[...])
    packed = jnp.concatenate(
        [
            jnp.where(half == 0, near, far),
            jnp.where(half == 0, far, near),
            jnp.where(half == 0, near_next, far_next),
            jnp.where(half == 0, far_next, near_next),
        ],
        axis=0,
    )
    gram_ref[...] = unpacked(packed)
    basis = start_ref[...]
    for _ in range(ITERS):
        image = jnp.dot(gram_ref[...], basis, precision=HIGHEST, preferred_element_type=jnp.float32)
        compact = lax.dot_general(
            image,
            image,
            (((0,), (0,)), ((), ())),
            precision=HIGHEST,
            preferred_element_type=jnp.float32,
        )
        basis = dot_nt(image, inverse_cholesky(compact), HIGHEST)
    basis_ref[...] = basis
    count = out_ref.shape[1]
    part = basis_ref[pl.ds(pl.multiple_of(half * count, count), count), :]
    out_ref[...] = dot_nt(basis, part, HIGHEST)


def projector_half(place, quarters, start):
    channels = start.shape[0]
    return pl.pallas_call(
        refine_kernel,
        in_specs=[pl.BlockSpec(memory_space=pltpu.SMEM)]
        + [pl.BlockSpec(memory_space=pltpu.VMEM)] * 5,
        out_specs=pl.BlockSpec(memory_space=pltpu.VMEM),
        out_shape=jax.ShapeDtypeStruct((channels, channels // 2), jnp.float32),
        scratch_shapes=[
            pltpu.VMEM((channels, channels), jnp.float32),
            pltpu.VMEM(start.shape, jnp.float32),
        ],
        compiler_params=pltpu.CompilerParams(vmem_limit_bytes=16 * 1024 * 1024),
        name="projector_half",
    )(place, *quarters, start)


def denoise_kernel(x_ref, rim_ref, projector_ref, table_ref, out_ref, mixed_ref):
    bands, own, count = out_ref.shape
    sources, _, samples = x_ref.shape
    rows = bands * own
    projector = jnp.concatenate(
        [
            jnp.concatenate([projector_ref[2 * b], projector_ref[2 * b + 1]], axis=1)
            for b in range(bands)
        ],
        axis=0,
    )
    stacked = jnp.concatenate(halves(projector), axis=0)

    def mix(x, first):
        both = jnp.dot(stacked, x, preferred_element_type=jnp.float32)
        high, low = halves(both[:rows] + both[rows:])
        mixed_ref[:rows, first : first + x.shape[1]] = high
        mixed_ref[rows:, first : first + x.shape[1]] = low

    for first in range(0, samples, STEP):
        mix(x_ref[:, :, first : first + STEP].reshape(sources * own, STEP), first)
    mix(rim_ref[...].reshape(sources * own, RIM), samples)
    blocks = count // 128
    for b in range(bands):
        windows = [
            mixed_ref[part + b * own : part + (b + 1) * own, STEP * m : STEP * m + WINDOW]
            for part in (0, rows)
            for m in range(blocks)
        ]
        both = dot_nt(jnp.concatenate(windows, axis=0), table_ref[128 * b : 128 * b + 128, :])
        result = both[: blocks * own] + both[blocks * own :]
        for m in range(blocks):
            out_ref[b, :, 128 * m : 128 * m + 128] = result[m * own : (m + 1) * own]


def denoise(gathered, projector, table):
    sources, own, extended = gathered.shape
    bands = table.shape[0] // 128
    samples = 4096
    steps = (extended - RIM) // samples
    return pl.pallas_call(
        denoise_kernel,
        grid=(steps,),
        in_specs=[
            pl.BlockSpec((sources, own, samples), lambda i: (0, 0, i)),
            pl.BlockSpec((sources, own, RIM), lambda i: (0, 0, (i + 1) * (samples // RIM))),
            pl.BlockSpec(projector.shape, lambda i: (0, 0, 0)),
            pl.BlockSpec(table.shape, lambda i: (0, 0)),
        ],
        out_specs=pl.BlockSpec((bands, own, samples // 4), lambda i: (0, 0, i)),
        out_shape=jax.ShapeDtypeStruct((bands, own, steps * samples // 4), jnp.float32),
        scratch_shapes=[pltpu.VMEM((2 * bands * own, samples + RIM), jnp.bfloat16)],
        compiler_params=pltpu.CompilerParams(vmem_limit_bytes=60 * 1024 * 1024),
        name="denoise",
    )(gathered, gathered, projector, table)


def shards(raw_strain, fir_taps, start_basis):
    own, samples = raw_strain.shape
    chan_count, tm_count = lax.axis_size("chan"), lax.axis_size("tm")
    channels = own * chan_count
    place, core = lax.axis_index("chan"), lax.axis_index("tm") % 2
    half = place % 2
    rim_piece = raw_strain[:, samples - RIM :]
    before = lax.ppermute(rim_piece, "tm", [(i, i + 1) for i in range(tm_count - 1)])
    extended, windows = overlapping(raw_strain, before, chan_count)
    gathered = lax.all_gather(extended, "chan", axis=0)

    windows = lax.all_to_all(windows, "chan", 0, 0, tiled=True)
    table = filter_table(fir_taps)
    kept, sent = decimated_gram(core, windows.reshape(channels, -1), table)

    quarters = (kept + swapped(sent, "tm", 1)).reshape(chan_count, 80, 128)
    quarter = jnp.sum(lax.all_to_all(quarters, "chan", 0, 0, tiled=True), axis=0)
    distance = 2
    while distance < tm_count:
        quarter = quarter + swapped(quarter, "tm", distance)
        distance *= 2

    everyone = range(chan_count * tm_count)
    across = [(i, i ^ (tm_count + 1)) for i in everyone]
    four = (
        quarter,
        swapped(quarter, "tm", 1),
        swapped(quarter, "chan", 1),
        lax.ppermute(quarter, ("chan", "tm"), across),
    )
    start = lax.dynamic_index_in_dim(start_basis, place // 2, 0, False)
    projector = projector_half(jnp.stack([core, half]), four, start)

    projector = projector.reshape(chan_count, own, channels // 2)
    projector = lax.all_to_all(projector, "chan", 0, 0, tiled=True)
    return denoise(gathered, projector, table)


def solution(mesh):
    placed = (P("chan", "tm"), P(), P())
    return jax.shard_map(
        shards, mesh=mesh, in_specs=placed, out_specs=P(None, "chan", "tm"), check_vma=False
    )
```

time: 166 us -> 115 us (0.69)
  local copies, waits for them, and re-layouts: 23.7 us -> 1.9 us
  blocking collectives: 42.1 us -> 26.5 us
  Pallas kernels: 26.3 us -> 21 us
  waiting for transfers between devices: 29.5 us -> 24.2 us
    unnamed x30 -> x8, local copies, waits for them, and re-layouts: 19.9 us -> 1.05 us
    all_to_all x1, blocking collectives: 30.2 us -> 16.3 us  [shards(): lax.all_to_all(quarters, 'chan', 0, 0, tiled=True)]
    ppermute x6, starting transfers between devices: 16.7 us -> 12 us  [swapped(): return lax.ppermute(block, axis, route)]
    pallas_call x1, Pallas kernels: 11.6 us -> 7.01 us  [projector_half(): pl.pallas_call(refine_kernel, in_specs=[pl.BlockSpec(memory_space=pltpu.S...]
    ppermute x0 -> x1, starting transfers between devices: none -> 3.89 us  [shards(): lax.ppermute(quarter, ('chan', 'tm'), across)]
    ppermute x6, waiting for transfers between devices: 14 us -> 10.4 us  [swapped(): return lax.ppermute(block, axis, route)]
    all_to_all x1, waiting for transfers between devices: 14.7 us -> 11.4 us  [shards(): windows = lax.all_to_all(windows, 'chan', 0, 0, tiled=True)]
    pallas_call x1 -> x3, Pallas kernels: 6.93 us -> 4.65 us  [the longest x1 3.41 us: decimated_gram(): pl.pallas_call(gram_kernel, grid=(bands // 2,), in_specs=[pl.BlockSpec(me...]
  transfers between devices with their start and end apart: 9 -> 10, of which waited for: 8 -> 8; matrix products, arithmetic and copies ran while one was open for 11% -> 0% of each run, Pallas kernels for 11% -> 9%
where the time goes in v2:
time: 115 us
  starting transfers between devices  27.6 us (24%)
  blocking collectives  26.5 us (23%)
  waiting for transfers between devices  24.2 us (21%)
  Pallas kernels  21 us (18%)
  between operations  13.5 us (12%)
  local copies, waits for them, and re-layouts  1.9 us (2%)
    all_to_all x1, blocking collectives, shards(): lax.all_to_all(quarters, 'chan', 0, 0, tiled=True)  16.3 us
    ppermute x6, starting transfers between devices, swapped(): return lax.ppermute(block, axis, route)  12 us
    all_to_all x1, waiting for transfers between devices, shards(): windows = lax.all_to_all(windows, 'chan', 0, 0, tiled=True)  11.4 us
    ppermute x6, waiting for transfers between devices, swapped(): return lax.ppermute(block, axis, route)  10.4 us
    all_to_all x1, blocking collectives, shards(): projector = lax.all_to_all(projector, 'chan', 0, 0, tiled=True)  10.2 us
    pallas_call x1, Pallas kernels, denoise(): pl.pallas_call(denoise_kernel, grid=(steps,), in_specs=[pl.BlockSpec((sou...  9.31 us
    pallas_call x1, Pallas kernels, projector_half(): pl.pallas_call(refine_kernel, in_specs=[pl.BlockSpec(memory_space=pltpu.S...  7.01 us
    all_to_all x1, starting transfers between devices, shards(): windows = lax.all_to_all(windows, 'chan', 0, 0, tiled=True)  6.77 us
  transfers between devices with their start and end apart: 10, of which 8 were waited for; matrix products, arithmetic and copies ran while one was open for 0% of the time, Pallas kernels for 9%

profile of v2, /device:TPU:1, one launch (start us, length us, event | category | flops | bytes accessed | tf_op | source)
XLA Modules:
  0.0 114.8 jit_solution(1189034422393222679)
XLA Ops:
  6.5 0.0 copy-start
  6.5 0.0 copy-start.3
  6.5 0.0 all-gather.3.cloned.1.call-start
  6.5 0.7 slice.3
  7.3 4.9 %collective-permute-start = (bf16[16,128]{1,0:T(8,128)(2,1)S(1)}, bf16[16,128]{1,0:T(8,128)(2,1)S(1)}, u32[]{:S(2)}, u32[]{:S(2)}) collective-permute-start(bf16[16,128]{1,0:T(8,128)(2,1)S(1)} %slice.3), channel_id=1, source_target_pairs={{0,1},{1,2},{2,3},{3,4},{4,5},{5,6},{6,7},{7,8},{8,9},{9,10},{10,1... | collective-permute-start | bytes 12296 | tf_op jit(solution)/shard_map/ppermute | solution.py:277
  12.2 0.7 collective-permute-done.before_ref
  12.9 0.0 copy-start.2
  13.0 1.0 copy-done.2
  14.0 1.1 overlapping.1
  15.1 0.0 all-gather.3.cloned.1.call-update
  15.1 6.8 %all-to-all-start = ((bf16[16,16,1152]{2,1,0:T(8,128)(2,1)}), bf16[16,16,1152]{2,1,0:T(8,128)(2,1)S(1)}, u32[]{:S(2)}, u32[]{:S(2)}) async-start(bf16[16,16,1152]{2,1,0:T(8,128)(2,1)} %get-tuple-element.10), calls=%async_computation | async-start | bytes 1179648 | tf_op jit(solution)/shard_map/all_to_all | solution.py:281
  21.9 0.0 copy-done.3
  21.9 0.2 filter_table.1.table_ref
  22.1 0.0 copy-start.1
  22.1 11.4 %all-to-all-done = bf16[16,16,1152]{2,1,0:T(8,128)(2,1)S(1)} async-done(((bf16[16,16,1152]{2,1,0:T(8,128)(2,1)}), bf16[16,16,1152]{2,1,0:T(8,128)(2,1)S(1)}, u32[]{:S(2)}, u32[]{:S(2)}) %all-to-all-start) | async-done | bytes 589856 | tf_op jit(solution)/shard_map/all_to_all | solution.py:281
  33.4 3.4 %decimated_gram.1 = (f32[8,160,128]{2,1,0:T(8,128)S(1)}, f32[8,160,128]{2,1,0:T(8,128)S(1)}) custom-call(s32[1]{0:T(128)} %bitcast.1.core_ref, bf16[256,1152]{1,0:T(8,128)(2,1)S(1)} %bitcast.8, bf16[1024,640]{1,0:T(8,128)(2,1)S(1)} %filter_table.1.table_ref), custom_call_target="tpu_custom_call" | custom-call | tf_op jit(solution)/shard_map/decimated_gram/pallas_call | solution.py:123
  36.9 0.1 collective-permute-start.1
  37.0 2.1 %collective-permute-done.1 = f32[8,160,128]{2,1,0:T(8,128)S(1)} collective-permute-done((f32[8,160,128]{2,1,0:T(8,128)S(1)}, f32[8,160,128]{2,1,0:T(8,128)S(1)}, u32[]{:S(2)}, u32[]{:S(2)}) %collective-permute-start.1) | collective-permute-done | bytes 655392 | tf_op jit(solution)/shard_map/ppermute | solution.py:18
  39.1 0.1 add.26
  39.1 16.3 %all_to_all.15 = f32[16,80,128]{2,1,0:T(8,128)S(1)} all-to-all(f32[16,80,128]{2,1,0:T(8,128)S(1)} %bitcast.13), channel_id=1, replica_groups=mesh['chan'=16,'tm'=16] {'chan'}, dimensions={0} | all-to-all | bytes 1310720 | tf_op jit(solution)/shard_map/all_to_all | solution.py:286
  55.4 0.0 copy-done.1
  55.5 1.6 %collective-permute-start.2 = (f32[80,128]{1,0:T(8,128)S(1)}, f32[80,128]{1,0:T(8,128)S(1)}, u32[]{:S(2)}, u32[]{:S(2)}) collective-permute-start(f32[80,128]{1,0:T(8,128)S(1)} %reduce_sum.9), channel_id=1, source_target_pairs={{0,2},{1,3},{2,0},{3,1},{4,6},{5,7},{6,4},{7,5},{8,10},{9,11},{10,... | collective-permute-start | bytes 122888 | tf_op jit(solution)/shard_map/ppermute | solution.py:18
  57.1 1.4 %collective-permute-done.2 = f32[80,128]{1,0:T(8,128)S(1)} collective-permute-done((f32[80,128]{1,0:T(8,128)S(1)}, f32[80,128]{1,0:T(8,128)S(1)}, u32[]{:S(2)}, u32[]{:S(2)}) %collective-permute-start.2) | collective-permute-done | bytes 40992 | tf_op jit(solution)/shard_map/ppermute | solution.py:18
  58.5 4.7 %collective-permute-start.3 = (f32[80,128]{1,0:T(8,128)S(1)}, f32[80,128]{1,0:T(8,128)S(1)}, u32[]{:S(2)}, u32[]{:S(2)}) collective-permute-start(f32[80,128]{1,0:T(8,128)S(1)} %add.27), channel_id=1, source_target_pairs={{0,4},{1,5},{2,6},{3,7},{4,0},{5,1},{6,2},{7,3},{8,12},{9,13},{10,... | collective-permute-start | bytes 122888 | tf_op jit(solution)/shard_map/ppermute | solution.py:18
  63.2 1.8 %collective-permute-done.3 = f32[80,128]{1,0:T(8,128)S(1)} collective-permute-done((f32[80,128]{1,0:T(8,128)S(1)}, f32[80,128]{1,0:T(8,128)S(1)}, u32[]{:S(2)}, u32[]{:S(2)}) %collective-permute-start.3) | collective-permute-done | bytes 40992 | tf_op jit(solution)/shard_map/ppermute | solution.py:18
  65.0 4.3 %collective-permute-start.4 = (f32[80,128]{1,0:T(8,128)S(1)}, f32[80,128]{1,0:T(8,128)S(1)}, u32[]{:S(2)}, u32[]{:S(2)}) collective-permute-start(f32[80,128]{1,0:T(8,128)S(1)} %add.28), channel_id=1, source_target_pairs={{0,8},{1,9},{2,10},{3,11},{4,12},{5,13},{6,14},{7,15},{8,0},{9,1},... | collective-permute-start | bytes 122888 | tf_op jit(solution)/shard_map/ppermute | solution.py:18
  69.3 0.0 copy-done
  69.3 2.5 %collective-permute-done.4 = f32[80,128]{1,0:T(8,128)S(1)} collective-permute-done((f32[80,128]{1,0:T(8,128)S(1)}, f32[80,128]{1,0:T(8,128)S(1)}, u32[]{:S(2)}, u32[]{:S(2)}) %collective-permute-start.4) | collective-permute-done | bytes 40992 | tf_op jit(solution)/shard_map/ppermute | solution.py:18
  71.8 3.9 %collective-permute-start.7 = (f32[80,128]{1,0:T(8,128)S(1)}, f32[80,128]{1,0:T(8,128)S(1)}, u32[]{:S(2)}, u32[]{:S(2)}) collective-permute-start(f32[80,128]{1,0:T(8,128)S(1)} %add.29.mine_ref), channel_id=1, source_target_pairs={{0,17},{1,16},{2,19},{3,18},{4,21},{5,20},{6,23},{7,22},{8,25},{9,... | collective-permute-start | bytes 122888 | tf_op jit(solution)/shard_map/ppermute | solution.py:298
  75.7 1.3 %collective-permute-start.6 = (f32[80,128]{1,0:T(8,128)S(1)}, f32[80,128]{1,0:T(8,128)S(1)}, u32[]{:S(2)}, u32[]{:S(2)}) collective-permute-start(f32[80,128]{1,0:T(8,128)S(1)} %add.29.mine_ref), channel_id=1, source_target_pairs={{0,16},{16,0},{32,48},{48,32},{64,80},{80,64},{96,112},{112,96},{1... | collective-permute-start | bytes 122888 | tf_op jit(solution)/shard_map/ppermute | solution.py:18
  77.0 0.0 collective-permute-start.5
  77.0 0.1 pad_add_fusion.place_ref
  77.0 0.1 copy.6
  77.1 1.6 %collective-permute-done.7.both_ref = f32[80,128]{1,0:T(8,128)S(1)} collective-permute-done((f32[80,128]{1,0:T(8,128)S(1)}, f32[80,128]{1,0:T(8,128)S(1)}, u32[]{:S(2)}, u32[]{:S(2)}) %collective-permute-start.7) | collective-permute-done | bytes 40992 | tf_op jit(solution)/shard_map/ppermute | solution.py:298
  78.7 2.7 %collective-permute-done.6.chan_ref = f32[80,128]{1,0:T(8,128)S(1)} collective-permute-done((f32[80,128]{1,0:T(8,128)S(1)}, f32[80,128]{1,0:T(8,128)S(1)}, u32[]{:S(2)}, u32[]{:S(2)}) %collective-permute-start.6) | collective-permute-done | bytes 40992 | tf_op jit(solution)/shard_map/ppermute | solution.py:18
  81.4 0.0 collective-permute-done.5.core_ref
  81.4 7.0 %projector_half.1 = f32[256,128]{1,0:T(8,128)S(1)} custom-call(s32[2]{0:T(128)S(1)} %pad_add_fusion.place_ref, f32[80,128]{1,0:T(8,128)S(1)} %add.29.mine_ref, f32[80,128]{1,0:T(8,128)S(1)} %collective-permute-done.5.core_ref, f32[80,128]{1,0:T(8,128)S(1)} %collective-permute-done.6.chan_ref, f32[80,128]{1,0:T(8,128)S(1)} %collective-permute-done.7.both_ref, ...), custom_call_target="tpu_custom_call" | custom-call | tf_op jit(solution)/shard_map/projector_half/pallas_call | solution.py:198
  88.5 10.2 %all_to_all.16.projector_ref = f32[16,16,128]{2,1,0:T(8,128)} all-to-all(f32[16,16,128]{2,1,0:T(8,128)S(1)} %bitcast.10), channel_id=1, replica_groups=mesh['chan'=16,'tm'=16] {'chan'}, dimensions={0} | all-to-all | bytes 262144 | tf_op jit(solution)/shard_map/all_to_all | solution.py:304
  98.7 0.0 all-gather.3.cloned.1.call-done
  98.7 9.3 %denoise.1 = f32[8,16,4096]{2,1,0:T(8,128)} custom-call(bf16[16,16,16512]{2,1,0:T(8,128)(2,1)} %bitcast.11, bf16[16,16,16512]{2,1,0:T(8,128)(2,1)} %bitcast.12, f32[16,16,128]{2,1,0:T(8,128)} %all_to_all.16.projector_ref, bf16[1024,640]{1,0:T(8,128)(2,1)} %copy-done.1), custom_call_target="tpu_custom_call" | custom-call | tf_op jit(solution)/shard_map/denoise/pallas_call | solution.py:253
  (6 shorter events, 0.1 us)
Async XLA Ops:
  6.5 62.8 %copy-start = (f32[8,256,32]{1,2,0:T(8,128)S(1)}, f32[8,256,32]{1,2,0:T(8,128)}, u32[]{:S(2)}) copy-start(f32[8,256,32]{1,2,0:T(8,128)} %param.5) | copy-start | bytes 786436
  6.5 15.3 %copy-start.3 = (bf16[8,128]{1,0:T(8,128)(2,1)S(1)}, bf16[8,128]{1,0:T(8,128)(2,1)}, u32[]{:S(2)}) copy-start(bf16[8,128]{1,0:T(8,128)(2,1)} %param.4) | copy-start | bytes 6148
  6.5 92.1 %all-gather.3.cloned.1.call-start = ((), (), s32[]{:S(2)}) async-start(), calls=%async_computation.3 | async-start | bytes 8982528 | tf_op jit(solution)/shard_map/all_gather | solution.py:279
  7.3 5.7 %collective-permute-start = (bf16[16,128]{1,0:T(8,128)(2,1)S(1)}, bf16[16,128]{1,0:T(8,128)(2,1)S(1)}, u32[]{:S(2)}, u32[]{:S(2)}) collective-permute-start(bf16[16,128]{1,0:T(8,128)(2,1)S(1)} %slice.3), channel_id=1, source_target_pairs={{0,1},{1,2},{2,3},{3,4},{4,5},{5,6},{6,7},{7,8},{8,9},{9,10},{10,1... | collective-permute-start | bytes 12296 | tf_op jit(solution)/shard_map/ppermute | solution.py:277
  12.9 1.0 copy-start.2
  15.1 18.4 %all-to-all-start = ((bf16[16,16,1152]{2,1,0:T(8,128)(2,1)}), bf16[16,16,1152]{2,1,0:T(8,128)(2,1)S(1)}, u32[]{:S(2)}, u32[]{:S(2)}) async-start(bf16[16,16,1152]{2,1,0:T(8,128)(2,1)} %get-tuple-element.10), calls=%async_computation | async-start | bytes 1179648 | tf_op jit(solution)/shard_map/all_to_all | solution.py:281
  22.1 33.4 %copy-start.1 = (bf16[1024,640]{1,0:T(8,128)(2,1)}, bf16[1024,640]{1,0:T(8,128)(2,1)S(1)}, u32[]{:S(2)}) copy-start(bf16[1024,640]{1,0:T(8,128)(2,1)S(1)} %filter_table.1.table_ref) | copy-start | bytes 3932164
  36.9 2.2 %collective-permute-start.1 = (f32[8,160,128]{2,1,0:T(8,128)S(1)}, f32[8,160,128]{2,1,0:T(8,128)S(1)}, u32[]{:S(2)}, u32[]{:S(2)}) collective-permute-start(f32[8,160,128]{2,1,0:T(8,128)S(1)} %get-tuple-element.12), channel_id=1, source_target_pairs={{0,1},{1,0},{2,3},{3,2},{4,5},{5,4},{6,7},{7,6},{8,9},{9,8},{10,11... | collective-permute-start | bytes 1966088 | tf_op jit(solution)/shard_map/ppermute | solution.py:18
  55.5 3.0 %collective-permute-start.2 = (f32[80,128]{1,0:T(8,128)S(1)}, f32[80,128]{1,0:T(8,128)S(1)}, u32[]{:S(2)}, u32[]{:S(2)}) collective-permute-start(f32[80,128]{1,0:T(8,128)S(1)} %reduce_sum.9), channel_id=1, source_target_pairs={{0,2},{1,3},{2,0},{3,1},{4,6},{5,7},{6,4},{7,5},{8,10},{9,11},{10,... | collective-permute-start | bytes 122888 | tf_op jit(solution)/shard_map/ppermute | solution.py:18
  58.5 6.5 %collective-permute-start.3 = (f32[80,128]{1,0:T(8,128)S(1)}, f32[80,128]{1,0:T(8,128)S(1)}, u32[]{:S(2)}, u32[]{:S(2)}) collective-permute-start(f32[80,128]{1,0:T(8,128)S(1)} %add.27), channel_id=1, source_target_pairs={{0,4},{1,5},{2,6},{3,7},{4,0},{5,1},{6,2},{7,3},{8,12},{9,13},{10,... | collective-permute-start | bytes 122888 | tf_op jit(solution)/shard_map/ppermute | solution.py:18
  65.0 6.8 %collective-permute-start.4 = (f32[80,128]{1,0:T(8,128)S(1)}, f32[80,128]{1,0:T(8,128)S(1)}, u32[]{:S(2)}, u32[]{:S(2)}) collective-permute-start(f32[80,128]{1,0:T(8,128)S(1)} %add.28), channel_id=1, source_target_pairs={{0,8},{1,9},{2,10},{3,11},{4,12},{5,13},{6,14},{7,15},{8,0},{9,1},... | collective-permute-start | bytes 122888 | tf_op jit(solution)/shard_map/ppermute | solution.py:18
  71.8 6.9 %collective-permute-start.7 = (f32[80,128]{1,0:T(8,128)S(1)}, f32[80,128]{1,0:T(8,128)S(1)}, u32[]{:S(2)}, u32[]{:S(2)}) collective-permute-start(f32[80,128]{1,0:T(8,128)S(1)} %add.29.mine_ref), channel_id=1, source_target_pairs={{0,17},{1,16},{2,19},{3,18},{4,21},{5,20},{6,23},{7,22},{8,25},{9,... | collective-permute-start | bytes 122888 | tf_op jit(solution)/shard_map/ppermute | solution.py:298
  75.7 5.8 %collective-permute-start.6 = (f32[80,128]{1,0:T(8,128)S(1)}, f32[80,128]{1,0:T(8,128)S(1)}, u32[]{:S(2)}, u32[]{:S(2)}) collective-permute-start(f32[80,128]{1,0:T(8,128)S(1)} %add.29.mine_ref), channel_id=1, source_target_pairs={{0,16},{16,0},{32,48},{48,32},{64,80},{80,64},{96,112},{112,96},{1... | collective-permute-start | bytes 122888 | tf_op jit(solution)/shard_map/ppermute | solution.py:18
  77.0 4.5 %collective-permute-start.5 = (f32[80,128]{1,0:T(8,128)S(1)}, f32[80,128]{1,0:T(8,128)S(1)}, u32[]{:S(2)}, u32[]{:S(2)}) collective-permute-start(f32[80,128]{1,0:T(8,128)S(1)} %add.29.mine_ref), channel_id=1, source_target_pairs={{0,1},{1,0},{2,3},{3,2},{4,5},{5,4},{6,7},{7,6},{8,9},{9,8},{10,11... | collective-permute-start | bytes 122888 | tf_op jit(solution)/shard_map/ppermute | solution.py:18
Sparse Core Ops, SparseCore 0:
  15.2 81.5 all-gather.2

commit v3 on v2

--- a/solution.py
+++ b/solution.py
@@ -29,28 +29,26 @@
     return high, (value - high.astype(jnp.float32)).astype(jnp.bfloat16)
 
 
-def windows_kernel(raw_ref, before_ref, extended_ref, windows_ref):
+def windows_kernel(raw_ref, before_ref, windows_ref):
     count, _, width = windows_ref.shape
-    part = width - RIM
-    extended_ref[:, :RIM] = before_ref[...]
-    extended_ref[:, RIM:] = raw_ref[...]
+    part = width - 2 * RIM
     for i in range(count):
         first = i * part - RIM
         if i:
-            windows_ref[i] = raw_ref[:, first : first + width]
+            windows_ref[i, :, : part + RIM] = raw_ref[:, first : first + part + RIM]
         else:
             windows_ref[i, :, :RIM] = before_ref[...]
-            windows_ref[i, :, RIM:] = raw_ref[:, :part]
+            windows_ref[i, :, RIM : part + RIM] = raw_ref[:, :part]
+        windows_ref[i, :, part + RIM :] = before_ref[...]
 
 
 def overlapping(raw_strain, before, count):
     own, samples = raw_strain.shape
     return pl.pallas_call(
         windows_kernel,
-        out_shape=[
-            jax.ShapeDtypeStruct((own, samples + RIM), raw_strain.dtype),
-            jax.ShapeDtypeStruct((count, own, samples // count + RIM), raw_strain.dtype),
-        ],
+        out_shape=jax.ShapeDtypeStruct(
+            (count, own, samples // count + 2 * RIM), raw_strain.dtype
+        ),
         compiler_params=pltpu.CompilerParams(vmem_limit_bytes=16 * 1024 * 1024),
         name="overlapping",
     )(raw_strain, before)
@@ -80,7 +78,7 @@
     lanes = lax.broadcasted_iota(jnp.int32, (64, 128), 1)
     pieces = [
         dot_nt(x_ref[:, first : first + WINDOW], table_ref[...])
-        for first in range(0, x_ref.shape[1] - RIM, STEP)
+        for first in range(0, x_ref.shape[1] - 2 * RIM, STEP)
     ]
     for b in range(kept_ref.shape[0]):
         decimated = jnp.concatenate([p[:, 128 * b : 128 * b + 128] for p in pieces], axis=1)
@@ -229,9 +227,16 @@
         mixed_ref[:rows, first : first + x.shape[1]] = high
         mixed_ref[rows:, first : first + x.shape[1]] = low
 
+    @pl.when(pl.program_id(0) == 0)
+    def _():
+        mix(rim_ref[...].reshape(sources * own, RIM), 0)
+
+    @pl.when(pl.program_id(0) > 0)
+    def _():
+        mixed_ref[:, :RIM] = mixed_ref[:, samples:]
+
     for first in range(0, samples, STEP):
-        mix(x_ref[:, :, first : first + STEP].reshape(sources * own, STEP), first)
-    mix(rim_ref[...].reshape(sources * own, RIM), samples)
+        mix(x_ref[:, :, first : first + STEP].reshape(sources * own, STEP), RIM + first)
     blocks = count // 128
     for b in range(bands):
         windows = [
@@ -245,26 +250,27 @@
             out_ref[b, :, 128 * m : 128 * m + 128] = result[m * own : (m + 1) * own]
 
 
-def denoise(gathered, projector, table):
-    sources, own, extended = gathered.shape
+def denoise(gathered, windows, projector, table):
+    sources, own, block = gathered.shape
     bands = table.shape[0] // 128
     samples = 4096
-    steps = (extended - RIM) // samples
+    steps = block // samples
+    rim_place = windows.shape[2] // RIM - 1
     return pl.pallas_call(
         denoise_kernel,
         grid=(steps,),
         in_specs=[
             pl.BlockSpec((sources, own, samples), lambda i: (0, 0, i)),
-            pl.BlockSpec((sources, own, RIM), lambda i: (0, 0, (i + 1) * (samples // RIM))),
+            pl.BlockSpec((sources, own, RIM), lambda i: (0, 0, rim_place)),
             pl.BlockSpec(projector.shape, lambda i: (0, 0, 0)),
             pl.BlockSpec(table.shape, lambda i: (0, 0)),
         ],
         out_specs=pl.BlockSpec((bands, own, samples // 4), lambda i: (0, 0, i)),
         out_shape=jax.ShapeDtypeStruct((bands, own, steps * samples // 4), jnp.float32),
         scratch_shapes=[pltpu.VMEM((2 * bands * own, samples + RIM), jnp.bfloat16)],
-        compiler_params=pltpu.CompilerParams(vmem_limit_bytes=60 * 1024 * 1024),
+        compiler_params=pltpu.CompilerParams(vmem_limit_bytes=58 * 1024 * 1024),
         name="denoise",
-    )(gathered, gathered, projector, table)
+    )(gathered, windows, projector, table)
 
 
 def shards(raw_strain, fir_taps, start_basis):
@@ -275,19 +281,18 @@
     half = place % 2
     rim_piece = raw_strain[:, samples - RIM :]
     before = lax.ppermute(rim_piece, "tm", [(i, i + 1) for i in range(tm_count - 1)])
-    extended, windows = overlapping(raw_strain, before, chan_count)
-    gathered = lax.all_gather(extended, "chan", axis=0)
-
+    gathered = lax.all_gather(raw_strain, "chan", axis=0)
+
+    windows = overlapping(raw_strain, before, chan_count)
     windows = lax.all_to_all(windows, "chan", 0, 0, tiled=True)
     table = filter_table(fir_taps)
     kept, sent = decimated_gram(core, windows.reshape(channels, -1), table)
 
     quarters = (kept + swapped(sent, "tm", 1)).reshape(chan_count, 80, 128)
     quarter = jnp.sum(lax.all_to_all(quarters, "chan", 0, 0, tiled=True), axis=0)
-    distance = 2
-    while distance < tm_count:
-        quarter = quarter + swapped(quarter, "tm", distance)
-        distance *= 2
+    near = [swapped(quarter, "tm", distance) for distance in (2, 4, 6)]
+    quarter = (quarter + near[0]) + (near[1] + near[2])
+    quarter = quarter + swapped(quarter, "tm", 8)
 
     everyone = range(chan_count * tm_count)
     across = [(i, i ^ (tm_count + 1)) for i in everyone]
@@ -302,7 +307,7 @@
 
     projector = projector.reshape(chan_count, own, channels // 2)
     projector = lax.all_to_all(projector, "chan", 0, 0, tiled=True)
-    return denoise(gathered, projector, table)
+    return denoise(gathered, windows, projector, table)
 
 
 def solution(mesh):

time: 115 us -> 128 us (1.11)
  starting transfers between devices: 27.6 us -> 33.7 us
  waiting for transfers between devices: 24.2 us -> 29.6 us
    ppermute x6 -> x7, starting transfers between devices: 12 us -> 15.5 us  [swapped(): return lax.ppermute(block, axis, route)]
    ppermute x6 -> x7, waiting for transfers between devices: 10.4 us -> 13.3 us  [swapped(): return lax.ppermute(block, axis, route)]
    ppermute x1, starting transfers between devices: 3.89 us -> 6.51 us  [shards(): lax.ppermute(quarter, ('chan', 'tm'), across)]
    all_to_all x1, waiting for transfers between devices: 11.4 us -> 13.5 us  [shards(): windows = lax.all_to_all(windows, 'chan', 0, 0, tiled=True)]
  transfers between devices with their start and end apart: 10 -> 11, of which waited for: 8 -> 8; matrix products, arithmetic and copies ran while one was open for 0% -> 1% of each run, Pallas kernels for 9% -> 9%
where the time goes in v3:
time: 128 us; the launch traced here: 127 us
  starting transfers between devices  33.7 us (26%)
  waiting for transfers between devices  29.6 us (23%)
  blocking collectives  27.6 us (22%)
  Pallas kernels  20.9 us (16%)
  between operations  13.5 us (11%)
  local copies, waits for them, and re-layouts  1.85 us (1%)
    all_to_all x1, blocking collectives, shards(): lax.all_to_all(quarters, 'chan', 0, 0, tiled=True)  16.4 us
    ppermute x7, starting transfers between devices, swapped(): return lax.ppermute(block, axis, route)  15.5 us
    all_to_all x1, waiting for transfers between devices, shards(): windows = lax.all_to_all(windows, 'chan', 0, 0, tiled=True)  13.5 us
    ppermute x7, waiting for transfers between devices, swapped(): return lax.ppermute(block, axis, route)  13.3 us
    all_to_all x1, blocking collectives, shards(): projector = lax.all_to_all(projector, 'chan', 0, 0, tiled=True)  11.2 us
    pallas_call x1, Pallas kernels, denoise(): pl.pallas_call(denoise_kernel, grid=(steps,), in_specs=[pl.BlockSpec((sou...  9.46 us
    pallas_call x1, Pallas kernels, projector_half(): pl.pallas_call(refine_kernel, in_specs=[pl.BlockSpec(memory_space=pltpu.S...  7.02 us
    all_to_all x1, starting transfers between devices, shards(): windows = lax.all_to_all(windows, 'chan', 0, 0, tiled=True)  6.75 us
  transfers between devices with their start and end apart: 11, of which 8 were waited for; matrix products, arithmetic and copies ran while one was open for 1% of the time, Pallas kernels for 9%

profile of v3, /device:TPU:1, one launch (start us, length us, event | category | flops | bytes accessed | tf_op | source)
XLA Modules:
  0.0 127.5 jit_solution(12355638305015638955)
XLA Ops:
  6.5 0.0 copy-start
  6.5 0.0 copy-start.4
  6.5 0.0 all-gather.3.cloned.1.call-start
  6.5 0.7 all-gather.3.cloned.1.call-update
  7.3 0.7 slice.3
  8.0 4.9 %collective-permute-start = (bf16[16,128]{1,0:T(8,128)(2,1)S(1)}, bf16[16,128]{1,0:T(8,128)(2,1)S(1)}, u32[]{:S(2)}, u32[]{:S(2)}) collective-permute-start(bf16[16,128]{1,0:T(8,128)(2,1)S(1)} %slice.3), channel_id=1, source_target_pairs={{0,1},{1,2},{2,3},{3,4},{4,5},{5,6},{6,7},{7,8},{8,9},{9,10},{10,1... | collective-permute-start | bytes 12296 | tf_op jit(solution)/shard_map/ppermute | solution.py:283
  12.9 0.7 collective-permute-done.before_ref
  13.6 0.0 copy-start.3
  13.6 1.0 copy-done.3
  14.7 0.9 overlapping.1
  15.5 6.8 %all-to-all-start = ((bf16[16,16,1280]{2,1,0:T(8,128)(2,1)}), bf16[16,16,1280]{2,1,0:T(8,128)(2,1)S(1)}, u32[]{:S(2)}, u32[]{:S(2)}) async-start(bf16[16,16,1280]{2,1,0:T(8,128)(2,1)} %overlapping.1), calls=%async_computation | async-start | bytes 1310720 | tf_op jit(solution)/shard_map/all_to_all | solution.py:287
  22.3 0.0 copy-done.4
  22.3 0.2 filter_table.1.table_ref
  22.5 0.0 copy-start.1
  22.5 13.5 %all-to-all-done.rim_ref = bf16[16,16,1280]{2,1,0:T(8,128)(2,1)S(1)} async-done(((bf16[16,16,1280]{2,1,0:T(8,128)(2,1)}), bf16[16,16,1280]{2,1,0:T(8,128)(2,1)S(1)}, u32[]{:S(2)}, u32[]{:S(2)}) %all-to-all-start) | async-done | bytes 655392 | tf_op jit(solution)/shard_map/all_to_all | solution.py:287
  36.0 0.0 copy-start.2
  36.0 3.4 %decimated_gram.1 = (f32[8,160,128]{2,1,0:T(8,128)S(1)}, f32[8,160,128]{2,1,0:T(8,128)S(1)}) custom-call(s32[1]{0:T(128)} %bitcast.1.core_ref, bf16[256,1280]{1,0:T(8,128)(2,1)S(1)} %bitcast.8, bf16[1024,640]{1,0:T(8,128)(2,1)S(1)} %filter_table.1.table_ref), custom_call_target="tpu_custom_call" | custom-call | tf_op jit(solution)/shard_map/decimated_gram/pallas_call | solution.py:121
  39.4 0.1 collective-permute-start.1
  39.5 2.1 %collective-permute-done.1 = f32[8,160,128]{2,1,0:T(8,128)S(1)} collective-permute-done((f32[8,160,128]{2,1,0:T(8,128)S(1)}, f32[8,160,128]{2,1,0:T(8,128)S(1)}, u32[]{:S(2)}, u32[]{:S(2)}) %collective-permute-start.1) | collective-permute-done | bytes 655392 | tf_op jit(solution)/shard_map/ppermute | solution.py:18
  41.6 0.1 add.29
  41.7 16.4 %all_to_all.15 = f32[16,80,128]{2,1,0:T(8,128)S(1)} all-to-all(f32[16,80,128]{2,1,0:T(8,128)S(1)} %bitcast.12), channel_id=1, replica_groups=mesh['chan'=16,'tm'=16] {'chan'}, dimensions={0} | all-to-all | bytes 1310720 | tf_op jit(solution)/shard_map/all_to_all | solution.py:292
  58.1 0.0 copy-done.1
  58.1 0.0 copy-done.2
  58.2 11.6 %collective-permute-start.4 = (f32[80,128]{1,0:T(8,128)S(1)}, f32[80,128]{1,0:T(8,128)S(1)}, u32[]{:S(2)}, u32[]{:S(2)}) collective-permute-start(f32[80,128]{1,0:T(8,128)S(1)} %reduce_sum.9), channel_id=1, source_target_pairs={{0,6},{1,7},{2,4},{3,5},{4,2},{5,3},{6,0},{7,1},{8,14},{9,15},{10,... | collective-permute-start | bytes 122888 | tf_op jit(solution)/shard_map/ppermute | solution.py:18
  69.8 0.0 collective-permute-start.3
  69.8 0.4 collective-permute-start.2
  70.2 1.2 collective-permute-done.4
  71.4 2.6 %collective-permute-done.3 = f32[80,128]{1,0:T(8,128)S(1)} collective-permute-done((f32[80,128]{1,0:T(8,128)S(1)}, f32[80,128]{1,0:T(8,128)S(1)}, u32[]{:S(2)}, u32[]{:S(2)}) %collective-permute-start.3) | collective-permute-done | bytes 40992 | tf_op jit(solution)/shard_map/ppermute | solution.py:18
  73.9 0.0 collective-permute-done.2
  73.9 2.0 %collective-permute-start.5 = (f32[80,128]{1,0:T(8,128)S(1)}, f32[80,128]{1,0:T(8,128)S(1)}, u32[]{:S(2)}, u32[]{:S(2)}) collective-permute-start(f32[80,128]{1,0:T(8,128)S(1)} %add_add_fusion), channel_id=1, source_target_pairs={{0,8},{1,9},{2,10},{3,11},{4,12},{5,13},{6,14},{7,15},{8,0},{9,1},... | collective-permute-start | bytes 122888 | tf_op jit(solution)/shard_map/ppermute | solution.py:18
  76.0 0.0 copy-done
  76.0 4.8 %collective-permute-done.5 = f32[80,128]{1,0:T(8,128)S(1)} collective-permute-done((f32[80,128]{1,0:T(8,128)S(1)}, f32[80,128]{1,0:T(8,128)S(1)}, u32[]{:S(2)}, u32[]{:S(2)}) %collective-permute-start.5) | collective-permute-done | bytes 40992 | tf_op jit(solution)/shard_map/ppermute | solution.py:18
  80.8 6.5 %collective-permute-start.8 = (f32[80,128]{1,0:T(8,128)S(1)}, f32[80,128]{1,0:T(8,128)S(1)}, u32[]{:S(2)}, u32[]{:S(2)}) collective-permute-start(f32[80,128]{1,0:T(8,128)S(1)} %add.33.mine_ref), channel_id=1, source_target_pairs={{0,17},{1,16},{2,19},{3,18},{4,21},{5,20},{6,23},{7,22},{8,25},{9,... | collective-permute-start | bytes 122888 | tf_op jit(solution)/shard_map/ppermute | solution.py:303
  87.3 1.4 %collective-permute-start.7 = (f32[80,128]{1,0:T(8,128)S(1)}, f32[80,128]{1,0:T(8,128)S(1)}, u32[]{:S(2)}, u32[]{:S(2)}) collective-permute-start(f32[80,128]{1,0:T(8,128)S(1)} %add.33.mine_ref), channel_id=1, source_target_pairs={{0,16},{16,0},{32,48},{48,32},{64,80},{80,64},{96,112},{112,96},{1... | collective-permute-start | bytes 122888 | tf_op jit(solution)/shard_map/ppermute | solution.py:18
  88.7 0.0 collective-permute-start.6
  88.7 0.1 pad_add_fusion.place_ref
  88.8 0.1 copy.6
  88.9 1.4 %collective-permute-done.8.both_ref = f32[80,128]{1,0:T(8,128)S(1)} collective-permute-done((f32[80,128]{1,0:T(8,128)S(1)}, f32[80,128]{1,0:T(8,128)S(1)}, u32[]{:S(2)}, u32[]{:S(2)}) %collective-permute-start.8) | collective-permute-done | bytes 40992 | tf_op jit(solution)/shard_map/ppermute | solution.py:303
  90.3 2.6 %collective-permute-done.7.chan_ref = f32[80,128]{1,0:T(8,128)S(1)} collective-permute-done((f32[80,128]{1,0:T(8,128)S(1)}, f32[80,128]{1,0:T(8,128)S(1)}, u32[]{:S(2)}, u32[]{:S(2)}) %collective-permute-start.7) | collective-permute-done | bytes 40992 | tf_op jit(solution)/shard_map/ppermute | solution.py:18
  92.9 0.0 collective-permute-done.6.core_ref
  92.9 7.0 %projector_half.1 = f32[256,128]{1,0:T(8,128)S(1)} custom-call(s32[2]{0:T(128)S(1)} %pad_add_fusion.place_ref, f32[80,128]{1,0:T(8,128)S(1)} %add.33.mine_ref, f32[80,128]{1,0:T(8,128)S(1)} %collective-permute-done.6.core_ref, f32[80,128]{1,0:T(8,128)S(1)} %collective-permute-done.7.chan_ref, f32[80,128]{1,0:T(8,128)S(1)} %collective-permute-done.8.both_ref, ...), custom_call_target="tpu_custom_call" | custom-call | tf_op jit(solution)/shard_map/projector_half/pallas_call | solution.py:196
  99.9 11.2 %all_to_all.16.projector_ref = f32[16,16,128]{2,1,0:T(8,128)} all-to-all(f32[16,16,128]{2,1,0:T(8,128)S(1)} %bitcast.10), channel_id=1, replica_groups=mesh['chan'=16,'tm'=16] {'chan'}, dimensions={0} | all-to-all | bytes 262144 | tf_op jit(solution)/shard_map/all_to_all | solution.py:309
  111.2 0.0 all-gather.3.cloned.1.call-done
  111.2 9.5 %denoise.1 = f32[8,16,4096]{2,1,0:T(8,128)} custom-call(bf16[16,16,16384]{2,1,0:T(8,128)(2,1)} %bitcast.11, bf16[16,16,1280]{2,1,0:T(8,128)(2,1)} %copy-done.2, f32[16,16,128]{2,1,0:T(8,128)} %all_to_all.16.projector_ref, bf16[1024,640]{1,0:T(8,128)(2,1)} %copy-done.1), custom_call_target="tpu_custom_call" | custom-call | tf_op jit(solution)/shard_map/denoise/pallas_call | solution.py:259
  (5 shorter events, 0.1 us)
Async XLA Ops:
  6.5 69.5 %copy-start = (f32[8,256,32]{1,2,0:T(8,128)S(1)}, f32[8,256,32]{1,2,0:T(8,128)}, u32[]{:S(2)}) copy-start(f32[8,256,32]{1,2,0:T(8,128)} %param.5) | copy-start | bytes 786436
  6.5 15.8 %copy-start.4 = (bf16[8,128]{1,0:T(8,128)(2,1)S(1)}, bf16[8,128]{1,0:T(8,128)(2,1)}, u32[]{:S(2)}) copy-start(bf16[8,128]{1,0:T(8,128)(2,1)} %param.4) | copy-start | bytes 6148
  6.5 104.6 %all-gather.3.cloned.1.call-start = ((), (), s32[]{:S(2)}) async-start(), calls=%async_computation.3 | async-start | bytes 8912896 | tf_op jit(solution)/shard_map/all_gather | solution.py:284
  8.0 5.7 %collective-permute-start = (bf16[16,128]{1,0:T(8,128)(2,1)S(1)}, bf16[16,128]{1,0:T(8,128)(2,1)S(1)}, u32[]{:S(2)}, u32[]{:S(2)}) collective-permute-start(bf16[16,128]{1,0:T(8,128)(2,1)S(1)} %slice.3), channel_id=1, source_target_pairs={{0,1},{1,2},{2,3},{3,4},{4,5},{5,6},{6,7},{7,8},{8,9},{9,10},{10,1... | collective-permute-start | bytes 12296 | tf_op jit(solution)/shard_map/ppermute | solution.py:283
  13.6 1.0 copy-start.3
  15.5 20.5 %all-to-all-start = ((bf16[16,16,1280]{2,1,0:T(8,128)(2,1)}), bf16[16,16,1280]{2,1,0:T(8,128)(2,1)S(1)}, u32[]{:S(2)}, u32[]{:S(2)}) async-start(bf16[16,16,1280]{2,1,0:T(8,128)(2,1)} %overlapping.1), calls=%async_computation | async-start | bytes 1310720 | tf_op jit(solution)/shard_map/all_to_all | solution.py:287
  22.5 35.6 %copy-start.1 = (bf16[1024,640]{1,0:T(8,128)(2,1)}, bf16[1024,640]{1,0:T(8,128)(2,1)S(1)}, u32[]{:S(2)}) copy-start(bf16[1024,640]{1,0:T(8,128)(2,1)S(1)} %filter_table.1.table_ref) | copy-start | bytes 3932164
  36.0 22.1 %copy-start.2 = (bf16[16,16,1280]{2,1,0:T(8,128)(2,1)}, bf16[16,16,1280]{2,1,0:T(8,128)(2,1)S(1)}, u32[]{:S(2)}) copy-start(bf16[16,16,1280]{2,1,0:T(8,128)(2,1)S(1)} %all-to-all-done.rim_ref) | copy-start | bytes 1966084
  39.4 2.2 %collective-permute-start.1 = (f32[8,160,128]{2,1,0:T(8,128)S(1)}, f32[8,160,128]{2,1,0:T(8,128)S(1)}, u32[]{:S(2)}, u32[]{:S(2)}) collective-permute-start(f32[8,160,128]{2,1,0:T(8,128)S(1)} %get-tuple-element.8), channel_id=1, source_target_pairs={{0,1},{1,0},{2,3},{3,2},{4,5},{5,4},{6,7},{7,6},{8,9},{9,8},{10,11... | collective-permute-start | bytes 1966088 | tf_op jit(solution)/shard_map/ppermute | solution.py:18
  58.2 13.2 %collective-permute-start.4 = (f32[80,128]{1,0:T(8,128)S(1)}, f32[80,128]{1,0:T(8,128)S(1)}, u32[]{:S(2)}, u32[]{:S(2)}) collective-permute-start(f32[80,128]{1,0:T(8,128)S(1)} %reduce_sum.9), channel_id=1, source_target_pairs={{0,6},{1,7},{2,4},{3,5},{4,2},{5,3},{6,0},{7,1},{8,14},{9,15},{10,... | collective-permute-start | bytes 122888 | tf_op jit(solution)/shard_map/ppermute | solution.py:18
  69.8 4.2 %collective-permute-start.3 = (f32[80,128]{1,0:T(8,128)S(1)}, f32[80,128]{1,0:T(8,128)S(1)}, u32[]{:S(2)}, u32[]{:S(2)}) collective-permute-start(f32[80,128]{1,0:T(8,128)S(1)} %reduce_sum.9), channel_id=1, source_target_pairs={{0,4},{1,5},{2,6},{3,7},{4,0},{5,1},{6,2},{7,3},{8,12},{9,13},{10,... | collective-permute-start | bytes 122888 | tf_op jit(solution)/shard_map/ppermute | solution.py:18
  69.8 4.2 %collective-permute-start.2 = (f32[80,128]{1,0:T(8,128)S(1)}, f32[80,128]{1,0:T(8,128)S(1)}, u32[]{:S(2)}, u32[]{:S(2)}) collective-permute-start(f32[80,128]{1,0:T(8,128)S(1)} %reduce_sum.9), channel_id=1, source_target_pairs={{0,2},{1,3},{2,0},{3,1},{4,6},{5,7},{6,4},{7,5},{8,10},{9,11},{10,... | collective-permute-start | bytes 122888 | tf_op jit(solution)/shard_map/ppermute | solution.py:18
  73.9 6.8 %collective-permute-start.5 = (f32[80,128]{1,0:T(8,128)S(1)}, f32[80,128]{1,0:T(8,128)S(1)}, u32[]{:S(2)}, u32[]{:S(2)}) collective-permute-start(f32[80,128]{1,0:T(8,128)S(1)} %add_add_fusion), channel_id=1, source_target_pairs={{0,8},{1,9},{2,10},{3,11},{4,12},{5,13},{6,14},{7,15},{8,0},{9,1},... | collective-permute-start | bytes 122888 | tf_op jit(solution)/shard_map/ppermute | solution.py:18
  80.8 9.5 %collective-permute-start.8 = (f32[80,128]{1,0:T(8,128)S(1)}, f32[80,128]{1,0:T(8,128)S(1)}, u32[]{:S(2)}, u32[]{:S(2)}) collective-permute-start(f32[80,128]{1,0:T(8,128)S(1)} %add.33.mine_ref), channel_id=1, source_target_pairs={{0,17},{1,16},{2,19},{3,18},{4,21},{5,20},{6,23},{7,22},{8,25},{9,... | collective-permute-start | bytes 122888 | tf_op jit(solution)/shard_map/ppermute | solution.py:303
  87.3 5.6 %collective-permute-start.7 = (f32[80,128]{1,0:T(8,128)S(1)}, f32[80,128]{1,0:T(8,128)S(1)}, u32[]{:S(2)}, u32[]{:S(2)}) collective-permute-start(f32[80,128]{1,0:T(8,128)S(1)} %add.33.mine_ref), channel_id=1, source_target_pairs={{0,16},{16,0},{32,48},{48,32},{64,80},{80,64},{96,112},{112,96},{1... | collective-permute-start | bytes 122888 | tf_op jit(solution)/shard_map/ppermute | solution.py:18
  88.7 4.2 %collective-permute-start.6 = (f32[80,128]{1,0:T(8,128)S(1)}, f32[80,128]{1,0:T(8,128)S(1)}, u32[]{:S(2)}, u32[]{:S(2)}) collective-permute-start(f32[80,128]{1,0:T(8,128)S(1)} %add.33.mine_ref), channel_id=1, source_target_pairs={{0,1},{1,0},{2,3},{3,2},{4,5},{5,4},{6,7},{7,6},{8,9},{9,8},{10,11... | collective-permute-start | bytes 122888 | tf_op jit(solution)/shard_map/ppermute | solution.py:18
Sparse Core Ops, SparseCore 0:
  9.8 83.2 all-gather.2

commit v4 on v2

--- a/solution.py
+++ b/solution.py
@@ -51,7 +51,7 @@
             jax.ShapeDtypeStruct((own, samples + RIM), raw_strain.dtype),
             jax.ShapeDtypeStruct((count, own, samples // count + RIM), raw_strain.dtype),
         ],
-        compiler_params=pltpu.CompilerParams(vmem_limit_bytes=16 * 1024 * 1024),
+        compiler_params=pltpu.CompilerParams(vmem_limit_bytes=60 * 1024 * 1024),
         name="overlapping",
     )(raw_strain, before)
 
@@ -262,7 +262,7 @@
         out_specs=pl.BlockSpec((bands, own, samples // 4), lambda i: (0, 0, i)),
         out_shape=jax.ShapeDtypeStruct((bands, own, steps * samples // 4), jnp.float32),
         scratch_shapes=[pltpu.VMEM((2 * bands * own, samples + RIM), jnp.bfloat16)],
-        compiler_params=pltpu.CompilerParams(vmem_limit_bytes=60 * 1024 * 1024),
+        compiler_params=pltpu.CompilerParams(vmem_limit_bytes=58 * 1024 * 1024),
         name="denoise",
     )(gathered, gathered, projector, table)
 
@@ -284,10 +284,9 @@
 
     quarters = (kept + swapped(sent, "tm", 1)).reshape(chan_count, 80, 128)
     quarter = jnp.sum(lax.all_to_all(quarters, "chan", 0, 0, tiled=True), axis=0)
-    distance = 2
-    while distance < tm_count:
-        quarter = quarter + swapped(quarter, "tm", distance)
-        distance *= 2
+    quarter = quarter + swapped(quarter, "tm", 2)
+    others = [swapped(quarter, "tm", distance) for distance in (4, 8, 12)]
+    quarter = (quarter + others[0]) + (others[1] + others[2])
 
     everyone = range(chan_count * tm_count)
     across = [(i, i ^ (tm_count + 1)) for i in everyone]

time: 115 us -> 116 us (level)
  starting transfers between devices: 27.6 us -> 26.2 us
  blocking collectives: 26.5 us -> 27.8 us
    ppermute x6 -> x7, starting transfers between devices: 12 us -> 10.6 us  [swapped(): return lax.ppermute(block, axis, route)]
    all_to_all x1, blocking collectives: 10.2 us -> 11.5 us  [shards(): projector = lax.all_to_all(projector, 'chan', 0, 0, tiled=True)]
    ppermute x6 -> x7, waiting for transfers between devices: 10.4 us -> 11.2 us  [swapped(): return lax.ppermute(block, axis, route)]
  transfers between devices with their start and end apart: 10 -> 11, of which waited for: 8 -> 8; matrix products, arithmetic and copies ran while one was open for 0% -> 0% of each run, Pallas kernels for 9% -> 9%
where the time goes in v4:
time: 116 us
  blocking collectives  27.8 us (24%)
  starting transfers between devices  26.2 us (23%)
  waiting for transfers between devices  24.8 us (21%)
  Pallas kernels  22 us (19%)
  between operations  13.5 us (12%)
  local copies, waits for them, and re-layouts  1.45 us (1%)
    all_to_all x1, blocking collectives, shards(): lax.all_to_all(quarters, 'chan', 0, 0, tiled=True)  16.4 us
    all_to_all x1, blocking collectives, shards(): projector = lax.all_to_all(projector, 'chan', 0, 0, tiled=True)  11.5 us
    all_to_all x1, waiting for transfers between devices, shards(): windows = lax.all_to_all(windows, 'chan', 0, 0, tiled=True)  11.4 us
    ppermute x7, waiting for transfers between devices, swapped(): return lax.ppermute(block, axis, route)  11.2 us
    ppermute x7, starting transfers between devices, swapped(): return lax.ppermute(block, axis, route)  10.6 us
    pallas_call x1, Pallas kernels, denoise(): pl.pallas_call(denoise_kernel, grid=(steps,), in_specs=[pl.BlockSpec((sou...  9.31 us
    pallas_call x1, Pallas kernels, projector_half(): pl.pallas_call(refine_kernel, in_specs=[pl.BlockSpec(memory_space=pltpu.S...  7.01 us
    all_to_all x1, starting transfers between devices, shards(): windows = lax.all_to_all(windows, 'chan', 0, 0, tiled=True)  6.77 us
  transfers between devices with their start and end apart: 11, of which 8 were waited for; matrix products, arithmetic and copies ran while one was open for 0% of the time, Pallas kernels for 9%

profile of v4, /device:TPU:1, one launch (start us, length us, event | category | flops | bytes accessed | tf_op | source)
XLA Modules:
  0.0 116.0 jit_solution(6314117256608086935)
XLA Ops:
  6.5 0.0 copy-start
  6.5 0.0 copy-start.3
  6.5 0.0 all-gather.3.cloned.1.call-start
  6.5 0.7 slice.3
  7.3 4.9 %collective-permute-start = (bf16[16,128]{1,0:T(8,128)(2,1)S(1)}, bf16[16,128]{1,0:T(8,128)(2,1)S(1)}, u32[]{:S(2)}, u32[]{:S(2)}) collective-permute-start(bf16[16,128]{1,0:T(8,128)(2,1)S(1)} %slice.3), channel_id=1, source_target_pairs={{0,1},{1,2},{2,3},{3,4},{4,5},{5,6},{6,7},{7,8},{8,9},{9,10},{10,1... | collective-permute-start | bytes 12296 | tf_op jit(solution)/shard_map/ppermute | solution.py:277
  12.2 0.7 collective-permute-done.before_ref
  12.9 0.0 copy-start.2
  13.0 0.6 copy-done.2
  13.5 2.1 %overlapping.1 = (bf16[16,16512]{1,0:T(8,128)(2,1)}, bf16[16,16,1152]{2,1,0:T(8,128)(2,1)}) custom-call(bf16[16,16384]{1,0:T(8,128)(2,1)} %raw_ref.1, bf16[16,128]{1,0:T(8,128)(2,1)} %copy-done.2), custom_call_target="tpu_custom_call" | custom-call | tf_op jit(solution)/shard_map/overlapping/pallas_call | solution.py:48
  15.6 0.0 all-gather.3.cloned.1.call-update
  15.6 6.8 %all-to-all-start = ((bf16[16,16,1152]{2,1,0:T(8,128)(2,1)}), bf16[16,16,1152]{2,1,0:T(8,128)(2,1)S(1)}, u32[]{:S(2)}, u32[]{:S(2)}) async-start(bf16[16,16,1152]{2,1,0:T(8,128)(2,1)} %get-tuple-element.10), calls=%async_computation | async-start | bytes 1179648 | tf_op jit(solution)/shard_map/all_to_all | solution.py:281
  22.4 0.0 copy-done.3
  22.4 0.2 filter_table.1.table_ref
  22.6 0.0 copy-start.1
  22.6 11.4 %all-to-all-done = bf16[16,16,1152]{2,1,0:T(8,128)(2,1)S(1)} async-done(((bf16[16,16,1152]{2,1,0:T(8,128)(2,1)}), bf16[16,16,1152]{2,1,0:T(8,128)(2,1)S(1)}, u32[]{:S(2)}, u32[]{:S(2)}) %all-to-all-start) | async-done | bytes 589856 | tf_op jit(solution)/shard_map/all_to_all | solution.py:281
  34.0 3.4 %decimated_gram.1 = (f32[8,160,128]{2,1,0:T(8,128)S(1)}, f32[8,160,128]{2,1,0:T(8,128)S(1)}) custom-call(s32[1]{0:T(128)} %bitcast.1.core_ref, bf16[256,1152]{1,0:T(8,128)(2,1)S(1)} %bitcast.8, bf16[1024,640]{1,0:T(8,128)(2,1)S(1)} %filter_table.1.table_ref), custom_call_target="tpu_custom_call" | custom-call | tf_op jit(solution)/shard_map/decimated_gram/pallas_call | solution.py:123
  37.4 0.1 collective-permute-start.1
  37.5 2.1 %collective-permute-done.1 = f32[8,160,128]{2,1,0:T(8,128)S(1)} collective-permute-done((f32[8,160,128]{2,1,0:T(8,128)S(1)}, f32[8,160,128]{2,1,0:T(8,128)S(1)}, u32[]{:S(2)}, u32[]{:S(2)}) %collective-permute-start.1) | collective-permute-done | bytes 655392 | tf_op jit(solution)/shard_map/ppermute | solution.py:18
  39.6 0.1 add.29
  39.7 16.4 %all_to_all.15 = f32[16,80,128]{2,1,0:T(8,128)S(1)} all-to-all(f32[16,80,128]{2,1,0:T(8,128)S(1)} %bitcast.13), channel_id=1, replica_groups=mesh['chan'=16,'tm'=16] {'chan'}, dimensions={0} | all-to-all | bytes 1310720 | tf_op jit(solution)/shard_map/all_to_all | solution.py:286
  56.0 0.0 copy-done.1
  56.1 1.5 %collective-permute-start.2 = (f32[80,128]{1,0:T(8,128)S(1)}, f32[80,128]{1,0:T(8,128)S(1)}, u32[]{:S(2)}, u32[]{:S(2)}) collective-permute-start(f32[80,128]{1,0:T(8,128)S(1)} %reduce_sum.9), channel_id=1, source_target_pairs={{0,2},{1,3},{2,0},{3,1},{4,6},{5,7},{6,4},{7,5},{8,10},{9,11},{10,... | collective-permute-start | bytes 122888 | tf_op jit(solution)/shard_map/ppermute | solution.py:18
  57.6 1.4 %collective-permute-done.2 = f32[80,128]{1,0:T(8,128)S(1)} collective-permute-done((f32[80,128]{1,0:T(8,128)S(1)}, f32[80,128]{1,0:T(8,128)S(1)}, u32[]{:S(2)}, u32[]{:S(2)}) %collective-permute-start.2) | collective-permute-done | bytes 40992 | tf_op jit(solution)/shard_map/ppermute | solution.py:18
  59.0 4.9 %collective-permute-start.5 = (f32[80,128]{1,0:T(8,128)S(1)}, f32[80,128]{1,0:T(8,128)S(1)}, u32[]{:S(2)}, u32[]{:S(2)}) collective-permute-start(f32[80,128]{1,0:T(8,128)S(1)} %add.30), channel_id=1, source_target_pairs={{0,12},{1,13},{2,14},{3,15},{4,8},{5,9},{6,10},{7,11},{8,4},{9,5},... | collective-permute-start | bytes 122888 | tf_op jit(solution)/shard_map/ppermute | solution.py:18
  63.9 2.7 %collective-permute-start.4 = (f32[80,128]{1,0:T(8,128)S(1)}, f32[80,128]{1,0:T(8,128)S(1)}, u32[]{:S(2)}, u32[]{:S(2)}) collective-permute-start(f32[80,128]{1,0:T(8,128)S(1)} %add.30), channel_id=1, source_target_pairs={{0,8},{1,9},{2,10},{3,11},{4,12},{5,13},{6,14},{7,15},{8,0},{9,1},... | collective-permute-start | bytes 122888 | tf_op jit(solution)/shard_map/ppermute | solution.py:18
  66.6 0.0 collective-permute-start.3
  66.7 0.0 copy-done
  66.7 0.0 collective-permute-done.5
  66.7 4.2 %collective-permute-done.4 = f32[80,128]{1,0:T(8,128)S(1)} collective-permute-done((f32[80,128]{1,0:T(8,128)S(1)}, f32[80,128]{1,0:T(8,128)S(1)}, u32[]{:S(2)}, u32[]{:S(2)}) %collective-permute-start.4) | collective-permute-done | bytes 40992 | tf_op jit(solution)/shard_map/ppermute | solution.py:18
  70.9 0.6 collective-permute-done.3
  71.6 3.9 %collective-permute-start.8 = (f32[80,128]{1,0:T(8,128)S(1)}, f32[80,128]{1,0:T(8,128)S(1)}, u32[]{:S(2)}, u32[]{:S(2)}) collective-permute-start(f32[80,128]{1,0:T(8,128)S(1)} %add_add_fusion.mine_ref), channel_id=1, source_target_pairs={{0,17},{1,16},{2,19},{3,18},{4,21},{5,20},{6,23},{7,22},{8,25},{9,... | collective-permute-start | bytes 122888 | tf_op jit(solution)/shard_map/ppermute | solution.py:297
  75.5 1.3 %collective-permute-start.7 = (f32[80,128]{1,0:T(8,128)S(1)}, f32[80,128]{1,0:T(8,128)S(1)}, u32[]{:S(2)}, u32[]{:S(2)}) collective-permute-start(f32[80,128]{1,0:T(8,128)S(1)} %add_add_fusion.mine_ref), channel_id=1, source_target_pairs={{0,16},{16,0},{32,48},{48,32},{64,80},{80,64},{96,112},{112,96},{1... | collective-permute-start | bytes 122888 | tf_op jit(solution)/shard_map/ppermute | solution.py:18
  76.9 0.0 collective-permute-start.6
  76.9 0.1 pad_add_fusion.place_ref
  77.0 0.1 copy.6
  77.1 1.5 %collective-permute-done.8.both_ref = f32[80,128]{1,0:T(8,128)S(1)} collective-permute-done((f32[80,128]{1,0:T(8,128)S(1)}, f32[80,128]{1,0:T(8,128)S(1)}, u32[]{:S(2)}, u32[]{:S(2)}) %collective-permute-start.8) | collective-permute-done | bytes 40992 | tf_op jit(solution)/shard_map/ppermute | solution.py:297
  78.6 2.8 %collective-permute-done.7.chan_ref = f32[80,128]{1,0:T(8,128)S(1)} collective-permute-done((f32[80,128]{1,0:T(8,128)S(1)}, f32[80,128]{1,0:T(8,128)S(1)}, u32[]{:S(2)}, u32[]{:S(2)}) %collective-permute-start.7) | collective-permute-done | bytes 40992 | tf_op jit(solution)/shard_map/ppermute | solution.py:18
  81.4 0.0 collective-permute-done.6.core_ref
  81.4 7.0 %projector_half.1 = f32[256,128]{1,0:T(8,128)S(1)} custom-call(s32[2]{0:T(128)S(1)} %pad_add_fusion.place_ref, f32[80,128]{1,0:T(8,128)S(1)} %add_add_fusion.mine_ref, f32[80,128]{1,0:T(8,128)S(1)} %collective-permute-done.6.core_ref, f32[80,128]{1,0:T(8,128)S(1)} %collective-permute-done.7.chan_ref, f32[80,128]{1,0:T(8,128)S(1)} %collective-permute-done.8.both_ref, ...), custom_call_target="tpu_custom_call" | custom-call | tf_op jit(solution)/shard_map/projector_half/pallas_call | solution.py:198
  88.4 11.5 %all_to_all.16.projector_ref = f32[16,16,128]{2,1,0:T(8,128)} all-to-all(f32[16,16,128]{2,1,0:T(8,128)S(1)} %bitcast.10), channel_id=1, replica_groups=mesh['chan'=16,'tm'=16] {'chan'}, dimensions={0} | all-to-all | bytes 262144 | tf_op jit(solution)/shard_map/all_to_all | solution.py:303
  99.8 0.0 all-gather.3.cloned.1.call-done
  99.8 9.3 %denoise.1 = f32[8,16,4096]{2,1,0:T(8,128)} custom-call(bf16[16,16,16512]{2,1,0:T(8,128)(2,1)} %bitcast.11, bf16[16,16,16512]{2,1,0:T(8,128)(2,1)} %bitcast.12, f32[16,16,128]{2,1,0:T(8,128)} %all_to_all.16.projector_ref, bf16[1024,640]{1,0:T(8,128)(2,1)} %copy-done.1), custom_call_target="tpu_custom_call" | custom-call | tf_op jit(solution)/shard_map/denoise/pallas_call | solution.py:253
  (5 shorter events, 0.1 us)
Async XLA Ops:
  6.5 60.1 %copy-start = (f32[8,256,32]{1,2,0:T(8,128)S(1)}, f32[8,256,32]{1,2,0:T(8,128)}, u32[]{:S(2)}) copy-start(f32[8,256,32]{1,2,0:T(8,128)} %param.5) | copy-start | bytes 786436
  6.5 15.9 %copy-start.3 = (bf16[8,128]{1,0:T(8,128)(2,1)S(1)}, bf16[8,128]{1,0:T(8,128)(2,1)}, u32[]{:S(2)}) copy-start(bf16[8,128]{1,0:T(8,128)(2,1)} %param.4) | copy-start | bytes 6148
  6.5 93.3 %all-gather.3.cloned.1.call-start = ((), (), s32[]{:S(2)}) async-start(), calls=%async_computation.3 | async-start | bytes 8982528 | tf_op jit(solution)/shard_map/all_gather | solution.py:279
  7.3 5.7 %collective-permute-start = (bf16[16,128]{1,0:T(8,128)(2,1)S(1)}, bf16[16,128]{1,0:T(8,128)(2,1)S(1)}, u32[]{:S(2)}, u32[]{:S(2)}) collective-permute-start(bf16[16,128]{1,0:T(8,128)(2,1)S(1)} %slice.3), channel_id=1, source_target_pairs={{0,1},{1,2},{2,3},{3,4},{4,5},{5,6},{6,7},{7,8},{8,9},{9,10},{10,1... | collective-permute-start | bytes 12296 | tf_op jit(solution)/shard_map/ppermute | solution.py:277
  12.9 0.6 copy-start.2
  15.6 18.4 %all-to-all-start = ((bf16[16,16,1152]{2,1,0:T(8,128)(2,1)}), bf16[16,16,1152]{2,1,0:T(8,128)(2,1)S(1)}, u32[]{:S(2)}, u32[]{:S(2)}) async-start(bf16[16,16,1152]{2,1,0:T(8,128)(2,1)} %get-tuple-element.10), calls=%async_computation | async-start | bytes 1179648 | tf_op jit(solution)/shard_map/all_to_all | solution.py:281
  22.6 33.4 %copy-start.1 = (bf16[1024,640]{1,0:T(8,128)(2,1)}, bf16[1024,640]{1,0:T(8,128)(2,1)S(1)}, u32[]{:S(2)}) copy-start(bf16[1024,640]{1,0:T(8,128)(2,1)S(1)} %filter_table.1.table_ref) | copy-start | bytes 3932164
  37.4 2.2 %collective-permute-start.1 = (f32[8,160,128]{2,1,0:T(8,128)S(1)}, f32[8,160,128]{2,1,0:T(8,128)S(1)}, u32[]{:S(2)}, u32[]{:S(2)}) collective-permute-start(f32[8,160,128]{2,1,0:T(8,128)S(1)} %get-tuple-element.12), channel_id=1, source_target_pairs={{0,1},{1,0},{2,3},{3,2},{4,5},{5,4},{6,7},{7,6},{8,9},{9,8},{10,11... | collective-permute-start | bytes 1966088 | tf_op jit(solution)/shard_map/ppermute | solution.py:18
  56.1 2.9 %collective-permute-start.2 = (f32[80,128]{1,0:T(8,128)S(1)}, f32[80,128]{1,0:T(8,128)S(1)}, u32[]{:S(2)}, u32[]{:S(2)}) collective-permute-start(f32[80,128]{1,0:T(8,128)S(1)} %reduce_sum.9), channel_id=1, source_target_pairs={{0,2},{1,3},{2,0},{3,1},{4,6},{5,7},{6,4},{7,5},{8,10},{9,11},{10,... | collective-permute-start | bytes 122888 | tf_op jit(solution)/shard_map/ppermute | solution.py:18
  59.0 7.7 %collective-permute-start.5 = (f32[80,128]{1,0:T(8,128)S(1)}, f32[80,128]{1,0:T(8,128)S(1)}, u32[]{:S(2)}, u32[]{:S(2)}) collective-permute-start(f32[80,128]{1,0:T(8,128)S(1)} %add.30), channel_id=1, source_target_pairs={{0,12},{1,13},{2,14},{3,15},{4,8},{5,9},{6,10},{7,11},{8,4},{9,5},... | collective-permute-start | bytes 122888 | tf_op jit(solution)/shard_map/ppermute | solution.py:18
  63.9 7.0 %collective-permute-start.4 = (f32[80,128]{1,0:T(8,128)S(1)}, f32[80,128]{1,0:T(8,128)S(1)}, u32[]{:S(2)}, u32[]{:S(2)}) collective-permute-start(f32[80,128]{1,0:T(8,128)S(1)} %add.30), channel_id=1, source_target_pairs={{0,8},{1,9},{2,10},{3,11},{4,12},{5,13},{6,14},{7,15},{8,0},{9,1},... | collective-permute-start | bytes 122888 | tf_op jit(solution)/shard_map/ppermute | solution.py:18
  66.6 4.9 %collective-permute-start.3 = (f32[80,128]{1,0:T(8,128)S(1)}, f32[80,128]{1,0:T(8,128)S(1)}, u32[]{:S(2)}, u32[]{:S(2)}) collective-permute-start(f32[80,128]{1,0:T(8,128)S(1)} %add.30), channel_id=1, source_target_pairs={{0,4},{1,5},{2,6},{3,7},{4,0},{5,1},{6,2},{7,3},{8,12},{9,13},{10,... | collective-permute-start | bytes 122888 | tf_op jit(solution)/shard_map/ppermute | solution.py:18
  71.6 7.0 %collective-permute-start.8 = (f32[80,128]{1,0:T(8,128)S(1)}, f32[80,128]{1,0:T(8,128)S(1)}, u32[]{:S(2)}, u32[]{:S(2)}) collective-permute-start(f32[80,128]{1,0:T(8,128)S(1)} %add_add_fusion.mine_ref), channel_id=1, source_target_pairs={{0,17},{1,16},{2,19},{3,18},{4,21},{5,20},{6,23},{7,22},{8,25},{9,... | collective-permute-start | bytes 122888 | tf_op jit(solution)/shard_map/ppermute | solution.py:297
  75.5 5.8 %collective-permute-start.7 = (f32[80,128]{1,0:T(8,128)S(1)}, f32[80,128]{1,0:T(8,128)S(1)}, u32[]{:S(2)}, u32[]{:S(2)}) collective-permute-start(f32[80,128]{1,0:T(8,128)S(1)} %add_add_fusion.mine_ref), channel_id=1, source_target_pairs={{0,16},{16,0},{32,48},{48,32},{64,80},{80,64},{96,112},{112,96},{1... | collective-permute-start | bytes 122888 | tf_op jit(solution)/shard_map/ppermute | solution.py:18
  76.9 4.5 %collective-permute-start.6 = (f32[80,128]{1,0:T(8,128)S(1)}, f32[80,128]{1,0:T(8,128)S(1)}, u32[]{:S(2)}, u32[]{:S(2)}) collective-permute-start(f32[80,128]{1,0:T(8,128)S(1)} %add_add_fusion.mine_ref), channel_id=1, source_target_pairs={{0,1},{1,0},{2,3},{3,2},{4,5},{5,4},{6,7},{7,6},{8,9},{9,8},{10,11... | collective-permute-start | bytes 122888 | tf_op jit(solution)/shard_map/ppermute | solution.py:18
Sparse Core Ops, SparseCore 0:
  15.8 82.9 all-gather.2

commit v5 on v4

--- a/solution.py
+++ b/solution.py
@@ -10,7 +10,7 @@
 STEP = 512
 WINDOW = STEP + RIM
 HIGHEST = lax.Precision.HIGHEST
-VMEM_LIMIT = 40 * 1024 * 1024
+VMEM_LIMIT = 24 * 1024 * 1024
 
 
 def swapped(block, axis, distance):
@@ -29,11 +29,9 @@
     return high, (value - high.astype(jnp.float32)).astype(jnp.bfloat16)
 
 
-def windows_kernel(raw_ref, before_ref, extended_ref, windows_ref):
+def windows_kernel(raw_ref, before_ref, windows_ref):
     count, _, width = windows_ref.shape
     part = width - RIM
-    extended_ref[:, :RIM] = before_ref[...]
-    extended_ref[:, RIM:] = raw_ref[...]
     for i in range(count):
         first = i * part - RIM
         if i:
@@ -47,11 +45,8 @@
     own, samples = raw_strain.shape
     return pl.pallas_call(
         windows_kernel,
-        out_shape=[
-            jax.ShapeDtypeStruct((own, samples + RIM), raw_strain.dtype),
-            jax.ShapeDtypeStruct((count, own, samples // count + RIM), raw_strain.dtype),
-        ],
-        compiler_params=pltpu.CompilerParams(vmem_limit_bytes=60 * 1024 * 1024),
+        out_shape=jax.ShapeDtypeStruct((count, own, samples // count + RIM), raw_strain.dtype),
+        compiler_params=pltpu.CompilerParams(vmem_limit_bytes=16 * 1024 * 1024),
         name="overlapping",
     )(raw_strain, before)
 
@@ -74,7 +69,7 @@
     )(fir_taps[:, None, :])
 
 
-def gram_kernel(core_ref, x_ref, table_ref, kept_ref, sent_ref, packed_ref):
+def gram_kernel(core_ref, x_ref, table_ref, kept_ref, sent_ref, high_ref, low_ref, packed_ref):
     core = core_ref[0]
     count = packed_ref.shape[0] // 2
     lanes = lax.broadcasted_iota(jnp.int32, (64, 128), 1)
@@ -85,6 +80,7 @@
     for b in range(kept_ref.shape[0]):
         decimated = jnp.concatenate([p[:, 128 * b : 128 * b + 128] for p in pieces], axis=1)
         high, low = halves(decimated)
+        high_ref[b], low_ref[b] = high, low
         gram = dot_nt(high, high) + dot_nt(high, low) + dot_nt(low, high)
         packed_ref[0:64, :] = gram[0:64, 0:128]
         packed_ref[64:128, :] = gram[0:64, 128:256]
@@ -120,6 +116,9 @@
     bands = table.shape[0] // 128
     half = jax.ShapeDtypeStruct((bands, 160, 128), jnp.float32)
     half_spec = pl.BlockSpec((2, 160, 128), lambda b: (b, 0, 0))
+    count = (samples - RIM) // 4
+    piece = jax.ShapeDtypeStruct((bands, channels, count), jnp.bfloat16)
+    piece_spec = pl.BlockSpec((2, channels, count), lambda b: (b, 0, 0))
     return pl.pallas_call(
         gram_kernel,
         grid=(bands // 2,),
@@ -128,8 +127,8 @@
             pl.BlockSpec((channels, samples), lambda b: (0, 0)),
             pl.BlockSpec((256, WINDOW), lambda b: (b, 0)),
         ],
-        out_specs=[half_spec, half_spec],
-        out_shape=[half, half],
+        out_specs=[half_spec, half_spec, piece_spec, piece_spec],
+        out_shape=[half, half, piece, piece],
         scratch_shapes=[pltpu.VMEM((320, 128), jnp.float32)],
         compiler_params=pltpu.CompilerParams(vmem_limit_bytes=VMEM_LIMIT),
         name="decimated_gram",
@@ -188,99 +187,95 @@
         )
         basis = dot_nt(image, inverse_cholesky(compact), HIGHEST)
     basis_ref[...] = basis
-    count = out_ref.shape[1]
-    part = basis_ref[pl.ds(pl.multiple_of(half * count, count), count), :]
-    out_ref[...] = dot_nt(basis, part, HIGHEST)
-
-
-def projector_half(place, quarters, start):
-    channels = start.shape[0]
+    rows = lax.broadcasted_iota(jnp.int32, gram_ref.shape, 0)
+    columns = lax.broadcasted_iota(jnp.int32, gram_ref.shape, 1)
+    trace = jnp.sum(jnp.where(rows == columns, gram_ref[...], 0.0), keepdims=True)
+    unit = jnp.sqrt(trace) * 2.0**-15
+    count = out_ref.shape[2]
+    part = basis_ref[pl.ds(pl.multiple_of(half * count, count), count), :].T
+    rank = part.shape[0]
+    for i in range(out_ref.shape[0]):
+        out_ref[i, :rank] = part
+        out_ref[i, rank:] = jnp.broadcast_to(unit, (8, count))
+
+
+def basis_half(place, quarters, start, receivers):
+    channels, rank = start.shape
     return pl.pallas_call(
         refine_kernel,
         in_specs=[pl.BlockSpec(memory_space=pltpu.SMEM)]
         + [pl.BlockSpec(memory_space=pltpu.VMEM)] * 5,
         out_specs=pl.BlockSpec(memory_space=pltpu.VMEM),
-        out_shape=jax.ShapeDtypeStruct((channels, channels // 2), jnp.float32),
+        out_shape=jax.ShapeDtypeStruct((receivers, rank + 8, channels // 2), jnp.float32),
         scratch_shapes=[
             pltpu.VMEM((channels, channels), jnp.float32),
             pltpu.VMEM(start.shape, jnp.float32),
         ],
         compiler_params=pltpu.CompilerParams(vmem_limit_bytes=16 * 1024 * 1024),
-        name="projector_half",
+        name="basis_half",
     )(place, *quarters, start)
 
 
-def denoise_kernel(x_ref, rim_ref, projector_ref, table_ref, out_ref, mixed_ref):
-    bands, own, count = out_ref.shape
-    sources, _, samples = x_ref.shape
-    rows = bands * own
-    projector = jnp.concatenate(
-        [
-            jnp.concatenate([projector_ref[2 * b], projector_ref[2 * b + 1]], axis=1)
-            for b in range(bands)
-        ],
-        axis=0,
-    )
-    stacked = jnp.concatenate(halves(projector), axis=0)
-
-    def mix(x, first):
-        both = jnp.dot(stacked, x, preferred_element_type=jnp.float32)
-        high, low = halves(both[:rows] + both[rows:])
-        mixed_ref[:rows, first : first + x.shape[1]] = high
-        mixed_ref[rows:, first : first + x.shape[1]] = low
-
-    for first in range(0, samples, STEP):
-        mix(x_ref[:, :, first : first + STEP].reshape(sources * own, STEP), first)
-    mix(rim_ref[...].reshape(sources * own, RIM), samples)
-    blocks = count // 128
+def denoise_kernel(basis_ref, high_ref, low_ref, out_ref):
+    receivers, bands, own, _ = out_ref.shape
+    rank = basis_ref.shape[1] - 8
     for b in range(bands):
-        windows = [
-            mixed_ref[part + b * own : part + (b + 1) * own, STEP * m : STEP * m + WINDOW]
-            for part in (0, rows)
-            for m in range(blocks)
-        ]
-        both = dot_nt(jnp.concatenate(windows, axis=0), table_ref[128 * b : 128 * b + 128, :])
-        result = both[: blocks * own] + both[blocks * own :]
-        for m in range(blocks):
-            out_ref[b, :, 128 * m : 128 * m + 128] = result[m * own : (m + 1) * own]
-
-
-def denoise(gathered, projector, table):
-    sources, own, extended = gathered.shape
-    bands = table.shape[0] // 128
-    samples = 4096
-    steps = (extended - RIM) // samples
+        pair = basis_ref[2 * b], basis_ref[2 * b + 1]
+        unit = pair[0][rank : rank + 1, 0:1]
+        basis = jnp.concatenate([pair[0][:rank], pair[1][:rank]], axis=1)
+        basis_high, basis_low = halves(basis)
+        both = jnp.dot(
+            jnp.concatenate([basis_high, basis_low], axis=0),
+            high_ref[b],
+            preferred_element_type=jnp.float32,
+        )
+        coefficients = both[:rank] + both[rank:]
+        coefficients += jnp.dot(basis_high, low_ref[b], preferred_element_type=jnp.float32)
+        left = jnp.concatenate([basis_high, basis_low, basis_high], axis=0)
+        high, low = halves(coefficients * (1.0 / unit))
+        result = lax.dot_general(
+            left,
+            jnp.concatenate([high, high, low], axis=0),
+            (((0,), (0,)), ((), ())),
+            preferred_element_type=jnp.float32,
+        )
+        for i in range(receivers):
+            out_ref[i, b] = result[i * own : (i + 1) * own]
+
+
+def denoise(basis, high, low, receivers):
+    bands, channels, count = high.shape
+    piece_spec = pl.BlockSpec((2, channels, count), lambda b: (b, 0, 0))
+    shape = (receivers, bands, channels // receivers, count)
     return pl.pallas_call(
         denoise_kernel,
-        grid=(steps,),
+        grid=(bands // 2,),
         in_specs=[
-            pl.BlockSpec((sources, own, samples), lambda i: (0, 0, i)),
-            pl.BlockSpec((sources, own, RIM), lambda i: (0, 0, (i + 1) * (samples // RIM))),
-            pl.BlockSpec(projector.shape, lambda i: (0, 0, 0)),
-            pl.BlockSpec(table.shape, lambda i: (0, 0)),
-        ],
-        out_specs=pl.BlockSpec((bands, own, samples // 4), lambda i: (0, 0, i)),
-        out_shape=jax.ShapeDtypeStruct((bands, own, steps * samples // 4), jnp.float32),
-        scratch_shapes=[pltpu.VMEM((2 * bands * own, samples + RIM), jnp.bfloat16)],
-        compiler_params=pltpu.CompilerParams(vmem_limit_bytes=58 * 1024 * 1024),
+            pl.BlockSpec((4,) + basis.shape[1:], lambda b: (b, 0, 0)),
+            piece_spec,
+            piece_spec,
+        ],
+        out_specs=pl.BlockSpec((receivers, 2) + shape[2:], lambda b: (0, b, 0, 0)),
+        out_shape=jax.ShapeDtypeStruct(shape, jnp.float32),
+        compiler_params=pltpu.CompilerParams(vmem_limit_bytes=24 * 1024 * 1024),
         name="denoise",
-    )(gathered, gathered, projector, table)
+    )(basis, high, low)
 
 
 def shards(raw_strain, fir_taps, start_basis):
     own, samples = raw_strain.shape
+    bands = fir_taps.shape[0]
     chan_count, tm_count = lax.axis_size("chan"), lax.axis_size("tm")
     channels = own * chan_count
     place, core = lax.axis_index("chan"), lax.axis_index("tm") % 2
     half = place % 2
     rim_piece = raw_strain[:, samples - RIM :]
     before = lax.ppermute(rim_piece, "tm", [(i, i + 1) for i in range(tm_count - 1)])
-    extended, windows = overlapping(raw_strain, before, chan_count)
-    gathered = lax.all_gather(extended, "chan", axis=0)
-
+
+    windows = overlapping(raw_strain, before, chan_count)
     windows = lax.all_to_all(windows, "chan", 0, 0, tiled=True)
     table = filter_table(fir_taps)
-    kept, sent = decimated_gram(core, windows.reshape(channels, -1), table)
+    kept, sent, high, low = decimated_gram(core, windows.reshape(channels, -1), table)
 
     quarters = (kept + swapped(sent, "tm", 1)).reshape(chan_count, 80, 128)
     quarter = jnp.sum(lax.all_to_all(quarters, "chan", 0, 0, tiled=True), axis=0)
@@ -297,11 +292,14 @@
         lax.ppermute(quarter, ("chan", "tm"), across),
     )
     start = lax.dynamic_index_in_dim(start_basis, place // 2, 0, False)
-    projector = projector_half(jnp.stack([core, half]), four, start)
-
-    projector = projector.reshape(chan_count, own, channels // 2)
-    projector = lax.all_to_all(projector, "chan", 0, 0, tiled=True)
-    return denoise(gathered, projector, table)
+    basis = basis_half(jnp.stack([core, half]), four, start, chan_count)
+
+    basis = lax.all_to_all(basis, "chan", 0, 0, tiled=True)
+    units = basis[::2, start.shape[1], 0]
+    result = denoise(basis, high, low, chan_count).astype(jnp.float16)
+    result = lax.all_to_all(result, "chan", 0, 0, tiled=True)
+    result = result.astype(jnp.float32) * units[None, :, None, None]
+    return jnp.transpose(result, (1, 2, 0, 3)).reshape(bands, own, samples // 4)
 
 
 def solution(mesh):

time: 116 us -> 119 us (1.026)
  between operations: 13.5 us -> 0.14 us
  waiting for transfers between devices: 24.8 us -> 37.5 us
  Pallas kernels: 22 us -> 13.8 us
  starting transfers between devices: 26.2 us -> 31.9 us
  local copies, waits for them, and re-layouts: 1.45 us -> 4.55 us
  other arithmetic: 0.2 us -> 2.96 us
    all_to_all x0 -> x1, waiting for transfers between devices: none -> 14.9 us  [shards(): result = lax.all_to_all(result, 'chan', 0, 0, tiled=True)]
    pallas_call x3, Pallas kernels: 18.4 us -> 10.2 us  [the longest x1 6.74 us: basis_half(): pl.pallas_call(refine_kernel, in_specs=[pl.BlockSpec(memory_space=pltpu.S...]
    all_to_all x0 -> x1, starting transfers between devices: none -> 4.05 us  [shards(): result = lax.all_to_all(result, 'chan', 0, 0, tiled=True)]
    ppermute x7, starting transfers between devices: 10.6 us -> 14.6 us  [swapped(): return lax.ppermute(block, axis, route)]
    ppermute x1, starting transfers between devices: 3.94 us -> 1.51 us  [shards(): lax.ppermute(quarter, ('chan', 'tm'), across)]
    ppermute x7, waiting for transfers between devices: 11.2 us -> 9.18 us  [swapped(): return lax.ppermute(block, axis, route)]
    reshape x0 -> x1, local copies, waits for them, and re-layouts: none -> 1.54 us  [shards(): return jnp.transpose(result, (1, 2, 0, 3)).reshape(bands, own, samples // 4)]
    unnamed x8 -> x10, local copies, waits for them, and re-layouts: 0.6 us -> 2.02 us
  transfers between devices with their start and end apart: 11 -> 11, of which waited for: 8 -> 9; matrix products, arithmetic and copies ran while one was open for 0% -> 0% of each run, Pallas kernels for 9% -> 0%
where the time goes in v5:
time: 119 us; the launch traced here: 118 us
  waiting for transfers between devices  37.5 us (32%)
  starting transfers between devices  31.9 us (27%)
  blocking collectives  27.1 us (23%)
  Pallas kernels  13.8 us (12%)
  local copies, waits for them, and re-layouts  4.55 us (4%)
  other arithmetic  2.96 us (2%)
    all_to_all x1, blocking collectives, shards(): lax.all_to_all(quarters, 'chan', 0, 0, tiled=True)  15.8 us
    all_to_all x1, waiting for transfers between devices, shards(): result = lax.all_to_all(result, 'chan', 0, 0, tiled=True)  14.9 us
    ppermute x7, starting transfers between devices, swapped(): return lax.ppermute(block, axis, route)  14.6 us
    all_to_all x1, waiting for transfers between devices, shards(): windows = lax.all_to_all(windows, 'chan', 0, 0, tiled=True)  11.4 us
    all_to_all x1, blocking collectives, shards(): basis = lax.all_to_all(basis, 'chan', 0, 0, tiled=True)  11.3 us
    ppermute x7, waiting for transfers between devices, swapped(): return lax.ppermute(block, axis, route)  9.18 us
    all_to_all x1, starting transfers between devices, shards(): windows = lax.all_to_all(windows, 'chan', 0, 0, tiled=True)  6.75 us
    pallas_call x1, Pallas kernels, basis_half(): pl.pallas_call(refine_kernel, in_specs=[pl.BlockSpec(memory_space=pltpu.S...  6.74 us
  transfers between devices with their start and end apart: 11, of which 9 were waited for; matrix products, arithmetic and copies ran while one was open for 0% of the time, Pallas kernels for 0%

profile of v5, /device:TPU:1, one launch (start us, length us, event | category | flops | bytes accessed | tf_op | source)
XLA Modules:
  0.0 117.9 jit_solution(15147552121404561645)
XLA Ops:
  0.0 0.0 copy-start
  0.0 0.0 copy-start.4
  0.0 0.7 slice.6
  0.8 4.9 %collective-permute-start = (bf16[16,128]{1,0:T(8,128)(2,1)S(1)}, bf16[16,128]{1,0:T(8,128)(2,1)S(1)}, u32[]{:S(2)}, u32[]{:S(2)}) collective-permute-start(bf16[16,128]{1,0:T(8,128)(2,1)S(1)} %slice.6), channel_id=1, source_target_pairs={{0,1},{1,2},{2,3},{3,4},{4,5},{5,6},{6,7},{7,8},{8,9},{9,10},{10,1... | collective-permute-start | bytes 12296 | tf_op jit(solution)/shard_map/ppermute | solution.py:273
  5.7 0.7 collective-permute-done.before_ref
  6.4 0.0 copy-start.3
  6.4 1.0 copy-done.3
  7.5 0.9 overlapping.1
  8.3 6.8 %all-to-all-start = ((bf16[16,16,1152]{2,1,0:T(8,128)(2,1)}), bf16[16,16,1152]{2,1,0:T(8,128)(2,1)S(1)}, u32[]{:S(2)}, u32[]{:S(2)}) async-start(bf16[16,16,1152]{2,1,0:T(8,128)(2,1)} %overlapping.1), calls=%async_computation | async-start | bytes 1179648 | tf_op jit(solution)/shard_map/all_to_all | solution.py:276
  15.1 0.0 copy-done.4
  15.1 0.2 filter_table.1.table_ref
  15.3 11.4 %all-to-all-done = bf16[16,16,1152]{2,1,0:T(8,128)(2,1)S(1)} async-done(((bf16[16,16,1152]{2,1,0:T(8,128)(2,1)}), bf16[16,16,1152]{2,1,0:T(8,128)(2,1)S(1)}, u32[]{:S(2)}, u32[]{:S(2)}) %all-to-all-start) | async-done | bytes 589856 | tf_op jit(solution)/shard_map/all_to_all | solution.py:276
  26.7 3.5 %decimated_gram.1 = (f32[8,160,128]{2,1,0:T(8,128)S(1)}, f32[8,160,128]{2,1,0:T(8,128)S(1)}, bf16[8,256,256]{2,1,0:T(8,128)(2,1)S(1)}, bf16[8,256,256]{2,1,0:T(8,128)(2,1)S(1)}) custom-call(s32[1]{0:T(128)} %bitcast.core_ref, bf16[256,1152]{1,0:T(8,128)(2,1)S(1)} %bitcast.10, bf16[1024,640]{1,0:T(8,128)(2,1)S(1)} %filter_table.1.table_ref), custom_call_target="tpu_custom_call" | custom-call | tf_op jit(solution)/shard_map/decimated_gram/pallas_call | solution.py:122
  30.1 0.0 copy-start.1
  30.1 1.0 copy-done.1
  31.1 0.0 collective-permute-start.1
  31.1 2.1 %collective-permute-done.1 = f32[8,160,128]{2,1,0:T(8,128)S(1)} collective-permute-done((f32[8,160,128]{2,1,0:T(8,128)S(1)}, f32[8,160,128]{2,1,0:T(8,128)S(1)}, u32[]{:S(2)}, u32[]{:S(2)}) %collective-permute-start.1) | collective-permute-done | bytes 655392 | tf_op jit(solution)/shard_map/ppermute | solution.py:18
  33.2 0.1 add.29
  33.3 0.0 copy-start.2
  33.3 15.8 %all_to_all.20 = f32[16,80,128]{2,1,0:T(8,128)} all-to-all(f32[16,80,128]{2,1,0:T(8,128)S(1)} %bitcast.12), channel_id=1, replica_groups=mesh['chan'=16,'tm'=16] {'chan'}, dimensions={0} | all-to-all | bytes 1310720 | tf_op jit(solution)/shard_map/all_to_all | solution.py:281
  49.1 1.1 reduce_sum.9
  50.2 2.3 %collective-permute-start.2 = (f32[80,128]{1,0:T(8,128)S(1)}, f32[80,128]{1,0:T(8,128)S(1)}, u32[]{:S(2)}, u32[]{:S(2)}) collective-permute-start(f32[80,128]{1,0:T(8,128)S(1)} %reduce_sum.9), channel_id=1, source_target_pairs={{0,2},{1,3},{2,0},{3,1},{4,6},{5,7},{6,4},{7,5},{8,10},{9,11},{10,... | collective-permute-start | bytes 122888 | tf_op jit(solution)/shard_map/ppermute | solution.py:18
  52.5 1.4 %collective-permute-done.2 = f32[80,128]{1,0:T(8,128)S(1)} collective-permute-done((f32[80,128]{1,0:T(8,128)S(1)}, f32[80,128]{1,0:T(8,128)S(1)}, u32[]{:S(2)}, u32[]{:S(2)}) %collective-permute-start.2) | collective-permute-done | bytes 40992 | tf_op jit(solution)/shard_map/ppermute | solution.py:18
  53.9 4.6 %collective-permute-start.3 = (f32[80,128]{1,0:T(8,128)S(1)}, f32[80,128]{1,0:T(8,128)S(1)}, u32[]{:S(2)}, u32[]{:S(2)}) collective-permute-start(f32[80,128]{1,0:T(8,128)S(1)} %add.30), channel_id=1, source_target_pairs={{0,4},{1,5},{2,6},{3,7},{4,0},{5,1},{6,2},{7,3},{8,12},{9,13},{10,... | collective-permute-start | bytes 122888 | tf_op jit(solution)/shard_map/ppermute | solution.py:18
  58.6 2.8 %collective-permute-start.4 = (f32[80,128]{1,0:T(8,128)S(1)}, f32[80,128]{1,0:T(8,128)S(1)}, u32[]{:S(2)}, u32[]{:S(2)}) collective-permute-start(f32[80,128]{1,0:T(8,128)S(1)} %add.30), channel_id=1, source_target_pairs={{0,8},{1,9},{2,10},{3,11},{4,12},{5,13},{6,14},{7,15},{8,0},{9,1},... | collective-permute-start | bytes 122888 | tf_op jit(solution)/shard_map/ppermute | solution.py:18
  61.4 0.6 collective-permute-start.5
  61.9 0.0 copy-done
  61.9 0.0 collective-permute-done.3
  62.0 3.5 %collective-permute-done.4 = f32[80,128]{1,0:T(8,128)S(1)} collective-permute-done((f32[80,128]{1,0:T(8,128)S(1)}, f32[80,128]{1,0:T(8,128)S(1)}, u32[]{:S(2)}, u32[]{:S(2)}) %collective-permute-start.4) | collective-permute-done | bytes 40992 | tf_op jit(solution)/shard_map/ppermute | solution.py:18
  65.4 1.3 %collective-permute-done.5 = f32[80,128]{1,0:T(8,128)S(1)} collective-permute-done((f32[80,128]{1,0:T(8,128)S(1)}, f32[80,128]{1,0:T(8,128)S(1)}, u32[]{:S(2)}, u32[]{:S(2)}) %collective-permute-start.5) | collective-permute-done | bytes 40992 | tf_op jit(solution)/shard_map/ppermute | solution.py:18
  66.7 4.1 %collective-permute-start.6 = (f32[80,128]{1,0:T(8,128)S(1)}, f32[80,128]{1,0:T(8,128)S(1)}, u32[]{:S(2)}, u32[]{:S(2)}) collective-permute-start(f32[80,128]{1,0:T(8,128)S(1)} %add_add_fusion.mine_ref), channel_id=1, source_target_pairs={{0,1},{1,0},{2,3},{3,2},{4,5},{5,4},{6,7},{7,6},{8,9},{9,8},{10,11... | collective-permute-start | bytes 122888 | tf_op jit(solution)/shard_map/ppermute | solution.py:18
  70.8 0.2 collective-permute-start.7
  71.0 1.5 %collective-permute-start.8 = (f32[80,128]{1,0:T(8,128)S(1)}, f32[80,128]{1,0:T(8,128)S(1)}, u32[]{:S(2)}, u32[]{:S(2)}) collective-permute-start(f32[80,128]{1,0:T(8,128)S(1)} %add_add_fusion.mine_ref), channel_id=1, source_target_pairs={{0,17},{1,16},{2,19},{3,18},{4,21},{5,20},{6,23},{7,22},{8,25},{9,... | collective-permute-start | bytes 122888 | tf_op jit(solution)/shard_map/ppermute | solution.py:292
  72.5 0.1 pad_add_fusion.place_ref
  72.6 0.1 copy.6
  72.7 0.0 collective-permute-done.6.core_ref
  72.7 1.0 collective-permute-done.7.chan_ref
  73.7 1.3 %collective-permute-done.8.both_ref = f32[80,128]{1,0:T(8,128)S(1)} collective-permute-done((f32[80,128]{1,0:T(8,128)S(1)}, f32[80,128]{1,0:T(8,128)S(1)}, u32[]{:S(2)}, u32[]{:S(2)}) %collective-permute-start.8) | collective-permute-done | bytes 40992 | tf_op jit(solution)/shard_map/ppermute | solution.py:292
  75.0 6.7 %basis_half.1 = f32[16,40,128]{2,1,0:T(8,128)S(1)} custom-call(s32[2]{0:T(128)S(1)} %pad_add_fusion.place_ref, f32[80,128]{1,0:T(8,128)S(1)} %add_add_fusion.mine_ref, f32[80,128]{1,0:T(8,128)S(1)} %collective-permute-done.6.core_ref, f32[80,128]{1,0:T(8,128)S(1)} %collective-permute-done.7.chan_ref, f32[80,128]{1,0:T(8,128)S(1)} %collective-permute-done.8.both_ref, ...), custom_call_target="tpu_custom_call" | custom-call | tf_op jit(solution)/shard_map/basis_half/pallas_call | solution.py:204
  81.7 11.3 %all_to_all.21.basis_ref = f32[16,40,128]{2,1,0:T(8,128)S(1)} all-to-all(f32[16,40,128]{2,1,0:T(8,128)S(1)} %basis_half.1), channel_id=1, replica_groups=mesh['chan'=16,'tm'=16] {'chan'}, dimensions={0} | all-to-all | bytes 655360 | tf_op jit(solution)/shard_map/all_to_all | solution.py:297
  93.0 0.0 copy-done.2
  93.0 2.6 %denoise.1 = f32[16,8,16,256]{3,2,1,0:T(8,128)S(1)} custom-call(f32[16,40,128]{2,1,0:T(8,128)S(1)} %all_to_all.21.basis_ref, bf16[8,256,256]{2,1,0:T(8,128)(2,1)S(1)} %get-tuple-element.11.high_ref, bf16[8,256,256]{2,1,0:T(8,128)(2,1)S(1)} %copy-done.2), custom_call_target="tpu_custom_call" | custom-call | tf_op jit(solution)/shard_map/denoise/pallas_call | solution.py:250
  95.6 1.3 %convert_element_type.6 = f16[16,8,16,256]{3,2,1,0:T(8,128)(2,1)} convert(f32[16,8,16,256]{3,2,1,0:T(8,128)S(1)} %denoise.1) | non-fusion elementwise | flops 524288 | bytes 3145728 | tf_op jit(solution)/shard_map/convert_element_type | solution.py:299
  96.9 4.0 %all-to-all-start.3 = ((f16[16,8,16,256]{3,2,1,0:T(8,128)(2,1)}), f16[16,8,16,256]{3,2,1,0:T(8,128)(2,1)S(1)}, u32[]{:S(2)}, u32[]{:S(2)}) async-start(f16[16,8,16,256]{3,2,1,0:T(8,128)(2,1)} %convert_element_type.6), calls=%async_computation.3 | async-start | bytes 2097152 | tf_op jit(solution)/shard_map/all_to_all | solution.py:300
  100.9 0.1 slice_reduce_fusion
  101.1 14.9 %all-to-all-done.3 = f16[16,8,16,256]{3,2,1,0:T(8,128)(2,1)S(1)} async-done(((f16[16,8,16,256]{3,2,1,0:T(8,128)(2,1)}), f16[16,8,16,256]{3,2,1,0:T(8,128)(2,1)S(1)}, u32[]{:S(2)}, u32[]{:S(2)}) %all-to-all-start.3) | async-done | bytes 1048608 | tf_op jit(solution)/shard_map/all_to_all | solution.py:300
  116.0 0.4 multiply_bitcast_fusion
  116.3 1.5 %copy.8 = f32[16,8,2,8,256]{4,3,0,2,1:T(8,128)} copy(f32[16,8,2,8,256]{4,3,2,1,0:T(8,128)S(1)} %multiply_bitcast_fusion) | data formatting | bytes 4194304 | tf_op jit(solution)/shard_map/reshape | solution.py:302
  (4 shorter events, 0.0 us)
Async XLA Ops:
  0.0 61.9 %copy-start = (f32[8,256,32]{1,2,0:T(8,128)S(1)}, f32[8,256,32]{1,2,0:T(8,128)}, u32[]{:S(2)}) copy-start(f32[8,256,32]{1,2,0:T(8,128)} %param.5) | copy-start | bytes 786436
  0.0 15.1 %copy-start.4 = (bf16[8,128]{1,0:T(8,128)(2,1)S(1)}, bf16[8,128]{1,0:T(8,128)(2,1)}, u32[]{:S(2)}) copy-start(bf16[8,128]{1,0:T(8,128)(2,1)} %param.4) | copy-start | bytes 6148
  0.8 5.7 %collective-permute-start = (bf16[16,128]{1,0:T(8,128)(2,1)S(1)}, bf16[16,128]{1,0:T(8,128)(2,1)S(1)}, u32[]{:S(2)}, u32[]{:S(2)}) collective-permute-start(bf16[16,128]{1,0:T(8,128)(2,1)S(1)} %slice.6), channel_id=1, source_target_pairs={{0,1},{1,2},{2,3},{3,4},{4,5},{5,6},{6,7},{7,8},{8,9},{9,10},{10,1... | collective-permute-start | bytes 12296 | tf_op jit(solution)/shard_map/ppermute | solution.py:273
  6.4 1.0 copy-start.3
  8.3 18.3 %all-to-all-start = ((bf16[16,16,1152]{2,1,0:T(8,128)(2,1)}), bf16[16,16,1152]{2,1,0:T(8,128)(2,1)S(1)}, u32[]{:S(2)}, u32[]{:S(2)}) async-start(bf16[16,16,1152]{2,1,0:T(8,128)(2,1)} %overlapping.1), calls=%async_computation | async-start | bytes 1179648 | tf_op jit(solution)/shard_map/all_to_all | solution.py:276
  30.1 1.0 copy-start.1
  31.1 2.1 %collective-permute-start.1 = (f32[8,160,128]{2,1,0:T(8,128)S(1)}, f32[8,160,128]{2,1,0:T(8,128)S(1)}, u32[]{:S(2)}, u32[]{:S(2)}) collective-permute-start(f32[8,160,128]{2,1,0:T(8,128)S(1)} %get-tuple-element.10), channel_id=1, source_target_pairs={{0,1},{1,0},{2,3},{3,2},{4,5},{5,4},{6,7},{7,6},{8,9},{9,8},{10,11... | collective-permute-start | bytes 1966088 | tf_op jit(solution)/shard_map/ppermute | solution.py:18
  33.3 59.7 %copy-start.2 = (bf16[8,256,256]{2,1,0:T(8,128)(2,1)S(1)}, bf16[8,256,256]{2,1,0:T(8,128)(2,1)}, u32[]{:S(2)}) copy-start(bf16[8,256,256]{2,1,0:T(8,128)(2,1)} %copy-done.1) | copy-start | bytes 3145732
  50.2 3.7 %collective-permute-start.2 = (f32[80,128]{1,0:T(8,128)S(1)}, f32[80,128]{1,0:T(8,128)S(1)}, u32[]{:S(2)}, u32[]{:S(2)}) collective-permute-start(f32[80,128]{1,0:T(8,128)S(1)} %reduce_sum.9), channel_id=1, source_target_pairs={{0,2},{1,3},{2,0},{3,1},{4,6},{5,7},{6,4},{7,5},{8,10},{9,11},{10,... | collective-permute-start | bytes 122888 | tf_op jit(solution)/shard_map/ppermute | solution.py:18
  53.9 8.0 %collective-permute-start.3 = (f32[80,128]{1,0:T(8,128)S(1)}, f32[80,128]{1,0:T(8,128)S(1)}, u32[]{:S(2)}, u32[]{:S(2)}) collective-permute-start(f32[80,128]{1,0:T(8,128)S(1)} %add.30), channel_id=1, source_target_pairs={{0,4},{1,5},{2,6},{3,7},{4,0},{5,1},{6,2},{7,3},{8,12},{9,13},{10,... | collective-permute-start | bytes 122888 | tf_op jit(solution)/shard_map/ppermute | solution.py:18
  58.6 6.9 %collective-permute-start.4 = (f32[80,128]{1,0:T(8,128)S(1)}, f32[80,128]{1,0:T(8,128)S(1)}, u32[]{:S(2)}, u32[]{:S(2)}) collective-permute-start(f32[80,128]{1,0:T(8,128)S(1)} %add.30), channel_id=1, source_target_pairs={{0,8},{1,9},{2,10},{3,11},{4,12},{5,13},{6,14},{7,15},{8,0},{9,1},... | collective-permute-start | bytes 122888 | tf_op jit(solution)/shard_map/ppermute | solution.py:18
  61.4 5.3 %collective-permute-start.5 = (f32[80,128]{1,0:T(8,128)S(1)}, f32[80,128]{1,0:T(8,128)S(1)}, u32[]{:S(2)}, u32[]{:S(2)}) collective-permute-start(f32[80,128]{1,0:T(8,128)S(1)} %add.30), channel_id=1, source_target_pairs={{0,12},{1,13},{2,14},{3,15},{4,8},{5,9},{6,10},{7,11},{8,4},{9,5},... | collective-permute-start | bytes 122888 | tf_op jit(solution)/shard_map/ppermute | solution.py:18
  66.7 6.0 %collective-permute-start.6 = (f32[80,128]{1,0:T(8,128)S(1)}, f32[80,128]{1,0:T(8,128)S(1)}, u32[]{:S(2)}, u32[]{:S(2)}) collective-permute-start(f32[80,128]{1,0:T(8,128)S(1)} %add_add_fusion.mine_ref), channel_id=1, source_target_pairs={{0,1},{1,0},{2,3},{3,2},{4,5},{5,4},{6,7},{7,6},{8,9},{9,8},{10,11... | collective-permute-start | bytes 122888 | tf_op jit(solution)/shard_map/ppermute | solution.py:18
  70.8 2.9 %collective-permute-start.7 = (f32[80,128]{1,0:T(8,128)S(1)}, f32[80,128]{1,0:T(8,128)S(1)}, u32[]{:S(2)}, u32[]{:S(2)}) collective-permute-start(f32[80,128]{1,0:T(8,128)S(1)} %add_add_fusion.mine_ref), channel_id=1, source_target_pairs={{0,16},{16,0},{32,48},{48,32},{64,80},{80,64},{96,112},{112,96},{1... | collective-permute-start | bytes 122888 | tf_op jit(solution)/shard_map/ppermute | solution.py:18
  71.0 4.0 %collective-permute-start.8 = (f32[80,128]{1,0:T(8,128)S(1)}, f32[80,128]{1,0:T(8,128)S(1)}, u32[]{:S(2)}, u32[]{:S(2)}) collective-permute-start(f32[80,128]{1,0:T(8,128)S(1)} %add_add_fusion.mine_ref), channel_id=1, source_target_pairs={{0,17},{1,16},{2,19},{3,18},{4,21},{5,20},{6,23},{7,22},{8,25},{9,... | collective-permute-start | bytes 122888 | tf_op jit(solution)/shard_map/ppermute | solution.py:292
  96.9 19.1 %all-to-all-start.3 = ((f16[16,8,16,256]{3,2,1,0:T(8,128)(2,1)}), f16[16,8,16,256]{3,2,1,0:T(8,128)(2,1)S(1)}, u32[]{:S(2)}, u32[]{:S(2)}) async-start(f16[16,8,16,256]{3,2,1,0:T(8,128)(2,1)} %convert_element_type.6), calls=%async_computation.3 | async-start | bytes 2097152 | tf_op jit(solution)/shard_map/all_to_all | solution.py:300

commit v6 on v5

v6 whole, which is shorter than its diff:
```python
import jax
import jax.numpy as jnp
from jax import lax
from jax.experimental import pallas as pl
from jax.experimental.pallas import tpu as pltpu
from jax.sharding import PartitionSpec as P

ITERS = 3
RIM = 128
STEP = 512
WINDOW = STEP + RIM
HIGHEST = lax.Precision.HIGHEST
VMEM_LIMIT = 24 * 1024 * 1024


def swapped(block, axis, distance):
    route = [(i, i ^ distance) for i in range(lax.axis_size(axis))]
    return lax.ppermute(block, axis, route)


def dot_nt(a, b, precision=None):
    return lax.dot_general(
        a, b, (((1,), (1,)), ((), ())), precision=precision, preferred_element_type=jnp.float32
    )


def halves(value):
    high = value.astype(jnp.bfloat16)
    return high, (value - high.astype(jnp.float32)).astype(jnp.bfloat16)


def table_kernel(taps_ref, table_ref):
    for b in range(taps_ref.shape[0]):
        row = jnp.concatenate(
            [taps_ref[b].astype(jnp.float32), jnp.zeros((1, STEP), jnp.float32)], axis=1
        )
        table = pltpu.roll(jnp.broadcast_to(row, (128, WINDOW)), 4, 1, stride=4, stride_axis=0)
        table_ref[128 * b : 128 * b + 128, :] = table.astype(table_ref.dtype)


def filter_table(fir_taps):
    return pl.pallas_call(
        table_kernel,
        out_shape=jax.ShapeDtypeStruct((128 * fir_taps.shape[0], WINDOW), fir_taps.dtype),
        compiler_params=pltpu.CompilerParams(vmem_limit_bytes=16 * 1024 * 1024),
        name="filter_table",
    )(fir_taps[:, None, :])


def filter_kernel(raw_ref, before_ref, table_ref, out_ref, extended_ref):
    own, samples = raw_ref.shape
    receivers, _, part = out_ref.shape
    extended_ref[:, :RIM] = before_ref[...]
    extended_ref[:, RIM:] = raw_ref[...]
    blocks = samples // STEP
    windows = jnp.concatenate(
        [extended_ref[:, STEP * m : STEP * m + WINDOW] for m in range(blocks)], axis=0
    )
    bands = table_ref.shape[0] // 128
    share = part // 128
    for pair in range(bands // 2):
        both = dot_nt(windows, table_ref[256 * pair : 256 * pair + 256, :])
        for b in range(2):
            for m in range(blocks):
                place = (2 * pair + b) * (receivers // bands) + m // share
                first = 128 * (m % share)
                out_ref[place, :, first : first + 128] = both[
                    m * own : (m + 1) * own, 128 * b : 128 * b + 128
                ]


def filtered(raw_strain, before, table, receivers):
    own, samples = raw_strain.shape
    part = table.shape[0] // 128 * (samples // 4) // receivers
    return pl.pallas_call(
        filter_kernel,
        out_shape=jax.ShapeDtypeStruct((receivers, own, part), jnp.float32),
        scratch_shapes=[pltpu.VMEM((own, samples + RIM), raw_strain.dtype)],
        compiler_params=pltpu.CompilerParams(vmem_limit_bytes=VMEM_LIMIT),
        name="filtered",
    )(raw_strain, before, table)


def gram_kernel(core_ref, samples_ref, kept_ref, sent_ref, packed_ref):
    core = core_ref[0]
    count = packed_ref.shape[0] // 2
    lanes = lax.broadcasted_iota(jnp.int32, (64, 128), 1)
    high, low = halves(samples_ref[...])
    gram = dot_nt(high, high) + dot_nt(high, low) + dot_nt(low, high)
    packed_ref[0:64, :] = gram[0:64, 0:128]
    packed_ref[64:128, :] = gram[0:64, 128:256]
    packed_ref[128:192, :] = gram[64:128, 128:256]
    packed_ref[192:256, :] = gram[128:192, 128:256]
    last = pltpu.roll(gram[192:256, 128:256], 64, 1)
    packed_ref[256:320, :] = jnp.where(lanes < 64, last, gram[64:128, 0:128])
    kept_ref[...] = packed_ref[pl.ds(pl.multiple_of(core * count, 8), count), :]
    sent_ref[...] = packed_ref[pl.ds(pl.multiple_of((1 - core) * count, 8), count), :]


def band_gram(core, samples):
    half = jax.ShapeDtypeStruct((160, 128), jnp.float32)
    return pl.pallas_call(
        gram_kernel,
        in_specs=[
            pl.BlockSpec(memory_space=pltpu.SMEM),
            pl.BlockSpec(memory_space=pltpu.VMEM),
        ],
        out_shape=[half, half],
        scratch_shapes=[pltpu.VMEM((320, 128), jnp.float32)],
        compiler_params=pltpu.CompilerParams(vmem_limit_bytes=VMEM_LIMIT),
        name="band_gram",
    )(core.reshape(1), samples)


def unpacked(packed):
    first, corner = packed[0:64], packed[256:320]
    upper = jnp.concatenate(
        [first, jnp.concatenate([first.T[64:128], corner[:, 64:128]], axis=1)], axis=0
    )
    third = packed[192:256]
    lower = jnp.concatenate(
        [third, jnp.concatenate([third.T[64:128], corner[:, 0:64]], axis=1)], axis=0
    )
    across = packed[64:192]
    return jnp.concatenate(
        [
            jnp.concatenate([upper, across], axis=1),
            jnp.concatenate([across.T, lower], axis=1),
        ],
        axis=0,
    )


def decimated_gram(core, windows, table):
    channels, samples = windows.shape
    bands = table.shape[0] // 128
    half = jax.ShapeDtypeStruct((bands, 160, 128), jnp.float32)
    half_spec = pl.BlockSpec((2, 160, 128), lambda b: (b, 0, 0))
    count = (samples - RIM) // 4
    piece = jax.ShapeDtypeStruct((bands, channels, count), jnp.bfloat16)
    piece_spec = pl.BlockSpec((2, channels, count), lambda b: (b, 0, 0))
    return pl.pallas_call(
        gram_kernel,
        grid=(bands // 2,),
        in_specs=[
            pl.BlockSpec(memory_space=pltpu.SMEM),
            pl.BlockSpec((channels, samples), lambda b: (0, 0)),
            pl.BlockSpec((256, WINDOW), lambda b: (b, 0)),
        ],
        out_specs=[half_spec, half_spec, piece_spec, piece_spec],
        out_shape=[half, half, piece, piece],
        scratch_shapes=[pltpu.VMEM((320, 128), jnp.float32)],
        compiler_params=pltpu.CompilerParams(vmem_limit_bytes=VMEM_LIMIT),
        name="decimated_gram",
    )(core.reshape(1), windows, table)


def inverse_cholesky(compact):
    rank = compact.shape[0]
    rows = lax.broadcasted_iota(jnp.int32, (rank, rank), 0)
    columns = lax.broadcasted_iota(jnp.int32, (rank, rank), 1)
    unit = (rows == columns).astype(jnp.float32)
    both = jnp.concatenate([compact, unit], axis=1)
    below = lax.broadcasted_iota(jnp.int32, both.shape, 0)
    for block in range(0, rank, 8):
        spread = [
            jnp.broadcast_to(both[:, block + p : block + p + 1], both.shape) for p in range(8)
        ]
        for p in range(8):
            j = block + p
            column = spread[p]
            factor = jnp.where(below > j, column * (1.0 / column[j : j + 1, :]), 0.0)
            both = both - factor * both[j : j + 1, :]
            for q in range(p + 1, 8):
                spread[q] = spread[q] - factor * spread[q][j : j + 1, :]
    pivots = jnp.sum(unit * both[:, :rank], axis=1, keepdims=True)
    return both[:, rank:] / jnp.sqrt(pivots)


def refine_kernel(
    place_ref, mine_ref, core_ref, chan_ref, both_ref, start_ref, samples_ref, out_ref, gram_ref
):
    core, half = place_ref[0], place_ref[1]
    near = jnp.where(core == 0, mine_ref[...], core_ref[...])
    near_next = jnp.where(core == 0, core_ref[...], mine_ref[...])
    far = jnp.where(core == 0, chan_ref[...], both_ref[...])
    far_next = jnp.where(core == 0, both_ref[...], chan_ref[...])
    packed = jnp.concatenate(
        [
            jnp.where(half == 0, near, far),
            jnp.where(half == 0, far, near),
            jnp.where(half == 0, near_next, far_next),
            jnp.where(half == 0, far_next, near_next),
        ],
        axis=0,
    )
    gram_ref[...] = unpacked(packed)
    basis = start_ref[...]
    for _ in range(ITERS):
        image = jnp.dot(gram_ref[...], basis, precision=HIGHEST, preferred_element_type=jnp.float32)
        compact = lax.dot_general(
            image,
            image,
            (((0,), (0,)), ((), ())),
            precision=HIGHEST,
            preferred_element_type=jnp.float32,
        )
        basis = dot_nt(image, inverse_cholesky(compact), HIGHEST)
    basis_high, basis_low = halves(basis)
    left = jnp.concatenate([basis_high, basis_low, basis_high], axis=1)
    rank = basis.shape[1]
    for first in range(0, samples_ref.shape[1], STEP):
        columns = slice(first, first + STEP)
        samples_high, samples_low = halves(samples_ref[:, columns])
        both = lax.dot_general(
            left[:, : 2 * rank],
            samples_high,
            (((0,), (0,)), ((), ())),
            preferred_element_type=jnp.float32,
        )
        coefficients = both[:rank] + both[rank:]
        coefficients += lax.dot_general(
            basis_high,
            samples_low,
            (((0,), (0,)), ((), ())),
            preferred_element_type=jnp.float32,
        )
        high, low = halves(coefficients)
        out_ref[:, columns] = jnp.dot(
            left,
            jnp.concatenate([high, high, low], axis=0),
            preferred_element_type=jnp.float32,
        )


def denoised_band(place, quarters, start, samples):
    channels = start.shape[0]
    return pl.pallas_call(
        refine_kernel,
        in_specs=[pl.BlockSpec(memory_space=pltpu.SMEM)]
        + [pl.BlockSpec(memory_space=pltpu.VMEM)] * 6,
        out_specs=pl.BlockSpec(memory_space=pltpu.VMEM),
        out_shape=jax.ShapeDtypeStruct(samples.shape, jnp.float32),
        scratch_shapes=[pltpu.VMEM((channels, channels), jnp.float32)],
        compiler_params=pltpu.CompilerParams(vmem_limit_bytes=VMEM_LIMIT),
        name="denoised_band",
    )(place, *quarters, start, samples)


def shards(raw_strain, fir_taps, start_basis):
    own, samples = raw_strain.shape
    bands = fir_taps.shape[0]
    chan_count, tm_count = lax.axis_size("chan"), lax.axis_size("tm")
    channels = own * chan_count
    place, core = lax.axis_index("chan"), lax.axis_index("tm") % 2
    half = place % 2
    rim_piece = raw_strain[:, samples - RIM :]
    before = lax.ppermute(rim_piece, "tm", [(i, i + 1) for i in range(tm_count - 1)])
    table = filter_table(fir_taps)

    decimated = filtered(raw_strain, before, table, chan_count)
    decimated = lax.all_to_all(decimated, "chan", 0, 0, tiled=True).reshape(channels, -1)
    kept, sent = band_gram(core, decimated)

    pair = (kept + swapped(sent, "tm", 1)).reshape(2, 80, 128)
    sent = swapped(lax.dynamic_index_in_dim(pair, 1 - half, 0, False), "chan", 1)
    quarter = lax.dynamic_index_in_dim(pair, half, 0, False) + sent
    quarter = quarter + swapped(quarter, "tm", 2)
    others = [swapped(quarter, "tm", distance) for distance in (4, 8, 12)]
    quarter = (quarter + others[0]) + (others[1] + others[2])

    everyone = range(chan_count * tm_count)
    across = [(i, i ^ (tm_count + 1)) for i in everyone]
    four = (
        quarter,
        swapped(quarter, "tm", 1),
        swapped(quarter, "chan", 1),
        lax.ppermute(quarter, ("chan", "tm"), across),
    )
    start = lax.dynamic_index_in_dim(start_basis, place // 2, 0, False)
    result = denoised_band(jnp.stack([core, half]), four, start, decimated)

    result = lax.all_to_all(result.reshape(chan_count, own, -1), "chan", 0, 0, tiled=True)
    result = jnp.transpose(result.reshape(bands, chan_count // bands, own, -1), (0, 2, 1, 3))
    return result.reshape(bands, own, samples // 4)


def solution(mesh):
    placed = (P("chan", "tm"), P(), P())
    return jax.shard_map(
        shards, mesh=mesh, in_specs=placed, out_specs=P(None, "chan", "tm"), check_vma=False
    )
```

time: 119 us -> 125 us (1.050)
  local copies, waits for them, and re-layouts: 4.55 us -> 10.9 us
  blocking collectives: 27.1 us -> 32.5 us
  starting transfers between devices: 31.9 us -> 27.7 us
  waiting for transfers between devices: 37.5 us -> 41.3 us
  Pallas kernels: 13.8 us -> 10.3 us
  other arithmetic: 2.96 us -> 0.11 us
    all_to_all x2 -> x1, blocking collectives: 27.1 us -> 32.5 us  [shards(): lax.all_to_all(result.reshape(chan_count, own, -1), 'chan', 0, 0, tiled=T...]
    reshape x1 -> x2, local copies, waits for them, and re-layouts: 1.54 us -> 6.98 us  [the longest x1 4.01 us: shards(): return result.reshape(bands, own, samples // 4)]
    all_to_all x2 -> x1, starting transfers between devices: 10.8 us -> 6.75 us  [shards(): lax.all_to_all(decimated, 'chan', 0, 0, tiled=True).reshape(channels, -1)]
    pallas_call x4 -> x3, Pallas kernels: 13.6 us -> 10.1 us  [the longest x1 7.95 us: denoised_band(): pl.pallas_call(refine_kernel, in_specs=[pl.BlockSpec(memory_space=pltpu.S...]
    all_to_all x2 -> x1, waiting for transfers between devices: 26.2 us -> 29.7 us  [shards(): lax.all_to_all(decimated, 'chan', 0, 0, tiled=True).reshape(channels, -1)]
    ppermute x7 -> x8, starting transfers between devices: 14.6 us -> 11.8 us  [swapped(): return lax.ppermute(block, axis, route)]
    ppermute x1, starting transfers between devices: 1.51 us -> 4.31 us  [shards(): lax.ppermute(quarter, ('chan', 'tm'), across)]
    ppermute x7 -> x8, waiting for transfers between devices: 9.18 us -> 11.3 us  [swapped(): return lax.ppermute(block, axis, route)]
  transfers between devices with their start and end apart: 11 -> 11, of which waited for: 9 -> 7; matrix products, arithmetic and copies ran while one was open for 0% -> 1% of each run, Pallas kernels for 0% -> 0%
where the time goes in v6:
time: 125 us; the launch traced here: 123 us
  waiting for transfers between devices  41.3 us (33%)
  blocking collectives  32.5 us (26%)
  starting transfers between devices  27.7 us (22%)
  local copies, waits for them, and re-layouts  10.9 us (9%)
  Pallas kernels  10.3 us (8%)
    all_to_all x1, blocking collectives, shards(): lax.all_to_all(result.reshape(chan_count, own, -1), 'chan', 0, 0, tiled=T...  32.5 us
    all_to_all x1, waiting for transfers between devices, shards(): lax.all_to_all(decimated, 'chan', 0, 0, tiled=True).reshape(channels, -1)  29.7 us
    ppermute x8, starting transfers between devices, swapped(): return lax.ppermute(block, axis, route)  11.8 us
    ppermute x8, waiting for transfers between devices, swapped(): return lax.ppermute(block, axis, route)  11.3 us
    pallas_call x1, Pallas kernels, denoised_band(): pl.pallas_call(refine_kernel, in_specs=[pl.BlockSpec(memory_space=pltpu.S...  7.95 us
    all_to_all x1, starting transfers between devices, shards(): lax.all_to_all(decimated, 'chan', 0, 0, tiled=True).reshape(channels, -1)  6.75 us
    ppermute x1, starting transfers between devices, shards(): lax.ppermute(rim_piece, 'tm', [(i, i + 1) for i in range(tm_count - 1)])  4.92 us
    ppermute x1, starting transfers between devices, shards(): lax.ppermute(quarter, ('chan', 'tm'), across)  4.31 us
  transfers between devices with their start and end apart: 11, of which 7 were waited for; matrix products, arithmetic and copies ran while one was open for 1% of the time, Pallas kernels for 0%

profile of v6, /device:TPU:1, one launch (start us, length us, event | category | flops | bytes accessed | tf_op | source)
XLA Modules:
  0.0 123.0 jit_solution(12460480703547173895)
XLA Ops:
  0.0 0.0 copy-start
  0.0 0.7 slice.3
  0.7 4.9 %collective-permute-start = (bf16[16,128]{1,0:T(8,128)(2,1)S(1)}, bf16[16,128]{1,0:T(8,128)(2,1)S(1)}, u32[]{:S(2)}, u32[]{:S(2)}) collective-permute-start(bf16[16,128]{1,0:T(8,128)(2,1)S(1)} %slice.3), channel_id=1, source_target_pairs={{0,1},{1,2},{2,3},{3,4},{4,5},{5,6},{6,7},{7,8},{8,9},{9,10},{10,1... | collective-permute-start | bytes 12296 | tf_op jit(solution)/shard_map/ppermute | solution.py:258
  5.7 0.7 copy.6.taps_ref
  6.4 0.2 filter_table.1.table_ref
  6.5 0.0 collective-permute-done.before_ref
  6.6 0.0 copy-start.2
  6.6 1.0 copy-done.2
  7.6 1.0 filtered.1
  8.6 0.0 copy-start.1
  8.7 1.3 %copy-done.1 = f32[16,16,2048]{2,1,0:T(8,128)} copy-done((f32[16,16,2048]{2,1,0:T(8,128)}, f32[16,16,2048]{2,1,0:T(8,128)S(1)}, u32[]{:S(2)}) %copy-start.1) | copy-done | bytes 2097176
  10.0 6.8 %all-to-all-start = ((f32[16,16,2048]{2,1,0:T(8,128)}), f32[16,16,2048]{2,1,0:T(8,128)S(1)}, u32[]{:S(2)}, u32[]{:S(2)}) async-start(f32[16,16,2048]{2,1,0:T(8,128)} %copy-done.1), calls=%async_computation | async-start | bytes 4194304 | tf_op jit(solution)/shard_map/all_to_all | solution.py:262
  16.7 29.7 %all-to-all-done = f32[16,16,2048]{2,1,0:T(8,128)S(1)} async-done(((f32[16,16,2048]{2,1,0:T(8,128)}), f32[16,16,2048]{2,1,0:T(8,128)S(1)}, u32[]{:S(2)}, u32[]{:S(2)}) %all-to-all-start) | async-done | bytes 2097184 | tf_op jit(solution)/shard_map/all_to_all | solution.py:262
  46.4 1.1 band_gram.1
  47.5 0.1 collective-permute-start.1
  47.7 1.2 %collective-permute-done.1 = f32[160,128]{1,0:T(8,128)S(1)} collective-permute-done((f32[160,128]{1,0:T(8,128)S(1)}, f32[160,128]{1,0:T(8,128)S(1)}, u32[]{:S(2)}, u32[]{:S(2)}) %collective-permute-start.1) | collective-permute-done | bytes 81952 | tf_op jit(solution)/shard_map/ppermute | solution.py:18
  48.9 0.5 collective-permute-start.2
  49.5 2.4 %collective-permute-done.2 = f32[80,128]{1,0:T(8,128)S(1)} collective-permute-done((f32[80,128]{1,0:T(8,128)S(1)}, f32[80,128]{1,0:T(8,128)S(1)}, u32[]{:S(2)}, u32[]{:S(2)}) %collective-permute-start.2) | collective-permute-done | bytes 40992 | tf_op jit(solution)/shard_map/ppermute | solution.py:18
  51.9 3.1 %collective-permute-start.3 = (f32[80,128]{1,0:T(8,128)S(1)}, f32[80,128]{1,0:T(8,128)S(1)}, u32[]{:S(2)}, u32[]{:S(2)}) collective-permute-start(f32[80,128]{1,0:T(8,128)S(1)} %bitcast_add_fusion), channel_id=1, source_target_pairs={{0,2},{1,3},{2,0},{3,1},{4,6},{5,7},{6,4},{7,5},{8,10},{9,11},{10,... | collective-permute-start | bytes 122888 | tf_op jit(solution)/shard_map/ppermute | solution.py:18
  54.9 1.4 %collective-permute-done.3 = f32[80,128]{1,0:T(8,128)S(1)} collective-permute-done((f32[80,128]{1,0:T(8,128)S(1)}, f32[80,128]{1,0:T(8,128)S(1)}, u32[]{:S(2)}, u32[]{:S(2)}) %collective-permute-start.3) | collective-permute-done | bytes 40992 | tf_op jit(solution)/shard_map/ppermute | solution.py:18
  56.3 4.3 %collective-permute-start.6 = (f32[80,128]{1,0:T(8,128)S(1)}, f32[80,128]{1,0:T(8,128)S(1)}, u32[]{:S(2)}, u32[]{:S(2)}) collective-permute-start(f32[80,128]{1,0:T(8,128)S(1)} %add.44), channel_id=1, source_target_pairs={{0,12},{1,13},{2,14},{3,15},{4,8},{5,9},{6,10},{7,11},{8,4},{9,5},... | collective-permute-start | bytes 122888 | tf_op jit(solution)/shard_map/ppermute | solution.py:18
  60.6 2.6 %collective-permute-start.5 = (f32[80,128]{1,0:T(8,128)S(1)}, f32[80,128]{1,0:T(8,128)S(1)}, u32[]{:S(2)}, u32[]{:S(2)}) collective-permute-start(f32[80,128]{1,0:T(8,128)S(1)} %add.44), channel_id=1, source_target_pairs={{0,8},{1,9},{2,10},{3,11},{4,12},{5,13},{6,14},{7,15},{8,0},{9,1},... | collective-permute-start | bytes 122888 | tf_op jit(solution)/shard_map/ppermute | solution.py:18
  63.2 0.0 collective-permute-start.4
  63.2 0.0 copy-done
  63.2 0.0 collective-permute-done.6
  63.2 4.4 %collective-permute-done.5 = f32[80,128]{1,0:T(8,128)S(1)} collective-permute-done((f32[80,128]{1,0:T(8,128)S(1)}, f32[80,128]{1,0:T(8,128)S(1)}, u32[]{:S(2)}, u32[]{:S(2)}) %collective-permute-start.5) | collective-permute-done | bytes 40992 | tf_op jit(solution)/shard_map/ppermute | solution.py:18
  67.6 0.0 collective-permute-done.4
  67.6 4.3 %collective-permute-start.9 = (f32[80,128]{1,0:T(8,128)S(1)}, f32[80,128]{1,0:T(8,128)S(1)}, u32[]{:S(2)}, u32[]{:S(2)}) collective-permute-start(f32[80,128]{1,0:T(8,128)S(1)} %add_add_fusion.mine_ref), channel_id=1, source_target_pairs={{0,17},{1,16},{2,19},{3,18},{4,21},{5,20},{6,23},{7,22},{8,25},{9,... | collective-permute-start | bytes 122888 | tf_op jit(solution)/shard_map/ppermute | solution.py:278
  71.9 1.2 collective-permute-start.8
  73.1 0.0 collective-permute-start.7
  73.1 0.1 pad_add_fusion.place_ref
  73.2 0.1 copy.7
  73.3 0.3 collective-permute-done.9.both_ref
  73.6 1.9 %collective-permute-done.8.chan_ref = f32[80,128]{1,0:T(8,128)S(1)} collective-permute-done((f32[80,128]{1,0:T(8,128)S(1)}, f32[80,128]{1,0:T(8,128)S(1)}, u32[]{:S(2)}, u32[]{:S(2)}) %collective-permute-start.8) | collective-permute-done | bytes 40992 | tf_op jit(solution)/shard_map/ppermute | solution.py:18
  75.5 0.0 collective-permute-done.7.core_ref
  75.5 8.0 %denoised_band.1 = f32[256,2048]{1,0:T(8,128)S(1)} custom-call(s32[2]{0:T(128)S(1)} %pad_add_fusion.place_ref, f32[80,128]{1,0:T(8,128)S(1)} %add_add_fusion.mine_ref, f32[80,128]{1,0:T(8,128)S(1)} %collective-permute-done.7.core_ref, f32[80,128]{1,0:T(8,128)S(1)} %collective-permute-done.8.chan_ref, f32[80,128]{1,0:T(8,128)S(1)} %collective-permute-done.9.both_ref, ...), custom_call_target="tpu_custom_call" | custom-call | tf_op jit(solution)/shard_map/denoised_band/pallas_call | solution.py:238
  83.5 32.5 %all_to_all.10 = f32[16,16,2048]{2,1,0:T(8,128)S(1)} all-to-all(f32[16,16,2048]{2,1,0:T(8,128)S(1)} %bitcast.17), channel_id=1, replica_groups=mesh['chan'=16,'tm'=16] {'chan'}, dimensions={0} | all-to-all | bytes 4194304 | tf_op jit(solution)/shard_map/all_to_all | solution.py:283
  116.0 3.0 %copy.10 = f32[8,2,16,2048]{3,1,2,0:T(2,128)} copy(f32[8,2,16,2048]{3,2,1,0:T(8,128)S(1)} %bitcast.19) | data formatting | bytes 4194304 | tf_op jit(solution)/shard_map/reshape | solution.py:284
  119.0 4.0 %reshape.20 = f32[8,16,4096]{2,1,0:T(8,128)} reshape(f32[8,16,2,2048]{3,2,1,0:T(2,128)} %bitcast.20) | data formatting | bytes 4194304 | tf_op jit(solution)/shard_map/reshape | solution.py:285
  (6 shorter events, 0.1 us)
Async XLA Ops:
  0.0 63.2 %copy-start = (f32[8,256,32]{1,2,0:T(8,128)S(1)}, f32[8,256,32]{1,2,0:T(8,128)}, u32[]{:S(2)}) copy-start(f32[8,256,32]{1,2,0:T(8,128)} %param.5) | copy-start | bytes 786436
  0.7 5.8 %collective-permute-start = (bf16[16,128]{1,0:T(8,128)(2,1)S(1)}, bf16[16,128]{1,0:T(8,128)(2,1)S(1)}, u32[]{:S(2)}, u32[]{:S(2)}) collective-permute-start(bf16[16,128]{1,0:T(8,128)(2,1)S(1)} %slice.3), channel_id=1, source_target_pairs={{0,1},{1,2},{2,3},{3,4},{4,5},{5,6},{6,7},{7,8},{8,9},{9,10},{10,1... | collective-permute-start | bytes 12296 | tf_op jit(solution)/shard_map/ppermute | solution.py:258
  6.6 1.0 copy-start.2
  8.6 1.3 %copy-start.1 = (f32[16,16,2048]{2,1,0:T(8,128)}, f32[16,16,2048]{2,1,0:T(8,128)S(1)}, u32[]{:S(2)}) copy-start(f32[16,16,2048]{2,1,0:T(8,128)S(1)} %filtered.1) | copy-start | bytes 6291460
  10.0 36.5 %all-to-all-start = ((f32[16,16,2048]{2,1,0:T(8,128)}), f32[16,16,2048]{2,1,0:T(8,128)S(1)}, u32[]{:S(2)}, u32[]{:S(2)}) async-start(f32[16,16,2048]{2,1,0:T(8,128)} %copy-done.1), calls=%async_computation | async-start | bytes 4194304 | tf_op jit(solution)/shard_map/all_to_all | solution.py:262
  47.5 1.4 %collective-permute-start.1 = (f32[160,128]{1,0:T(8,128)S(1)}, f32[160,128]{1,0:T(8,128)S(1)}, u32[]{:S(2)}, u32[]{:S(2)}) collective-permute-start(f32[160,128]{1,0:T(8,128)S(1)} %get-tuple-element.8), channel_id=1, source_target_pairs={{0,1},{1,0},{2,3},{3,2},{4,5},{5,4},{6,7},{7,6},{8,9},{9,8},{10,11... | collective-permute-start | bytes 245768 | tf_op jit(solution)/shard_map/ppermute | solution.py:18
  48.9 2.9 %collective-permute-start.2 = (f32[80,128]{1,0:T(8,128)S(1)}, f32[80,128]{1,0:T(8,128)S(1)}, u32[]{:S(2)}, u32[]{:S(2)}) collective-permute-start(f32[80,128]{1,0:T(8,128)S(1)} %dynamic-slice_bitcast_fusion), channel_id=1, source_target_pairs={{0,16},{16,0},{32,48},{48,32},{64,80},{80,64},{96,112},{112,96},{1... | collective-permute-start | bytes 122888 | tf_op jit(solution)/shard_map/ppermute | solution.py:18
  51.9 4.4 %collective-permute-start.3 = (f32[80,128]{1,0:T(8,128)S(1)}, f32[80,128]{1,0:T(8,128)S(1)}, u32[]{:S(2)}, u32[]{:S(2)}) collective-permute-start(f32[80,128]{1,0:T(8,128)S(1)} %bitcast_add_fusion), channel_id=1, source_target_pairs={{0,2},{1,3},{2,0},{3,1},{4,6},{5,7},{6,4},{7,5},{8,10},{9,11},{10,... | collective-permute-start | bytes 122888 | tf_op jit(solution)/shard_map/ppermute | solution.py:18
  56.3 6.9 %collective-permute-start.6 = (f32[80,128]{1,0:T(8,128)S(1)}, f32[80,128]{1,0:T(8,128)S(1)}, u32[]{:S(2)}, u32[]{:S(2)}) collective-permute-start(f32[80,128]{1,0:T(8,128)S(1)} %add.44), channel_id=1, source_target_pairs={{0,12},{1,13},{2,14},{3,15},{4,8},{5,9},{6,10},{7,11},{8,4},{9,5},... | collective-permute-start | bytes 122888 | tf_op jit(solution)/shard_map/ppermute | solution.py:18
  60.6 7.0 %collective-permute-start.5 = (f32[80,128]{1,0:T(8,128)S(1)}, f32[80,128]{1,0:T(8,128)S(1)}, u32[]{:S(2)}, u32[]{:S(2)}) collective-permute-start(f32[80,128]{1,0:T(8,128)S(1)} %add.44), channel_id=1, source_target_pairs={{0,8},{1,9},{2,10},{3,11},{4,12},{5,13},{6,14},{7,15},{8,0},{9,1},... | collective-permute-start | bytes 122888 | tf_op jit(solution)/shard_map/ppermute | solution.py:18
  63.2 4.4 %collective-permute-start.4 = (f32[80,128]{1,0:T(8,128)S(1)}, f32[80,128]{1,0:T(8,128)S(1)}, u32[]{:S(2)}, u32[]{:S(2)}) collective-permute-start(f32[80,128]{1,0:T(8,128)S(1)} %add.44), channel_id=1, source_target_pairs={{0,4},{1,5},{2,6},{3,7},{4,0},{5,1},{6,2},{7,3},{8,12},{9,13},{10,... | collective-permute-start | bytes 122888 | tf_op jit(solution)/shard_map/ppermute | solution.py:18
  67.6 6.0 %collective-permute-start.9 = (f32[80,128]{1,0:T(8,128)S(1)}, f32[80,128]{1,0:T(8,128)S(1)}, u32[]{:S(2)}, u32[]{:S(2)}) collective-permute-start(f32[80,128]{1,0:T(8,128)S(1)} %add_add_fusion.mine_ref), channel_id=1, source_target_pairs={{0,17},{1,16},{2,19},{3,18},{4,21},{5,20},{6,23},{7,22},{8,25},{9,... | collective-permute-start | bytes 122888 | tf_op jit(solution)/shard_map/ppermute | solution.py:278
  71.9 3.6 %collective-permute-start.8 = (f32[80,128]{1,0:T(8,128)S(1)}, f32[80,128]{1,0:T(8,128)S(1)}, u32[]{:S(2)}, u32[]{:S(2)}) collective-permute-start(f32[80,128]{1,0:T(8,128)S(1)} %add_add_fusion.mine_ref), channel_id=1, source_target_pairs={{0,16},{16,0},{32,48},{48,32},{64,80},{80,64},{96,112},{112,96},{1... | collective-permute-start | bytes 122888 | tf_op jit(solution)/shard_map/ppermute | solution.py:18
  73.1 2.4 %collective-permute-start.7 = (f32[80,128]{1,0:T(8,128)S(1)}, f32[80,128]{1,0:T(8,128)S(1)}, u32[]{:S(2)}, u32[]{:S(2)}) collective-permute-start(f32[80,128]{1,0:T(8,128)S(1)} %add_add_fusion.mine_ref), channel_id=1, source_target_pairs={{0,1},{1,0},{2,3},{3,2},{4,5},{5,4},{6,7},{7,6},{8,9},{9,8},{10,11... | collective-permute-start | bytes 122888 | tf_op jit(solution)/shard_map/ppermute | solution.py:18

commit v7 on v6

--- a/solution.py
+++ b/solution.py
@@ -11,6 +11,9 @@
 WINDOW = STEP + RIM
 HIGHEST = lax.Precision.HIGHEST
 VMEM_LIMIT = 24 * 1024 * 1024
+SENT = jnp.float16
+RESULT_SENT = jnp.float32
+POWERS = (14,) * 9 + (8, 4, 2, 1)
 
 
 def swapped(block, axis, distance):
@@ -47,9 +50,49 @@
     )(fir_taps[:, None, :])
 
 
+def powers_below(value):
+    value = jnp.maximum(value, 2.0**-100)
+    factors = []
+    for power in POWERS:
+        factor = jnp.where(
+            value >= 2.0**power, 2.0**power, jnp.where(value < 2.0**-power, 2.0**-power, 1.0)
+        )
+        value = value / factor
+        factors.append(factor)
+    return factors
+
+
+def product(factors):
+    total = factors[0]
+    for factor in factors[1:]:
+        total = total * factor
+    return total
+
+
+def on_lanes(factors, shape):
+    lanes = lax.broadcasted_iota(jnp.int32, shape, len(shape) - 1)
+    result = jnp.ones(shape, jnp.float32)
+    for number, factor in enumerate(factors):
+        result = jnp.where(lanes == number, factor, result)
+    return result
+
+
+def off_lanes(row):
+    return product([row[..., number : number + 1] for number in range(len(POWERS))])
+
+
 def filter_kernel(raw_ref, before_ref, table_ref, out_ref, extended_ref):
     own, samples = raw_ref.shape
-    receivers, _, part = out_ref.shape
+    receivers, _, width = out_ref.shape
+    part = width - 128
+    largest = jnp.max(jnp.abs(raw_ref[...].astype(jnp.float32)), keepdims=True)
+    before = jnp.max(jnp.abs(before_ref[...].astype(jnp.float32)), keepdims=True)
+    tap = jnp.max(jnp.abs(table_ref[...].astype(jnp.float32)), keepdims=True)
+    factors = powers_below(jnp.maximum(largest, before) * tap * 2.0**-7)
+    scale = 1.0 / product(factors)
+    marks = on_lanes(factors, (own, 128))
+    for i in range(receivers):
+        out_ref[i, :, part:] = marks
     extended_ref[:, :RIM] = before_ref[...]
     extended_ref[:, RIM:] = raw_ref[...]
     blocks = samples // STEP
@@ -59,7 +102,7 @@
     bands = table_ref.shape[0] // 128
     share = part // 128
     for pair in range(bands // 2):
-        both = dot_nt(windows, table_ref[256 * pair : 256 * pair + 256, :])
+        both = dot_nt(windows, table_ref[256 * pair : 256 * pair + 256, :]) * scale
         for b in range(2):
             for m in range(blocks):
                 place = (2 * pair + b) * (receivers // bands) + m // share
@@ -74,17 +117,21 @@
     part = table.shape[0] // 128 * (samples // 4) // receivers
     return pl.pallas_call(
         filter_kernel,
-        out_shape=jax.ShapeDtypeStruct((receivers, own, part), jnp.float32),
+        out_shape=jax.ShapeDtypeStruct((receivers, own, part + 128), jnp.float32),
         scratch_shapes=[pltpu.VMEM((own, samples + RIM), raw_strain.dtype)],
         compiler_params=pltpu.CompilerParams(vmem_limit_bytes=VMEM_LIMIT),
         name="filtered",
     )(raw_strain, before, table)
 
 
-def gram_kernel(core_ref, samples_ref, kept_ref, sent_ref, packed_ref):
+def gram_kernel(core_ref, message_ref, kept_ref, sent_ref, samples_ref, packed_ref):
     core = core_ref[0]
     count = packed_ref.shape[0] // 2
     lanes = lax.broadcasted_iota(jnp.int32, (64, 128), 1)
+    sources, own, width = message_ref.shape
+    for i in range(sources):
+        unit = off_lanes(message_ref[i, 0:1, width - 128 :])
+        samples_ref[i * own : (i + 1) * own, :] = message_ref[i, :, : width - 128] * unit
     high, low = halves(samples_ref[...])
     gram = dot_nt(high, high) + dot_nt(high, low) + dot_nt(low, high)
     packed_ref[0:64, :] = gram[0:64, 0:128]
@@ -97,7 +144,9 @@
     sent_ref[...] = packed_ref[pl.ds(pl.multiple_of((1 - core) * count, 8), count), :]
 
 
-def band_gram(core, samples):
+def band_gram(core, message):
+    sources, own, width = message.shape
+    samples = jax.ShapeDtypeStruct((sources * own, width - 128), jnp.float32)
     half = jax.ShapeDtypeStruct((160, 128), jnp.float32)
     return pl.pallas_call(
         gram_kernel,
@@ -105,11 +154,11 @@
             pl.BlockSpec(memory_space=pltpu.SMEM),
             pl.BlockSpec(memory_space=pltpu.VMEM),
         ],
-        out_shape=[half, half],
+        out_shape=[half, half, samples],
         scratch_shapes=[pltpu.VMEM((320, 128), jnp.float32)],
         compiler_params=pltpu.CompilerParams(vmem_limit_bytes=VMEM_LIMIT),
         name="band_gram",
-    )(core.reshape(1), samples)
+    )(core.reshape(1), message)
 
 
 def unpacked(packed):
@@ -206,10 +255,17 @@
             preferred_element_type=jnp.float32,
         )
         basis = dot_nt(image, inverse_cholesky(compact), HIGHEST)
+    rows = lax.broadcasted_iota(jnp.int32, gram_ref.shape, 0)
+    columns = lax.broadcasted_iota(jnp.int32, gram_ref.shape, 1)
+    trace = jnp.sum(jnp.where(rows == columns, gram_ref[...], 0.0), keepdims=True)
+    factors = powers_below(jnp.sqrt(trace) * 2.0**-14)
+    scale = 1.0 / product(factors)
+    part = samples_ref.shape[1]
+    out_ref[:, part:] = on_lanes(factors, (out_ref.shape[0], 128))
     basis_high, basis_low = halves(basis)
     left = jnp.concatenate([basis_high, basis_low, basis_high], axis=1)
     rank = basis.shape[1]
-    for first in range(0, samples_ref.shape[1], STEP):
+    for first in range(0, part, STEP):
         columns = slice(first, first + STEP)
         samples_high, samples_low = halves(samples_ref[:, columns])
         both = lax.dot_general(
@@ -225,7 +281,7 @@
             (((0,), (0,)), ((), ())),
             preferred_element_type=jnp.float32,
         )
-        high, low = halves(coefficients)
+        high, low = halves(coefficients * scale)
         out_ref[:, columns] = jnp.dot(
             left,
             jnp.concatenate([high, high, low], axis=0),
@@ -240,27 +296,49 @@
         in_specs=[pl.BlockSpec(memory_space=pltpu.SMEM)]
         + [pl.BlockSpec(memory_space=pltpu.VMEM)] * 6,
         out_specs=pl.BlockSpec(memory_space=pltpu.VMEM),
-        out_shape=jax.ShapeDtypeStruct(samples.shape, jnp.float32),
+        out_shape=jax.ShapeDtypeStruct((channels, samples.shape[1] + 128), jnp.float32),
         scratch_shapes=[pltpu.VMEM((channels, channels), jnp.float32)],
         compiler_params=pltpu.CompilerParams(vmem_limit_bytes=VMEM_LIMIT),
         name="denoised_band",
     )(place, *quarters, start, samples)
+
+
+def restore_kernel(message_ref, out_ref):
+    shares, _, width = message_ref.shape
+    part = width - 128
+    for i in range(shares):
+        unit = off_lanes(message_ref[i, 0:1, part:])
+        out_ref[0, :, i * part : (i + 1) * part] = message_ref[i, :, :part] * unit
+
+
+def restored(message, bands):
+    sources, own, width = message.shape
+    shares = sources // bands
+    total = shares * (width - 128)
+    return pl.pallas_call(
+        restore_kernel,
+        grid=(bands,),
+        in_specs=[pl.BlockSpec((shares, own, width), lambda b: (b, 0, 0))],
+        out_specs=pl.BlockSpec((1, own, total), lambda b: (b, 0, 0)),
+        out_shape=jax.ShapeDtypeStruct((bands, own, total), jnp.float32),
+        compiler_params=pltpu.CompilerParams(vmem_limit_bytes=VMEM_LIMIT),
+        name="restored",
+    )(message)
 
 
 def shards(raw_strain, fir_taps, start_basis):
     own, samples = raw_strain.shape
     bands = fir_taps.shape[0]
     chan_count, tm_count = lax.axis_size("chan"), lax.axis_size("tm")
-    channels = own * chan_count
     place, core = lax.axis_index("chan"), lax.axis_index("tm") % 2
     half = place % 2
     rim_piece = raw_strain[:, samples - RIM :]
     before = lax.ppermute(rim_piece, "tm", [(i, i + 1) for i in range(tm_count - 1)])
     table = filter_table(fir_taps)
 
-    decimated = filtered(raw_strain, before, table, chan_count)
-    decimated = lax.all_to_all(decimated, "chan", 0, 0, tiled=True).reshape(channels, -1)
-    kept, sent = band_gram(core, decimated)
+    message = filtered(raw_strain, before, table, chan_count).astype(SENT)
+    message = lax.all_to_all(message, "chan", 0, 0, tiled=True).astype(jnp.float32)
+    kept, sent, decimated = band_gram(core, message)
 
     pair = (kept + swapped(sent, "tm", 1)).reshape(2, 80, 128)
     sent = swapped(lax.dynamic_index_in_dim(pair, 1 - half, 0, False), "chan", 1)
@@ -280,9 +358,9 @@
     start = lax.dynamic_index_in_dim(start_basis, place // 2, 0, False)
     result = denoised_band(jnp.stack([core, half]), four, start, decimated)
 
-    result = lax.all_to_all(result.reshape(chan_count, own, -1), "chan", 0, 0, tiled=True)
-    result = jnp.transpose(result.reshape(bands, chan_count // bands, own, -1), (0, 2, 1, 3))
-    return result.reshape(bands, own, samples // 4)
+    result = result.reshape(chan_count, own, -1).astype(RESULT_SENT)
+    result = lax.all_to_all(result, "chan", 0, 0, tiled=True)
+    return restored(result.astype(jnp.float32), bands)
 
 
 def solution(mesh):

time: 125 us -> 109 us (0.87); the launches traced: 123 us -> 108 us
  waiting for transfers between devices: 41.3 us -> 29.4 us
  local copies, waits for them, and re-layouts: 10.9 us -> 2.57 us
  Pallas kernels: 10.3 us -> 14.1 us
  other arithmetic: 0.11 us -> 1.37 us
    all_to_all x1, waiting for transfers between devices: 29.7 us -> 17.9 us  [shards(): lax.all_to_all(message, 'chan', 0, 0, tiled=True).astype(jnp.float32)]
    reshape x2 -> x0, local copies, waits for them, and re-layouts: 6.98 us -> none  [the longest x1 4.01 us: shards(): return result.reshape(bands, own, samples // 4)]
    ppermute x8, starting transfers between devices: 11.8 us -> 15.7 us  [swapped(): return lax.ppermute(block, axis, route)]
    pallas_call x0 -> x1, Pallas kernels: none -> 3.55 us  [restored(): pl.pallas_call(restore_kernel, grid=(bands,), in_specs=[pl.BlockSpec((sha...]
    ppermute x1, starting transfers between devices: 4.31 us -> 1.43 us  [shards(): lax.ppermute(quarter, ('chan', 'tm'), across)]
    unnamed x6 -> x4, local copies, waits for them, and re-layouts: 2.35 us -> 1.04 us
    convert_element_type x0 -> x2, other arithmetic: none -> 1.25 us  [the longest x1 1.11 us: shards(): message = filtered(raw_strain, before, table, chan_count).astype(SENT)]
  transfers between devices with their start and end apart: 11 -> 11, of which waited for: 7 -> 8; matrix products, arithmetic and copies ran while one was open for 1% -> 1% of each run, Pallas kernels for 0% -> 0%
where the time goes in v7:
time: 109 us; the launch traced here: 108 us
  blocking collectives  31.9 us (29%)
  waiting for transfers between devices  29.4 us (27%)
  starting transfers between devices  28.9 us (27%)
  Pallas kernels  14.1 us (13%)
  local copies, waits for them, and re-layouts  2.57 us (2%)
  other arithmetic  1.37 us (1%)
    all_to_all x1, blocking collectives, shards(): result = lax.all_to_all(result, 'chan', 0, 0, tiled=True)  31.9 us
    all_to_all x1, waiting for transfers between devices, shards(): lax.all_to_all(message, 'chan', 0, 0, tiled=True).astype(jnp.float32)  17.9 us
    ppermute x8, starting transfers between devices, swapped(): return lax.ppermute(block, axis, route)  15.7 us
    ppermute x8, waiting for transfers between devices, swapped(): return lax.ppermute(block, axis, route)  10.2 us
    pallas_call x1, Pallas kernels, denoised_band(): pl.pallas_call(refine_kernel, in_specs=[pl.BlockSpec(memory_space=pltpu.S...  7.94 us
    all_to_all x1, starting transfers between devices, shards(): lax.all_to_all(message, 'chan', 0, 0, tiled=True).astype(jnp.float32)  6.75 us
    ppermute x1, starting transfers between devices, shards(): lax.ppermute(rim_piece, 'tm', [(i, i + 1) for i in range(tm_count - 1)])  4.92 us
    pallas_call x1, Pallas kernels, restored(): pl.pallas_call(restore_kernel, grid=(bands,), in_specs=[pl.BlockSpec((sha...  3.55 us
  transfers between devices with their start and end apart: 11, of which 8 were waited for; matrix products, arithmetic and copies ran while one was open for 1% of the time, Pallas kernels for 0%

profile of v7, /device:TPU:1, one launch (start us, length us, event | category | flops | bytes accessed | tf_op | source)
XLA Modules:
  0.0 108.4 jit_solution(11080819690435770293)
XLA Ops:
  0.0 0.0 copy-start
  0.0 0.7 slice.3
  0.7 4.9 %collective-permute-start = (bf16[16,128]{1,0:T(8,128)(2,1)S(1)}, bf16[16,128]{1,0:T(8,128)(2,1)S(1)}, u32[]{:S(2)}, u32[]{:S(2)}) collective-permute-start(bf16[16,128]{1,0:T(8,128)(2,1)S(1)} %slice.3), channel_id=1, source_target_pairs={{0,1},{1,2},{2,3},{3,4},{4,5},{5,6},{6,7},{7,8},{8,9},{9,10},{10,1... | collective-permute-start | bytes 12296 | tf_op jit(solution)/shard_map/ppermute | solution.py:336
  5.7 0.7 copy.5.taps_ref
  6.4 0.2 filter_table.1.table_ref
  6.5 0.0 collective-permute-done.before_ref
  6.6 0.0 copy-start.1
  6.6 1.0 copy-done.1
  7.6 1.1 filtered.1
  8.7 1.1 %convert_element_type.6 = f16[16,16,2176]{2,1,0:T(8,128)(2,1)} convert(f32[16,16,2176]{2,1,0:T(8,128)S(1)} %filtered.1) | non-fusion elementwise | flops 557056 | bytes 3342336 | tf_op jit(solution)/shard_map/convert_element_type | solution.py:339
  9.8 6.8 %all-to-all-start = ((f16[16,16,2176]{2,1,0:T(8,128)(2,1)}), f16[16,16,2176]{2,1,0:T(8,128)(2,1)S(1)}, u32[]{:S(2)}, u32[]{:S(2)}) async-start(f16[16,16,2176]{2,1,0:T(8,128)(2,1)} %convert_element_type.6), calls=%async_computation | async-start | bytes 2228224 | tf_op jit(solution)/shard_map/all_to_all | solution.py:340
  16.6 17.9 %all-to-all-done = f16[16,16,2176]{2,1,0:T(8,128)(2,1)S(1)} async-done(((f16[16,16,2176]{2,1,0:T(8,128)(2,1)}), f16[16,16,2176]{2,1,0:T(8,128)(2,1)S(1)}, u32[]{:S(2)}, u32[]{:S(2)}) %all-to-all-start) | async-done | bytes 1114144 | tf_op jit(solution)/shard_map/all_to_all | solution.py:340
  34.4 0.1 convert_element_type.7.message_ref
  34.6 1.4 %band_gram.1 = (f32[160,128]{1,0:T(8,128)S(1)}, f32[160,128]{1,0:T(8,128)S(1)}, f32[256,2048]{1,0:T(8,128)S(1)}) custom-call(s32[1]{0:T(128)} %bitcast.core_ref, f32[16,16,2176]{2,1,0:T(8,128)S(1)} %convert_element_type.7.message_ref), custom_call_target="tpu_custom_call" | custom-call | tf_op jit(solution)/shard_map/band_gram/pallas_call | solution.py:151
  36.0 0.1 collective-permute-start.1
  36.1 1.2 %collective-permute-done.1 = f32[160,128]{1,0:T(8,128)S(1)} collective-permute-done((f32[160,128]{1,0:T(8,128)S(1)}, f32[160,128]{1,0:T(8,128)S(1)}, u32[]{:S(2)}, u32[]{:S(2)}) %collective-permute-start.1) | collective-permute-done | bytes 81952 | tf_op jit(solution)/shard_map/ppermute | solution.py:21
  37.4 0.4 collective-permute-start.2
  37.8 2.6 %collective-permute-done.2 = f32[80,128]{1,0:T(8,128)S(1)} collective-permute-done((f32[80,128]{1,0:T(8,128)S(1)}, f32[80,128]{1,0:T(8,128)S(1)}, u32[]{:S(2)}, u32[]{:S(2)}) %collective-permute-start.2) | collective-permute-done | bytes 40992 | tf_op jit(solution)/shard_map/ppermute | solution.py:21
  40.3 3.0 %collective-permute-start.3 = (f32[80,128]{1,0:T(8,128)S(1)}, f32[80,128]{1,0:T(8,128)S(1)}, u32[]{:S(2)}, u32[]{:S(2)}) collective-permute-start(f32[80,128]{1,0:T(8,128)S(1)} %bitcast_add_fusion), channel_id=1, source_target_pairs={{0,2},{1,3},{2,0},{3,1},{4,6},{5,7},{6,4},{7,5},{8,10},{9,11},{10,... | collective-permute-start | bytes 122888 | tf_op jit(solution)/shard_map/ppermute | solution.py:21
  43.3 1.4 %collective-permute-done.3 = f32[80,128]{1,0:T(8,128)S(1)} collective-permute-done((f32[80,128]{1,0:T(8,128)S(1)}, f32[80,128]{1,0:T(8,128)S(1)}, u32[]{:S(2)}, u32[]{:S(2)}) %collective-permute-start.3) | collective-permute-done | bytes 40992 | tf_op jit(solution)/shard_map/ppermute | solution.py:21
  44.7 4.6 %collective-permute-start.4 = (f32[80,128]{1,0:T(8,128)S(1)}, f32[80,128]{1,0:T(8,128)S(1)}, u32[]{:S(2)}, u32[]{:S(2)}) collective-permute-start(f32[80,128]{1,0:T(8,128)S(1)} %add.44), channel_id=1, source_target_pairs={{0,4},{1,5},{2,6},{3,7},{4,0},{5,1},{6,2},{7,3},{8,12},{9,13},{10,... | collective-permute-start | bytes 122888 | tf_op jit(solution)/shard_map/ppermute | solution.py:21
  49.3 2.0 %collective-permute-start.5 = (f32[80,128]{1,0:T(8,128)S(1)}, f32[80,128]{1,0:T(8,128)S(1)}, u32[]{:S(2)}, u32[]{:S(2)}) collective-permute-start(f32[80,128]{1,0:T(8,128)S(1)} %add.44), channel_id=1, source_target_pairs={{0,8},{1,9},{2,10},{3,11},{4,12},{5,13},{6,14},{7,15},{8,0},{9,1},... | collective-permute-start | bytes 122888 | tf_op jit(solution)/shard_map/ppermute | solution.py:21
  51.3 1.4 %collective-permute-start.6 = (f32[80,128]{1,0:T(8,128)S(1)}, f32[80,128]{1,0:T(8,128)S(1)}, u32[]{:S(2)}, u32[]{:S(2)}) collective-permute-start(f32[80,128]{1,0:T(8,128)S(1)} %add.44), channel_id=1, source_target_pairs={{0,12},{1,13},{2,14},{3,15},{4,8},{5,9},{6,10},{7,11},{8,4},{9,5},... | collective-permute-start | bytes 122888 | tf_op jit(solution)/shard_map/ppermute | solution.py:21
  52.7 0.0 copy-done
  52.7 0.0 collective-permute-done.4
  52.7 3.6 %collective-permute-done.5 = f32[80,128]{1,0:T(8,128)S(1)} collective-permute-done((f32[80,128]{1,0:T(8,128)S(1)}, f32[80,128]{1,0:T(8,128)S(1)}, u32[]{:S(2)}, u32[]{:S(2)}) %collective-permute-start.5) | collective-permute-done | bytes 40992 | tf_op jit(solution)/shard_map/ppermute | solution.py:21
  56.3 0.4 collective-permute-done.6
  56.8 4.0 %collective-permute-start.7 = (f32[80,128]{1,0:T(8,128)S(1)}, f32[80,128]{1,0:T(8,128)S(1)}, u32[]{:S(2)}, u32[]{:S(2)}) collective-permute-start(f32[80,128]{1,0:T(8,128)S(1)} %add_add_fusion.mine_ref), channel_id=1, source_target_pairs={{0,1},{1,0},{2,3},{3,2},{4,5},{5,4},{6,7},{7,6},{8,9},{9,8},{10,11... | collective-permute-start | bytes 122888 | tf_op jit(solution)/shard_map/ppermute | solution.py:21
  60.7 0.3 collective-permute-start.8
  61.0 1.4 %collective-permute-start.9 = (f32[80,128]{1,0:T(8,128)S(1)}, f32[80,128]{1,0:T(8,128)S(1)}, u32[]{:S(2)}, u32[]{:S(2)}) collective-permute-start(f32[80,128]{1,0:T(8,128)S(1)} %add_add_fusion.mine_ref), channel_id=1, source_target_pairs={{0,17},{1,16},{2,19},{3,18},{4,21},{5,20},{6,23},{7,22},{8,25},{9,... | collective-permute-start | bytes 122888 | tf_op jit(solution)/shard_map/ppermute | solution.py:356
  62.5 0.1 pad_add_fusion.place_ref
  62.5 0.1 copy.6
  62.6 0.0 collective-permute-done.7.core_ref
  62.6 1.0 collective-permute-done.8.chan_ref
  63.6 1.4 %collective-permute-done.9.both_ref = f32[80,128]{1,0:T(8,128)S(1)} collective-permute-done((f32[80,128]{1,0:T(8,128)S(1)}, f32[80,128]{1,0:T(8,128)S(1)}, u32[]{:S(2)}, u32[]{:S(2)}) %collective-permute-start.9) | collective-permute-done | bytes 40992 | tf_op jit(solution)/shard_map/ppermute | solution.py:356
  65.0 7.9 %denoised_band.1 = f32[256,2176]{1,0:T(8,128)S(1)} custom-call(s32[2]{0:T(128)S(1)} %pad_add_fusion.place_ref, f32[80,128]{1,0:T(8,128)S(1)} %add_add_fusion.mine_ref, f32[80,128]{1,0:T(8,128)S(1)} %collective-permute-done.7.core_ref, f32[80,128]{1,0:T(8,128)S(1)} %collective-permute-done.8.chan_ref, f32[80,128]{1,0:T(8,128)S(1)} %collective-permute-done.9.both_ref, ...), custom_call_target="tpu_custom_call" | custom-call | tf_op jit(solution)/shard_map/denoised_band/pallas_call | solution.py:294
  73.0 31.9 %all_to_all.10.message_ref = f32[16,16,2176]{2,1,0:T(8,128)S(1)} all-to-all(f32[16,16,2176]{2,1,0:T(8,128)S(1)} %bitcast.10), channel_id=1, replica_groups=mesh['chan'=16,'tm'=16] {'chan'}, dimensions={0} | all-to-all | bytes 4456448 | tf_op jit(solution)/shard_map/all_to_all | solution.py:362
  104.8 3.5 %restored.1 = f32[8,16,4096]{2,1,0:T(8,128)} custom-call(f32[16,16,2176]{2,1,0:T(8,128)S(1)} %all_to_all.10.message_ref), custom_call_target="tpu_custom_call" | custom-call | tf_op jit(solution)/shard_map/restored/pallas_call | solution.py:318
  (6 shorter events, 0.1 us)
Async XLA Ops:
  0.0 52.7 %copy-start = (f32[8,256,32]{1,2,0:T(8,128)S(1)}, f32[8,256,32]{1,2,0:T(8,128)}, u32[]{:S(2)}) copy-start(f32[8,256,32]{1,2,0:T(8,128)} %param.5) | copy-start | bytes 786436
  0.7 5.8 %collective-permute-start = (bf16[16,128]{1,0:T(8,128)(2,1)S(1)}, bf16[16,128]{1,0:T(8,128)(2,1)S(1)}, u32[]{:S(2)}, u32[]{:S(2)}) collective-permute-start(bf16[16,128]{1,0:T(8,128)(2,1)S(1)} %slice.3), channel_id=1, source_target_pairs={{0,1},{1,2},{2,3},{3,4},{4,5},{5,6},{6,7},{7,8},{8,9},{9,10},{10,1... | collective-permute-start | bytes 12296 | tf_op jit(solution)/shard_map/ppermute | solution.py:336
  6.6 1.0 copy-start.1
  9.8 24.6 %all-to-all-start = ((f16[16,16,2176]{2,1,0:T(8,128)(2,1)}), f16[16,16,2176]{2,1,0:T(8,128)(2,1)S(1)}, u32[]{:S(2)}, u32[]{:S(2)}) async-start(f16[16,16,2176]{2,1,0:T(8,128)(2,1)} %convert_element_type.6), calls=%async_computation | async-start | bytes 2228224 | tf_op jit(solution)/shard_map/all_to_all | solution.py:340
  36.0 1.4 %collective-permute-start.1 = (f32[160,128]{1,0:T(8,128)S(1)}, f32[160,128]{1,0:T(8,128)S(1)}, u32[]{:S(2)}, u32[]{:S(2)}) collective-permute-start(f32[160,128]{1,0:T(8,128)S(1)} %get-tuple-element.9), channel_id=1, source_target_pairs={{0,1},{1,0},{2,3},{3,2},{4,5},{5,4},{6,7},{7,6},{8,9},{9,8},{10,11... | collective-permute-start | bytes 245768 | tf_op jit(solution)/shard_map/ppermute | solution.py:21
  37.4 2.9 %collective-permute-start.2 = (f32[80,128]{1,0:T(8,128)S(1)}, f32[80,128]{1,0:T(8,128)S(1)}, u32[]{:S(2)}, u32[]{:S(2)}) collective-permute-start(f32[80,128]{1,0:T(8,128)S(1)} %dynamic-slice_bitcast_fusion), channel_id=1, source_target_pairs={{0,16},{16,0},{32,48},{48,32},{64,80},{80,64},{96,112},{112,96},{1... | collective-permute-start | bytes 122888 | tf_op jit(solution)/shard_map/ppermute | solution.py:21
  40.3 4.4 %collective-permute-start.3 = (f32[80,128]{1,0:T(8,128)S(1)}, f32[80,128]{1,0:T(8,128)S(1)}, u32[]{:S(2)}, u32[]{:S(2)}) collective-permute-start(f32[80,128]{1,0:T(8,128)S(1)} %bitcast_add_fusion), channel_id=1, source_target_pairs={{0,2},{1,3},{2,0},{3,1},{4,6},{5,7},{6,4},{7,5},{8,10},{9,11},{10,... | collective-permute-start | bytes 122888 | tf_op jit(solution)/shard_map/ppermute | solution.py:21
  44.7 8.0 %collective-permute-start.4 = (f32[80,128]{1,0:T(8,128)S(1)}, f32[80,128]{1,0:T(8,128)S(1)}, u32[]{:S(2)}, u32[]{:S(2)}) collective-permute-start(f32[80,128]{1,0:T(8,128)S(1)} %add.44), channel_id=1, source_target_pairs={{0,4},{1,5},{2,6},{3,7},{4,0},{5,1},{6,2},{7,3},{8,12},{9,13},{10,... | collective-permute-start | bytes 122888 | tf_op jit(solution)/shard_map/ppermute | solution.py:21
  49.3 7.0 %collective-permute-start.5 = (f32[80,128]{1,0:T(8,128)S(1)}, f32[80,128]{1,0:T(8,128)S(1)}, u32[]{:S(2)}, u32[]{:S(2)}) collective-permute-start(f32[80,128]{1,0:T(8,128)S(1)} %add.44), channel_id=1, source_target_pairs={{0,8},{1,9},{2,10},{3,11},{4,12},{5,13},{6,14},{7,15},{8,0},{9,1},... | collective-permute-start | bytes 122888 | tf_op jit(solution)/shard_map/ppermute | solution.py:21
  51.3 5.4 %collective-permute-start.6 = (f32[80,128]{1,0:T(8,128)S(1)}, f32[80,128]{1,0:T(8,128)S(1)}, u32[]{:S(2)}, u32[]{:S(2)}) collective-permute-start(f32[80,128]{1,0:T(8,128)S(1)} %add.44), channel_id=1, source_target_pairs={{0,12},{1,13},{2,14},{3,15},{4,8},{5,9},{6,10},{7,11},{8,4},{9,5},... | collective-permute-start | bytes 122888 | tf_op jit(solution)/shard_map/ppermute | solution.py:21
  56.8 5.9 %collective-permute-start.7 = (f32[80,128]{1,0:T(8,128)S(1)}, f32[80,128]{1,0:T(8,128)S(1)}, u32[]{:S(2)}, u32[]{:S(2)}) collective-permute-start(f32[80,128]{1,0:T(8,128)S(1)} %add_add_fusion.mine_ref), channel_id=1, source_target_pairs={{0,1},{1,0},{2,3},{3,2},{4,5},{5,4},{6,7},{7,6},{8,9},{9,8},{10,11... | collective-permute-start | bytes 122888 | tf_op jit(solution)/shard_map/ppermute | solution.py:21
  60.7 2.9 %collective-permute-start.8 = (f32[80,128]{1,0:T(8,128)S(1)}, f32[80,128]{1,0:T(8,128)S(1)}, u32[]{:S(2)}, u32[]{:S(2)}) collective-permute-start(f32[80,128]{1,0:T(8,128)S(1)} %add_add_fusion.mine_ref), channel_id=1, source_target_pairs={{0,16},{16,0},{32,48},{48,32},{64,80},{80,64},{96,112},{112,96},{1... | collective-permute-start | bytes 122888 | tf_op jit(solution)/shard_map/ppermute | solution.py:21
  61.0 4.0 %collective-permute-start.9 = (f32[80,128]{1,0:T(8,128)S(1)}, f32[80,128]{1,0:T(8,128)S(1)}, u32[]{:S(2)}, u32[]{:S(2)}) collective-permute-start(f32[80,128]{1,0:T(8,128)S(1)} %add_add_fusion.mine_ref), channel_id=1, source_target_pairs={{0,17},{1,16},{2,19},{3,18},{4,21},{5,20},{6,23},{7,22},{8,25},{9,... | collective-permute-start | bytes 122888 | tf_op jit(solution)/shard_map/ppermute | solution.py:356

commit v8 on v7

--- a/solution.py
+++ b/solution.py
@@ -12,7 +12,6 @@
 HIGHEST = lax.Precision.HIGHEST
 VMEM_LIMIT = 24 * 1024 * 1024
 SENT = jnp.float16
-RESULT_SENT = jnp.float32
 POWERS = (14,) * 9 + (8, 4, 2, 1)
 
 
@@ -81,18 +80,19 @@
     return product([row[..., number : number + 1] for number in range(len(POWERS))])
 
 
+def squared(value):
+    return value * jnp.abs(value)
+
+
+def unsquared(value):
+    root = jnp.sqrt(jnp.abs(value))
+    return jnp.where(value < 0, -root, root)
+
+
 def filter_kernel(raw_ref, before_ref, table_ref, out_ref, extended_ref):
     own, samples = raw_ref.shape
     receivers, _, width = out_ref.shape
     part = width - 128
-    largest = jnp.max(jnp.abs(raw_ref[...].astype(jnp.float32)), keepdims=True)
-    before = jnp.max(jnp.abs(before_ref[...].astype(jnp.float32)), keepdims=True)
-    tap = jnp.max(jnp.abs(table_ref[...].astype(jnp.float32)), keepdims=True)
-    factors = powers_below(jnp.maximum(largest, before) * tap * 2.0**-7)
-    scale = 1.0 / product(factors)
-    marks = on_lanes(factors, (own, 128))
-    for i in range(receivers):
-        out_ref[i, :, part:] = marks
     extended_ref[:, :RIM] = before_ref[...]
     extended_ref[:, RIM:] = raw_ref[...]
     blocks = samples // STEP
@@ -101,15 +101,24 @@
     )
     bands = table_ref.shape[0] // 128
     share = part // 128
+    peaks = []
     for pair in range(bands // 2):
-        both = dot_nt(windows, table_ref[256 * pair : 256 * pair + 256, :]) * scale
+        both = dot_nt(windows, table_ref[256 * pair : 256 * pair + 256, :])
         for b in range(2):
+            largest = jnp.max(jnp.abs(both[:, 128 * b : 128 * b + 128]), axis=0, keepdims=True)
+            peaks.append(jnp.max(largest, axis=1, keepdims=True))
             for m in range(blocks):
                 place = (2 * pair + b) * (receivers // bands) + m // share
                 first = 128 * (m % share)
                 out_ref[place, :, first : first + 128] = both[
                     m * own : (m + 1) * own, 128 * b : 128 * b + 128
                 ]
+    factors = powers_below(jnp.concatenate(peaks, axis=0) * 2.0**-6)
+    scale = 1.0 / product(factors)
+    for i in range(receivers):
+        b = i // (receivers // bands)
+        out_ref[i, :, :part] = squared(out_ref[i, :, :part] * scale[b : b + 1, :])
+        out_ref[i, :, part:] = on_lanes([factor[b : b + 1, :] for factor in factors], (own, 128))
 
 
 def filtered(raw_strain, before, table, receivers):
@@ -131,7 +140,9 @@
     sources, own, width = message_ref.shape
     for i in range(sources):
         unit = off_lanes(message_ref[i, 0:1, width - 128 :])
-        samples_ref[i * own : (i + 1) * own, :] = message_ref[i, :, : width - 128] * unit
+        samples_ref[i * own : (i + 1) * own, :] = (
+            unsquared(message_ref[i, :, : width - 128]) * unit
+        )
     high, low = halves(samples_ref[...])
     gram = dot_nt(high, high) + dot_nt(high, low) + dot_nt(low, high)
     packed_ref[0:64, :] = gram[0:64, 0:128]
@@ -255,13 +266,8 @@
             preferred_element_type=jnp.float32,
         )
         basis = dot_nt(image, inverse_cholesky(compact), HIGHEST)
-    rows = lax.broadcasted_iota(jnp.int32, gram_ref.shape, 0)
-    columns = lax.broadcasted_iota(jnp.int32, gram_ref.shape, 1)
-    trace = jnp.sum(jnp.where(rows == columns, gram_ref[...], 0.0), keepdims=True)
-    factors = powers_below(jnp.sqrt(trace) * 2.0**-14)
-    scale = 1.0 / product(factors)
     part = samples_ref.shape[1]
-    out_ref[:, part:] = on_lanes(factors, (out_ref.shape[0], 128))
+    peak = jnp.zeros((1, STEP), jnp.float32)
     basis_high, basis_low = halves(basis)
     left = jnp.concatenate([basis_high, basis_low, basis_high], axis=1)
     rank = basis.shape[1]
@@ -281,12 +287,20 @@
             (((0,), (0,)), ((), ())),
             preferred_element_type=jnp.float32,
         )
-        high, low = halves(coefficients * scale)
-        out_ref[:, columns] = jnp.dot(
+        high, low = halves(coefficients)
+        result = jnp.dot(
             left,
             jnp.concatenate([high, high, low], axis=0),
             preferred_element_type=jnp.float32,
         )
+        out_ref[:, columns] = result
+        peak = jnp.maximum(peak, jnp.max(jnp.abs(result), axis=0, keepdims=True))
+    factors = powers_below(jnp.max(peak, axis=1, keepdims=True) * 2.0**-6)
+    scale = 1.0 / product(factors)
+    for first in range(0, part, STEP):
+        columns = slice(first, first + STEP)
+        out_ref[:, columns] = squared(out_ref[:, columns] * scale)
+    out_ref[:, part:] = on_lanes(factors, (out_ref.shape[0], 128))
 
 
 def denoised_band(place, quarters, start, samples):
@@ -308,7 +322,9 @@
     part = width - 128
     for i in range(shares):
         unit = off_lanes(message_ref[i, 0:1, part:])
-        out_ref[0, :, i * part : (i + 1) * part] = message_ref[i, :, :part] * unit
+        out_ref[0, :, i * part : (i + 1) * part] = (
+            unsquared(message_ref[i, :, :part]) * unit
+        )
 
 
 def restored(message, bands):
@@ -358,7 +374,7 @@
     start = lax.dynamic_index_in_dim(start_basis, place // 2, 0, False)
     result = denoised_band(jnp.stack([core, half]), four, start, decimated)
 
-    result = result.reshape(chan_count, own, -1).astype(RESULT_SENT)
+    result = result.reshape(chan_count, own, -1).astype(SENT)
     result = lax.all_to_all(result, "chan", 0, 0, tiled=True)
     return restored(result.astype(jnp.float32), bands)
 

time: 109 us -> 98.9 us (0.907)
  blocking collectives: 31.9 us -> 20.2 us
  Pallas kernels: 14.1 us -> 15.8 us
    all_to_all x1, blocking collectives: 31.9 us -> 20.2 us  [shards(): result = lax.all_to_all(result, 'chan', 0, 0, tiled=True)]
where the time goes in v8:
time: 98.9 us; the launch traced here: 98.6 us
  waiting for transfers between devices  29.4 us (30%)
  starting transfers between devices  28.8 us (29%)
  blocking collectives  20.2 us (20%)
  Pallas kernels  15.8 us (16%)
  local copies, waits for them, and re-layouts  2.57 us (3%)
  other arithmetic  1.63 us (2%)
    all_to_all x1, blocking collectives, shards(): result = lax.all_to_all(result, 'chan', 0, 0, tiled=True)  20.2 us
    all_to_all x1, waiting for transfers between devices, shards(): lax.all_to_all(message, 'chan', 0, 0, tiled=True).astype(jnp.float32)  17.9 us
    ppermute x8, starting transfers between devices, swapped(): return lax.ppermute(block, axis, route)  15.7 us
    ppermute x8, waiting for transfers between devices, swapped(): return lax.ppermute(block, axis, route)  10.2 us
    pallas_call x1, Pallas kernels, denoised_band(): pl.pallas_call(refine_kernel, in_specs=[pl.BlockSpec(memory_space=pltpu.S...  8.45 us
    all_to_all x1, starting transfers between devices, shards(): lax.all_to_all(message, 'chan', 0, 0, tiled=True).astype(jnp.float32)  6.75 us
    ppermute x1, starting transfers between devices, shards(): lax.ppermute(rim_piece, 'tm', [(i, i + 1) for i in range(tm_count - 1)])  4.92 us
    pallas_call x1, Pallas kernels, restored(): pl.pallas_call(restore_kernel, grid=(bands,), in_specs=[pl.BlockSpec((sha...  3.69 us
  transfers between devices with their start and end apart: 11, of which 8 were waited for; matrix products, arithmetic and copies ran while one was open for 1% of the time, Pallas kernels for 0%

profile of v8, /device:TPU:1, one launch (start us, length us, event | category | flops | bytes accessed | tf_op | source)
XLA Modules:
  0.0 98.6 jit_solution(17544374797165635995)
XLA Ops:
  0.0 0.0 copy-start
  0.0 0.7 slice.3
  0.7 4.9 %collective-permute-start = (bf16[16,128]{1,0:T(8,128)(2,1)S(1)}, bf16[16,128]{1,0:T(8,128)(2,1)S(1)}, u32[]{:S(2)}, u32[]{:S(2)}) collective-permute-start(bf16[16,128]{1,0:T(8,128)(2,1)S(1)} %slice.3), channel_id=1, source_target_pairs={{0,1},{1,2},{2,3},{3,4},{4,5},{5,6},{6,7},{7,8},{8,9},{9,10},{10,1... | collective-permute-start | bytes 12296 | tf_op jit(solution)/shard_map/ppermute | solution.py:352
  5.7 0.7 copy.5.taps_ref
  6.4 0.2 filter_table.1.table_ref
  6.5 0.0 collective-permute-done.before_ref
  6.6 0.0 copy-start.1
  6.6 1.0 %copy-done.1 = bf16[16,16384]{1,0:T(8,128)(2,1)S(1)} copy-done((bf16[16,16384]{1,0:T(8,128)(2,1)S(1)}, bf16[16,16384]{1,0:T(8,128)(2,1)}, u32[]{:S(2)}) %copy-start.1) | copy-done | bytes 524312
  7.6 1.5 %filtered.1 = f32[16,16,2176]{2,1,0:T(8,128)S(1)} custom-call(bf16[16,16384]{1,0:T(8,128)(2,1)S(1)} %copy-done.1, bf16[16,128]{1,0:T(8,128)(2,1)S(1)} %collective-permute-done.before_ref, bf16[1024,640]{1,0:T(8,128)(2,1)S(1)} %filter_table.1.table_ref), custom_call_target="tpu_custom_call" | custom-call | tf_op jit(solution)/shard_map/filtered/pallas_call | solution.py:127
  9.1 1.1 %convert_element_type.15 = f16[16,16,2176]{2,1,0:T(8,128)(2,1)} convert(f32[16,16,2176]{2,1,0:T(8,128)S(1)} %filtered.1) | non-fusion elementwise | flops 557056 | bytes 3342336 | tf_op jit(solution)/shard_map/convert_element_type | solution.py:355
  10.2 6.8 %all-to-all-start = ((f16[16,16,2176]{2,1,0:T(8,128)(2,1)}), f16[16,16,2176]{2,1,0:T(8,128)(2,1)S(1)}, u32[]{:S(2)}, u32[]{:S(2)}) async-start(f16[16,16,2176]{2,1,0:T(8,128)(2,1)} %convert_element_type.15), calls=%async_computation | async-start | bytes 2228224 | tf_op jit(solution)/shard_map/all_to_all | solution.py:356
  17.0 17.9 %all-to-all-done = f16[16,16,2176]{2,1,0:T(8,128)(2,1)S(1)} async-done(((f16[16,16,2176]{2,1,0:T(8,128)(2,1)}), f16[16,16,2176]{2,1,0:T(8,128)(2,1)S(1)}, u32[]{:S(2)}, u32[]{:S(2)}) %all-to-all-start) | async-done | bytes 1114144 | tf_op jit(solution)/shard_map/all_to_all | solution.py:356
  34.9 0.1 convert_element_type.16.message_ref
  35.0 2.0 %band_gram.1 = (f32[160,128]{1,0:T(8,128)S(1)}, f32[160,128]{1,0:T(8,128)S(1)}, f32[256,2048]{1,0:T(8,128)S(1)}) custom-call(s32[1]{0:T(128)} %bitcast.core_ref, f32[16,16,2176]{2,1,0:T(8,128)S(1)} %convert_element_type.16.message_ref), custom_call_target="tpu_custom_call" | custom-call | tf_op jit(solution)/shard_map/band_gram/pallas_call | solution.py:162
  37.0 0.1 collective-permute-start.1
  37.1 1.2 %collective-permute-done.1 = f32[160,128]{1,0:T(8,128)S(1)} collective-permute-done((f32[160,128]{1,0:T(8,128)S(1)}, f32[160,128]{1,0:T(8,128)S(1)}, u32[]{:S(2)}, u32[]{:S(2)}) %collective-permute-start.1) | collective-permute-done | bytes 81952 | tf_op jit(solution)/shard_map/ppermute | solution.py:20
  38.4 0.4 collective-permute-start.2
  38.8 2.6 %collective-permute-done.2 = f32[80,128]{1,0:T(8,128)S(1)} collective-permute-done((f32[80,128]{1,0:T(8,128)S(1)}, f32[80,128]{1,0:T(8,128)S(1)}, u32[]{:S(2)}, u32[]{:S(2)}) %collective-permute-start.2) | collective-permute-done | bytes 40992 | tf_op jit(solution)/shard_map/ppermute | solution.py:20
  41.3 3.0 %collective-permute-start.3 = (f32[80,128]{1,0:T(8,128)S(1)}, f32[80,128]{1,0:T(8,128)S(1)}, u32[]{:S(2)}, u32[]{:S(2)}) collective-permute-start(f32[80,128]{1,0:T(8,128)S(1)} %bitcast_add_fusion), channel_id=1, source_target_pairs={{0,2},{1,3},{2,0},{3,1},{4,6},{5,7},{6,4},{7,5},{8,10},{9,11},{10,... | collective-permute-start | bytes 122888 | tf_op jit(solution)/shard_map/ppermute | solution.py:20
  44.3 1.4 %collective-permute-done.3 = f32[80,128]{1,0:T(8,128)S(1)} collective-permute-done((f32[80,128]{1,0:T(8,128)S(1)}, f32[80,128]{1,0:T(8,128)S(1)}, u32[]{:S(2)}, u32[]{:S(2)}) %collective-permute-start.3) | collective-permute-done | bytes 40992 | tf_op jit(solution)/shard_map/ppermute | solution.py:20
  45.7 4.6 %collective-permute-start.4 = (f32[80,128]{1,0:T(8,128)S(1)}, f32[80,128]{1,0:T(8,128)S(1)}, u32[]{:S(2)}, u32[]{:S(2)}) collective-permute-start(f32[80,128]{1,0:T(8,128)S(1)} %add.44), channel_id=1, source_target_pairs={{0,4},{1,5},{2,6},{3,7},{4,0},{5,1},{6,2},{7,3},{8,12},{9,13},{10,... | collective-permute-start | bytes 122888 | tf_op jit(solution)/shard_map/ppermute | solution.py:20
  50.3 2.0 %collective-permute-start.5 = (f32[80,128]{1,0:T(8,128)S(1)}, f32[80,128]{1,0:T(8,128)S(1)}, u32[]{:S(2)}, u32[]{:S(2)}) collective-permute-start(f32[80,128]{1,0:T(8,128)S(1)} %add.44), channel_id=1, source_target_pairs={{0,8},{1,9},{2,10},{3,11},{4,12},{5,13},{6,14},{7,15},{8,0},{9,1},... | collective-permute-start | bytes 122888 | tf_op jit(solution)/shard_map/ppermute | solution.py:20
  52.3 1.4 %collective-permute-start.6 = (f32[80,128]{1,0:T(8,128)S(1)}, f32[80,128]{1,0:T(8,128)S(1)}, u32[]{:S(2)}, u32[]{:S(2)}) collective-permute-start(f32[80,128]{1,0:T(8,128)S(1)} %add.44), channel_id=1, source_target_pairs={{0,12},{1,13},{2,14},{3,15},{4,8},{5,9},{6,10},{7,11},{8,4},{9,5},... | collective-permute-start | bytes 122888 | tf_op jit(solution)/shard_map/ppermute | solution.py:20
  53.7 0.0 copy-done
  53.7 0.0 collective-permute-done.4
  53.7 3.6 %collective-permute-done.5 = f32[80,128]{1,0:T(8,128)S(1)} collective-permute-done((f32[80,128]{1,0:T(8,128)S(1)}, f32[80,128]{1,0:T(8,128)S(1)}, u32[]{:S(2)}, u32[]{:S(2)}) %collective-permute-start.5) | collective-permute-done | bytes 40992 | tf_op jit(solution)/shard_map/ppermute | solution.py:20
  57.3 0.4 collective-permute-done.6
  57.8 4.0 %collective-permute-start.7 = (f32[80,128]{1,0:T(8,128)S(1)}, f32[80,128]{1,0:T(8,128)S(1)}, u32[]{:S(2)}, u32[]{:S(2)}) collective-permute-start(f32[80,128]{1,0:T(8,128)S(1)} %add_add_fusion.mine_ref), channel_id=1, source_target_pairs={{0,1},{1,0},{2,3},{3,2},{4,5},{5,4},{6,7},{7,6},{8,9},{9,8},{10,11... | collective-permute-start | bytes 122888 | tf_op jit(solution)/shard_map/ppermute | solution.py:20
  61.7 0.3 collective-permute-start.8
  62.0 1.4 %collective-permute-start.9 = (f32[80,128]{1,0:T(8,128)S(1)}, f32[80,128]{1,0:T(8,128)S(1)}, u32[]{:S(2)}, u32[]{:S(2)}) collective-permute-start(f32[80,128]{1,0:T(8,128)S(1)} %add_add_fusion.mine_ref), channel_id=1, source_target_pairs={{0,17},{1,16},{2,19},{3,18},{4,21},{5,20},{6,23},{7,22},{8,25},{9,... | collective-permute-start | bytes 122888 | tf_op jit(solution)/shard_map/ppermute | solution.py:372
  63.5 0.1 pad_add_fusion.place_ref
  63.5 0.1 copy.6
  63.6 0.0 collective-permute-done.7.core_ref
  63.6 1.0 collective-permute-done.8.chan_ref
  64.6 1.4 %collective-permute-done.9.both_ref = f32[80,128]{1,0:T(8,128)S(1)} collective-permute-done((f32[80,128]{1,0:T(8,128)S(1)}, f32[80,128]{1,0:T(8,128)S(1)}, u32[]{:S(2)}, u32[]{:S(2)}) %collective-permute-start.9) | collective-permute-done | bytes 40992 | tf_op jit(solution)/shard_map/ppermute | solution.py:372
  66.0 8.5 %denoised_band.1 = f32[256,2176]{1,0:T(8,128)S(1)} custom-call(s32[2]{0:T(128)S(1)} %pad_add_fusion.place_ref, f32[80,128]{1,0:T(8,128)S(1)} %add_add_fusion.mine_ref, f32[80,128]{1,0:T(8,128)S(1)} %collective-permute-done.7.core_ref, f32[80,128]{1,0:T(8,128)S(1)} %collective-permute-done.8.chan_ref, f32[80,128]{1,0:T(8,128)S(1)} %collective-permute-done.9.both_ref, ...), custom_call_target="tpu_custom_call" | custom-call | tf_op jit(solution)/shard_map/denoised_band/pallas_call | solution.py:308
  74.5 0.1 convert_element_type.17
  74.6 20.2 %all_to_all.10 = f16[16,16,2176]{2,1,0:T(8,128)(2,1)S(1)} all-to-all(f16[16,16,2176]{2,1,0:T(8,128)(2,1)S(1)} %bitcast.11), channel_id=1, replica_groups=mesh['chan'=16,'tm'=16] {'chan'}, dimensions={0} | all-to-all | bytes 2228224 | tf_op jit(solution)/shard_map/all_to_all | solution.py:378
  94.8 0.1 convert_element_type.19.message_ref
  94.9 3.7 %restored.1 = f32[8,16,4096]{2,1,0:T(8,128)} custom-call(f32[16,16,2176]{2,1,0:T(8,128)S(1)} %convert_element_type.19.message_ref), custom_call_target="tpu_custom_call" | custom-call | tf_op jit(solution)/shard_map/restored/pallas_call | solution.py:334
  (6 shorter events, 0.1 us)
Async XLA Ops:
  0.0 53.7 %copy-start = (f32[8,256,32]{1,2,0:T(8,128)S(1)}, f32[8,256,32]{1,2,0:T(8,128)}, u32[]{:S(2)}) copy-start(f32[8,256,32]{1,2,0:T(8,128)} %param.5) | copy-start | bytes 786436
  0.7 5.8 %collective-permute-start = (bf16[16,128]{1,0:T(8,128)(2,1)S(1)}, bf16[16,128]{1,0:T(8,128)(2,1)S(1)}, u32[]{:S(2)}, u32[]{:S(2)}) collective-permute-start(bf16[16,128]{1,0:T(8,128)(2,1)S(1)} %slice.3), channel_id=1, source_target_pairs={{0,1},{1,2},{2,3},{3,4},{4,5},{5,6},{6,7},{7,8},{8,9},{9,10},{10,1... | collective-permute-start | bytes 12296 | tf_op jit(solution)/shard_map/ppermute | solution.py:352
  6.6 1.0 %copy-start.1 = (bf16[16,16384]{1,0:T(8,128)(2,1)S(1)}, bf16[16,16384]{1,0:T(8,128)(2,1)}, u32[]{:S(2)}) copy-start(bf16[16,16384]{1,0:T(8,128)(2,1)} %raw_ref.1) | copy-start | bytes 1572868
  10.2 24.6 %all-to-all-start = ((f16[16,16,2176]{2,1,0:T(8,128)(2,1)}), f16[16,16,2176]{2,1,0:T(8,128)(2,1)S(1)}, u32[]{:S(2)}, u32[]{:S(2)}) async-start(f16[16,16,2176]{2,1,0:T(8,128)(2,1)} %convert_element_type.15), calls=%async_computation | async-start | bytes 2228224 | tf_op jit(solution)/shard_map/all_to_all | solution.py:356
  37.0 1.4 %collective-permute-start.1 = (f32[160,128]{1,0:T(8,128)S(1)}, f32[160,128]{1,0:T(8,128)S(1)}, u32[]{:S(2)}, u32[]{:S(2)}) collective-permute-start(f32[160,128]{1,0:T(8,128)S(1)} %get-tuple-element.9), channel_id=1, source_target_pairs={{0,1},{1,0},{2,3},{3,2},{4,5},{5,4},{6,7},{7,6},{8,9},{9,8},{10,11... | collective-permute-start | bytes 245768 | tf_op jit(solution)/shard_map/ppermute | solution.py:20
  38.4 2.9 %collective-permute-start.2 = (f32[80,128]{1,0:T(8,128)S(1)}, f32[80,128]{1,0:T(8,128)S(1)}, u32[]{:S(2)}, u32[]{:S(2)}) collective-permute-start(f32[80,128]{1,0:T(8,128)S(1)} %dynamic-slice_bitcast_fusion), channel_id=1, source_target_pairs={{0,16},{16,0},{32,48},{48,32},{64,80},{80,64},{96,112},{112,96},{1... | collective-permute-start | bytes 122888 | tf_op jit(solution)/shard_map/ppermute | solution.py:20
  41.3 4.4 %collective-permute-start.3 = (f32[80,128]{1,0:T(8,128)S(1)}, f32[80,128]{1,0:T(8,128)S(1)}, u32[]{:S(2)}, u32[]{:S(2)}) collective-permute-start(f32[80,128]{1,0:T(8,128)S(1)} %bitcast_add_fusion), channel_id=1, source_target_pairs={{0,2},{1,3},{2,0},{3,1},{4,6},{5,7},{6,4},{7,5},{8,10},{9,11},{10,... | collective-permute-start | bytes 122888 | tf_op jit(solution)/shard_map/ppermute | solution.py:20
  45.7 8.0 %collective-permute-start.4 = (f32[80,128]{1,0:T(8,128)S(1)}, f32[80,128]{1,0:T(8,128)S(1)}, u32[]{:S(2)}, u32[]{:S(2)}) collective-permute-start(f32[80,128]{1,0:T(8,128)S(1)} %add.44), channel_id=1, source_target_pairs={{0,4},{1,5},{2,6},{3,7},{4,0},{5,1},{6,2},{7,3},{8,12},{9,13},{10,... | collective-permute-start | bytes 122888 | tf_op jit(solution)/shard_map/ppermute | solution.py:20
  50.3 7.0 %collective-permute-start.5 = (f32[80,128]{1,0:T(8,128)S(1)}, f32[80,128]{1,0:T(8,128)S(1)}, u32[]{:S(2)}, u32[]{:S(2)}) collective-permute-start(f32[80,128]{1,0:T(8,128)S(1)} %add.44), channel_id=1, source_target_pairs={{0,8},{1,9},{2,10},{3,11},{4,12},{5,13},{6,14},{7,15},{8,0},{9,1},... | collective-permute-start | bytes 122888 | tf_op jit(solution)/shard_map/ppermute | solution.py:20
  52.3 5.4 %collective-permute-start.6 = (f32[80,128]{1,0:T(8,128)S(1)}, f32[80,128]{1,0:T(8,128)S(1)}, u32[]{:S(2)}, u32[]{:S(2)}) collective-permute-start(f32[80,128]{1,0:T(8,128)S(1)} %add.44), channel_id=1, source_target_pairs={{0,12},{1,13},{2,14},{3,15},{4,8},{5,9},{6,10},{7,11},{8,4},{9,5},... | collective-permute-start | bytes 122888 | tf_op jit(solution)/shard_map/ppermute | solution.py:20
  57.8 5.9 %collective-permute-start.7 = (f32[80,128]{1,0:T(8,128)S(1)}, f32[80,128]{1,0:T(8,128)S(1)}, u32[]{:S(2)}, u32[]{:S(2)}) collective-permute-start(f32[80,128]{1,0:T(8,128)S(1)} %add_add_fusion.mine_ref), channel_id=1, source_target_pairs={{0,1},{1,0},{2,3},{3,2},{4,5},{5,4},{6,7},{7,6},{8,9},{9,8},{10,11... | collective-permute-start | bytes 122888 | tf_op jit(solution)/shard_map/ppermute | solution.py:20
  61.7 2.9 %collective-permute-start.8 = (f32[80,128]{1,0:T(8,128)S(1)}, f32[80,128]{1,0:T(8,128)S(1)}, u32[]{:S(2)}, u32[]{:S(2)}) collective-permute-start(f32[80,128]{1,0:T(8,128)S(1)} %add_add_fusion.mine_ref), channel_id=1, source_target_pairs={{0,16},{16,0},{32,48},{48,32},{64,80},{80,64},{96,112},{112,96},{1... | collective-permute-start | bytes 122888 | tf_op jit(solution)/shard_map/ppermute | solution.py:20
  62.0 4.0 %collective-permute-start.9 = (f32[80,128]{1,0:T(8,128)S(1)}, f32[80,128]{1,0:T(8,128)S(1)}, u32[]{:S(2)}, u32[]{:S(2)}) collective-permute-start(f32[80,128]{1,0:T(8,128)S(1)} %add_add_fusion.mine_ref), channel_id=1, source_target_pairs={{0,17},{1,16},{2,19},{3,18},{4,21},{5,20},{6,23},{7,22},{8,25},{9,... | collective-permute-start | bytes 122888 | tf_op jit(solution)/shard_map/ppermute | solution.py:372

commit v9 on v8

--- a/solution.py
+++ b/solution.py
@@ -318,24 +318,24 @@
 
 
 def restore_kernel(message_ref, out_ref):
-    shares, _, width = message_ref.shape
+    bands, _, total = out_ref.shape
+    sources, _, width = message_ref.shape
     part = width - 128
-    for i in range(shares):
+    for i in range(sources):
         unit = off_lanes(message_ref[i, 0:1, part:])
-        out_ref[0, :, i * part : (i + 1) * part] = (
-            unsquared(message_ref[i, :, :part]) * unit
-        )
+        b, first = divmod(i * part, total)
+        out_ref[b, :, first : first + part] = unsquared(message_ref[i, :, :part]) * unit
 
 
 def restored(message, bands):
     sources, own, width = message.shape
-    shares = sources // bands
-    total = shares * (width - 128)
+    total = sources // bands * (width - 128)
+    steps = 2
     return pl.pallas_call(
         restore_kernel,
-        grid=(bands,),
-        in_specs=[pl.BlockSpec((shares, own, width), lambda b: (b, 0, 0))],
-        out_specs=pl.BlockSpec((1, own, total), lambda b: (b, 0, 0)),
+        grid=(steps,),
+        in_specs=[pl.BlockSpec((sources // steps, own, width), lambda b: (b, 0, 0))],
+        out_specs=pl.BlockSpec((bands // steps, own, total), lambda b: (b, 0, 0)),
         out_shape=jax.ShapeDtypeStruct((bands, own, total), jnp.float32),
         compiler_params=pltpu.CompilerParams(vmem_limit_bytes=VMEM_LIMIT),
         name="restored",
@@ -360,7 +360,7 @@
     sent = swapped(lax.dynamic_index_in_dim(pair, 1 - half, 0, False), "chan", 1)
     quarter = lax.dynamic_index_in_dim(pair, half, 0, False) + sent
     quarter = quarter + swapped(quarter, "tm", 2)
-    others = [swapped(quarter, "tm", distance) for distance in (4, 8, 12)]
+    others = [swapped(quarter, "tm", distance) for distance in (8, 4, 12)]
     quarter = (quarter + others[0]) + (others[1] + others[2])
 
     everyone = range(chan_count * tm_count)

time: 98.9 us -> 97.6 us (0.987)
  Pallas kernels: 15.8 us -> 14.1 us
    pallas_call x1, Pallas kernels: 3.69 us -> 2.03 us  [restored(): pl.pallas_call(restore_kernel, grid=(steps,), in_specs=[pl.BlockSpec((sou...]
where the time goes in v9:
time: 97.6 us; the launch traced here: 97.3 us
  waiting for transfers between devices  29.5 us (30%)
  starting transfers between devices  29 us (30%)
  blocking collectives  20.3 us (21%)
  Pallas kernels  14.1 us (14%)
  local copies, waits for them, and re-layouts  2.57 us (3%)
  other arithmetic  1.63 us (2%)
    all_to_all x1, blocking collectives, shards(): result = lax.all_to_all(result, 'chan', 0, 0, tiled=True)  20.3 us
    all_to_all x1, waiting for transfers between devices, shards(): lax.all_to_all(message, 'chan', 0, 0, tiled=True).astype(jnp.float32)  17.9 us
    ppermute x8, starting transfers between devices, swapped(): return lax.ppermute(block, axis, route)  15.8 us
    ppermute x8, waiting for transfers between devices, swapped(): return lax.ppermute(block, axis, route)  10.3 us
    pallas_call x1, Pallas kernels, denoised_band(): pl.pallas_call(refine_kernel, in_specs=[pl.BlockSpec(memory_space=pltpu.S...  8.45 us
    all_to_all x1, starting transfers between devices, shards(): lax.all_to_all(message, 'chan', 0, 0, tiled=True).astype(jnp.float32)  6.75 us
    ppermute x1, starting transfers between devices, shards(): lax.ppermute(rim_piece, 'tm', [(i, i + 1) for i in range(tm_count - 1)])  4.92 us
    pallas_call x1, Pallas kernels, restored(): pl.pallas_call(restore_kernel, grid=(steps,), in_specs=[pl.BlockSpec((sou...  2.03 us
  transfers between devices with their start and end apart: 11, of which 8 were waited for; matrix products, arithmetic and copies ran while one was open for 1% of the time, Pallas kernels for 0%

profile of v9, /device:TPU:1, one launch (start us, length us, event | category | flops | bytes accessed | tf_op | source)
XLA Modules:
  0.0 97.3 jit_solution(17314629413640959404)
XLA Ops:
  0.0 0.0 copy-start
  0.0 0.7 slice.3
  0.7 4.9 %collective-permute-start = (bf16[16,128]{1,0:T(8,128)(2,1)S(1)}, bf16[16,128]{1,0:T(8,128)(2,1)S(1)}, u32[]{:S(2)}, u32[]{:S(2)}) collective-permute-start(bf16[16,128]{1,0:T(8,128)(2,1)S(1)} %slice.3), channel_id=1, source_target_pairs={{0,1},{1,2},{2,3},{3,4},{4,5},{5,6},{6,7},{7,8},{8,9},{9,10},{10,1... | collective-permute-start | bytes 12296 | tf_op jit(solution)/shard_map/ppermute | solution.py:352
  5.7 0.7 copy.5.taps_ref
  6.4 0.2 filter_table.1.table_ref
  6.5 0.0 collective-permute-done.before_ref
  6.6 0.0 copy-start.1
  6.6 1.0 %copy-done.1 = bf16[16,16384]{1,0:T(8,128)(2,1)S(1)} copy-done((bf16[16,16384]{1,0:T(8,128)(2,1)S(1)}, bf16[16,16384]{1,0:T(8,128)(2,1)}, u32[]{:S(2)}) %copy-start.1) | copy-done | bytes 524312
  7.6 1.5 %filtered.1 = f32[16,16,2176]{2,1,0:T(8,128)S(1)} custom-call(bf16[16,16384]{1,0:T(8,128)(2,1)S(1)} %copy-done.1, bf16[16,128]{1,0:T(8,128)(2,1)S(1)} %collective-permute-done.before_ref, bf16[1024,640]{1,0:T(8,128)(2,1)S(1)} %filter_table.1.table_ref), custom_call_target="tpu_custom_call" | custom-call | tf_op jit(solution)/shard_map/filtered/pallas_call | solution.py:127
  9.1 1.1 %convert_element_type.15 = f16[16,16,2176]{2,1,0:T(8,128)(2,1)} convert(f32[16,16,2176]{2,1,0:T(8,128)S(1)} %filtered.1) | non-fusion elementwise | flops 557056 | bytes 3342336 | tf_op jit(solution)/shard_map/convert_element_type | solution.py:355
  10.2 6.8 %all-to-all-start = ((f16[16,16,2176]{2,1,0:T(8,128)(2,1)}), f16[16,16,2176]{2,1,0:T(8,128)(2,1)S(1)}, u32[]{:S(2)}, u32[]{:S(2)}) async-start(f16[16,16,2176]{2,1,0:T(8,128)(2,1)} %convert_element_type.15), calls=%async_computation | async-start | bytes 2228224 | tf_op jit(solution)/shard_map/all_to_all | solution.py:356
  17.0 17.9 %all-to-all-done = f16[16,16,2176]{2,1,0:T(8,128)(2,1)S(1)} async-done(((f16[16,16,2176]{2,1,0:T(8,128)(2,1)}), f16[16,16,2176]{2,1,0:T(8,128)(2,1)S(1)}, u32[]{:S(2)}, u32[]{:S(2)}) %all-to-all-start) | async-done | bytes 1114144 | tf_op jit(solution)/shard_map/all_to_all | solution.py:356
  34.9 0.1 convert_element_type.16.message_ref
  35.0 2.0 %band_gram.1 = (f32[160,128]{1,0:T(8,128)S(1)}, f32[160,128]{1,0:T(8,128)S(1)}, f32[256,2048]{1,0:T(8,128)S(1)}) custom-call(s32[1]{0:T(128)} %bitcast.core_ref, f32[16,16,2176]{2,1,0:T(8,128)S(1)} %convert_element_type.16.message_ref), custom_call_target="tpu_custom_call" | custom-call | tf_op jit(solution)/shard_map/band_gram/pallas_call | solution.py:162
  37.0 0.1 collective-permute-start.1
  37.1 1.2 %collective-permute-done.1 = f32[160,128]{1,0:T(8,128)S(1)} collective-permute-done((f32[160,128]{1,0:T(8,128)S(1)}, f32[160,128]{1,0:T(8,128)S(1)}, u32[]{:S(2)}, u32[]{:S(2)}) %collective-permute-start.1) | collective-permute-done | bytes 81952 | tf_op jit(solution)/shard_map/ppermute | solution.py:20
  38.4 0.4 collective-permute-start.2
  38.8 2.6 %collective-permute-done.2 = f32[80,128]{1,0:T(8,128)S(1)} collective-permute-done((f32[80,128]{1,0:T(8,128)S(1)}, f32[80,128]{1,0:T(8,128)S(1)}, u32[]{:S(2)}, u32[]{:S(2)}) %collective-permute-start.2) | collective-permute-done | bytes 40992 | tf_op jit(solution)/shard_map/ppermute | solution.py:20
  41.3 3.0 %collective-permute-start.3 = (f32[80,128]{1,0:T(8,128)S(1)}, f32[80,128]{1,0:T(8,128)S(1)}, u32[]{:S(2)}, u32[]{:S(2)}) collective-permute-start(f32[80,128]{1,0:T(8,128)S(1)} %bitcast_add_fusion), channel_id=1, source_target_pairs={{0,2},{1,3},{2,0},{3,1},{4,6},{5,7},{6,4},{7,5},{8,10},{9,11},{10,... | collective-permute-start | bytes 122888 | tf_op jit(solution)/shard_map/ppermute | solution.py:20
  44.3 1.4 %collective-permute-done.3 = f32[80,128]{1,0:T(8,128)S(1)} collective-permute-done((f32[80,128]{1,0:T(8,128)S(1)}, f32[80,128]{1,0:T(8,128)S(1)}, u32[]{:S(2)}, u32[]{:S(2)}) %collective-permute-start.3) | collective-permute-done | bytes 40992 | tf_op jit(solution)/shard_map/ppermute | solution.py:20
  45.7 5.1 %collective-permute-start.4 = (f32[80,128]{1,0:T(8,128)S(1)}, f32[80,128]{1,0:T(8,128)S(1)}, u32[]{:S(2)}, u32[]{:S(2)}) collective-permute-start(f32[80,128]{1,0:T(8,128)S(1)} %add.44), channel_id=1, source_target_pairs={{0,8},{1,9},{2,10},{3,11},{4,12},{5,13},{6,14},{7,15},{8,0},{9,1},... | collective-permute-start | bytes 122888 | tf_op jit(solution)/shard_map/ppermute | solution.py:20
  50.8 1.5 %collective-permute-start.5 = (f32[80,128]{1,0:T(8,128)S(1)}, f32[80,128]{1,0:T(8,128)S(1)}, u32[]{:S(2)}, u32[]{:S(2)}) collective-permute-start(f32[80,128]{1,0:T(8,128)S(1)} %add.44), channel_id=1, source_target_pairs={{0,4},{1,5},{2,6},{3,7},{4,0},{5,1},{6,2},{7,3},{8,12},{9,13},{10,... | collective-permute-start | bytes 122888 | tf_op jit(solution)/shard_map/ppermute | solution.py:20
  52.3 1.3 %collective-permute-start.6 = (f32[80,128]{1,0:T(8,128)S(1)}, f32[80,128]{1,0:T(8,128)S(1)}, u32[]{:S(2)}, u32[]{:S(2)}) collective-permute-start(f32[80,128]{1,0:T(8,128)S(1)} %add.44), channel_id=1, source_target_pairs={{0,12},{1,13},{2,14},{3,15},{4,8},{5,9},{6,10},{7,11},{8,4},{9,5},... | collective-permute-start | bytes 122888 | tf_op jit(solution)/shard_map/ppermute | solution.py:20
  53.6 0.0 copy-done
  53.6 0.0 collective-permute-done.4
  53.6 1.2 %collective-permute-done.5 = f32[80,128]{1,0:T(8,128)S(1)} collective-permute-done((f32[80,128]{1,0:T(8,128)S(1)}, f32[80,128]{1,0:T(8,128)S(1)}, u32[]{:S(2)}, u32[]{:S(2)}) %collective-permute-start.5) | collective-permute-done | bytes 40992 | tf_op jit(solution)/shard_map/ppermute | solution.py:20
  54.9 2.9 %collective-permute-done.6 = f32[80,128]{1,0:T(8,128)S(1)} collective-permute-done((f32[80,128]{1,0:T(8,128)S(1)}, f32[80,128]{1,0:T(8,128)S(1)}, u32[]{:S(2)}, u32[]{:S(2)}) %collective-permute-start.6) | collective-permute-done | bytes 40992 | tf_op jit(solution)/shard_map/ppermute | solution.py:20
  57.8 4.2 %collective-permute-start.7 = (f32[80,128]{1,0:T(8,128)S(1)}, f32[80,128]{1,0:T(8,128)S(1)}, u32[]{:S(2)}, u32[]{:S(2)}) collective-permute-start(f32[80,128]{1,0:T(8,128)S(1)} %add_add_fusion.mine_ref), channel_id=1, source_target_pairs={{0,1},{1,0},{2,3},{3,2},{4,5},{5,4},{6,7},{7,6},{8,9},{9,8},{10,11... | collective-permute-start | bytes 122888 | tf_op jit(solution)/shard_map/ppermute | solution.py:20
  62.0 0.2 collective-permute-start.8
  62.2 1.5 %collective-permute-start.9 = (f32[80,128]{1,0:T(8,128)S(1)}, f32[80,128]{1,0:T(8,128)S(1)}, u32[]{:S(2)}, u32[]{:S(2)}) collective-permute-start(f32[80,128]{1,0:T(8,128)S(1)} %add_add_fusion.mine_ref), channel_id=1, source_target_pairs={{0,17},{1,16},{2,19},{3,18},{4,21},{5,20},{6,23},{7,22},{8,25},{9,... | collective-permute-start | bytes 122888 | tf_op jit(solution)/shard_map/ppermute | solution.py:372
  63.7 0.1 pad_add_fusion.place_ref
  63.8 0.1 copy.6
  63.9 0.0 collective-permute-done.7.core_ref
  63.9 1.0 collective-permute-done.8.chan_ref
  64.9 1.3 %collective-permute-done.9.both_ref = f32[80,128]{1,0:T(8,128)S(1)} collective-permute-done((f32[80,128]{1,0:T(8,128)S(1)}, f32[80,128]{1,0:T(8,128)S(1)}, u32[]{:S(2)}, u32[]{:S(2)}) %collective-permute-start.9) | collective-permute-done | bytes 40992 | tf_op jit(solution)/shard_map/ppermute | solution.py:372
  66.2 8.5 %denoised_band.1 = f32[256,2176]{1,0:T(8,128)S(1)} custom-call(s32[2]{0:T(128)S(1)} %pad_add_fusion.place_ref, f32[80,128]{1,0:T(8,128)S(1)} %add_add_fusion.mine_ref, f32[80,128]{1,0:T(8,128)S(1)} %collective-permute-done.7.core_ref, f32[80,128]{1,0:T(8,128)S(1)} %collective-permute-done.8.chan_ref, f32[80,128]{1,0:T(8,128)S(1)} %collective-permute-done.9.both_ref, ...), custom_call_target="tpu_custom_call" | custom-call | tf_op jit(solution)/shard_map/denoised_band/pallas_call | solution.py:308
  74.7 0.1 convert_element_type.17
  74.8 20.3 %all_to_all.10 = f16[16,16,2176]{2,1,0:T(8,128)(2,1)S(1)} all-to-all(f16[16,16,2176]{2,1,0:T(8,128)(2,1)S(1)} %bitcast.11), channel_id=1, replica_groups=mesh['chan'=16,'tm'=16] {'chan'}, dimensions={0} | all-to-all | bytes 2228224 | tf_op jit(solution)/shard_map/all_to_all | solution.py:378
  95.1 0.1 convert_element_type.19.message_ref
  95.3 2.0 %restored.1 = f32[8,16,4096]{2,1,0:T(8,128)} custom-call(f32[16,16,2176]{2,1,0:T(8,128)S(1)} %convert_element_type.19.message_ref), custom_call_target="tpu_custom_call" | custom-call | tf_op jit(solution)/shard_map/restored/pallas_call | solution.py:334
  (6 shorter events, 0.1 us)
Async XLA Ops:
  0.0 53.6 %copy-start = (f32[8,256,32]{1,2,0:T(8,128)S(1)}, f32[8,256,32]{1,2,0:T(8,128)}, u32[]{:S(2)}) copy-start(f32[8,256,32]{1,2,0:T(8,128)} %param.5) | copy-start | bytes 786436
  0.7 5.8 %collective-permute-start = (bf16[16,128]{1,0:T(8,128)(2,1)S(1)}, bf16[16,128]{1,0:T(8,128)(2,1)S(1)}, u32[]{:S(2)}, u32[]{:S(2)}) collective-permute-start(bf16[16,128]{1,0:T(8,128)(2,1)S(1)} %slice.3), channel_id=1, source_target_pairs={{0,1},{1,2},{2,3},{3,4},{4,5},{5,6},{6,7},{7,8},{8,9},{9,10},{10,1... | collective-permute-start | bytes 12296 | tf_op jit(solution)/shard_map/ppermute | solution.py:352
  6.6 1.0 %copy-start.1 = (bf16[16,16384]{1,0:T(8,128)(2,1)S(1)}, bf16[16,16384]{1,0:T(8,128)(2,1)}, u32[]{:S(2)}) copy-start(bf16[16,16384]{1,0:T(8,128)(2,1)} %raw_ref.1) | copy-start | bytes 1572868
  10.2 24.6 %all-to-all-start = ((f16[16,16,2176]{2,1,0:T(8,128)(2,1)}), f16[16,16,2176]{2,1,0:T(8,128)(2,1)S(1)}, u32[]{:S(2)}, u32[]{:S(2)}) async-start(f16[16,16,2176]{2,1,0:T(8,128)(2,1)} %convert_element_type.15), calls=%async_computation | async-start | bytes 2228224 | tf_op jit(solution)/shard_map/all_to_all | solution.py:356
  37.0 1.4 %collective-permute-start.1 = (f32[160,128]{1,0:T(8,128)S(1)}, f32[160,128]{1,0:T(8,128)S(1)}, u32[]{:S(2)}, u32[]{:S(2)}) collective-permute-start(f32[160,128]{1,0:T(8,128)S(1)} %get-tuple-element.9), channel_id=1, source_target_pairs={{0,1},{1,0},{2,3},{3,2},{4,5},{5,4},{6,7},{7,6},{8,9},{9,8},{10,11... | collective-permute-start | bytes 245768 | tf_op jit(solution)/shard_map/ppermute | solution.py:20
  38.4 2.9 %collective-permute-start.2 = (f32[80,128]{1,0:T(8,128)S(1)}, f32[80,128]{1,0:T(8,128)S(1)}, u32[]{:S(2)}, u32[]{:S(2)}) collective-permute-start(f32[80,128]{1,0:T(8,128)S(1)} %dynamic-slice_bitcast_fusion), channel_id=1, source_target_pairs={{0,16},{16,0},{32,48},{48,32},{64,80},{80,64},{96,112},{112,96},{1... | collective-permute-start | bytes 122888 | tf_op jit(solution)/shard_map/ppermute | solution.py:20
  41.3 4.4 %collective-permute-start.3 = (f32[80,128]{1,0:T(8,128)S(1)}, f32[80,128]{1,0:T(8,128)S(1)}, u32[]{:S(2)}, u32[]{:S(2)}) collective-permute-start(f32[80,128]{1,0:T(8,128)S(1)} %bitcast_add_fusion), channel_id=1, source_target_pairs={{0,2},{1,3},{2,0},{3,1},{4,6},{5,7},{6,4},{7,5},{8,10},{9,11},{10,... | collective-permute-start | bytes 122888 | tf_op jit(solution)/shard_map/ppermute | solution.py:20
  45.7 7.9 %collective-permute-start.4 = (f32[80,128]{1,0:T(8,128)S(1)}, f32[80,128]{1,0:T(8,128)S(1)}, u32[]{:S(2)}, u32[]{:S(2)}) collective-permute-start(f32[80,128]{1,0:T(8,128)S(1)} %add.44), channel_id=1, source_target_pairs={{0,8},{1,9},{2,10},{3,11},{4,12},{5,13},{6,14},{7,15},{8,0},{9,1},... | collective-permute-start | bytes 122888 | tf_op jit(solution)/shard_map/ppermute | solution.py:20
  50.8 4.0 %collective-permute-start.5 = (f32[80,128]{1,0:T(8,128)S(1)}, f32[80,128]{1,0:T(8,128)S(1)}, u32[]{:S(2)}, u32[]{:S(2)}) collective-permute-start(f32[80,128]{1,0:T(8,128)S(1)} %add.44), channel_id=1, source_target_pairs={{0,4},{1,5},{2,6},{3,7},{4,0},{5,1},{6,2},{7,3},{8,12},{9,13},{10,... | collective-permute-start | bytes 122888 | tf_op jit(solution)/shard_map/ppermute | solution.py:20
  52.3 5.5 %collective-permute-start.6 = (f32[80,128]{1,0:T(8,128)S(1)}, f32[80,128]{1,0:T(8,128)S(1)}, u32[]{:S(2)}, u32[]{:S(2)}) collective-permute-start(f32[80,128]{1,0:T(8,128)S(1)} %add.44), channel_id=1, source_target_pairs={{0,12},{1,13},{2,14},{3,15},{4,8},{5,9},{6,10},{7,11},{8,4},{9,5},... | collective-permute-start | bytes 122888 | tf_op jit(solution)/shard_map/ppermute | solution.py:20
  57.8 6.1 %collective-permute-start.7 = (f32[80,128]{1,0:T(8,128)S(1)}, f32[80,128]{1,0:T(8,128)S(1)}, u32[]{:S(2)}, u32[]{:S(2)}) collective-permute-start(f32[80,128]{1,0:T(8,128)S(1)} %add_add_fusion.mine_ref), channel_id=1, source_target_pairs={{0,1},{1,0},{2,3},{3,2},{4,5},{5,4},{6,7},{7,6},{8,9},{9,8},{10,11... | collective-permute-start | bytes 122888 | tf_op jit(solution)/shard_map/ppermute | solution.py:20
  62.0 2.9 %collective-permute-start.8 = (f32[80,128]{1,0:T(8,128)S(1)}, f32[80,128]{1,0:T(8,128)S(1)}, u32[]{:S(2)}, u32[]{:S(2)}) collective-permute-start(f32[80,128]{1,0:T(8,128)S(1)} %add_add_fusion.mine_ref), channel_id=1, source_target_pairs={{0,16},{16,0},{32,48},{48,32},{64,80},{80,64},{96,112},{112,96},{1... | collective-permute-start | bytes 122888 | tf_op jit(solution)/shard_map/ppermute | solution.py:20
  62.2 4.0 %collective-permute-start.9 = (f32[80,128]{1,0:T(8,128)S(1)}, f32[80,128]{1,0:T(8,128)S(1)}, u32[]{:S(2)}, u32[]{:S(2)}) collective-permute-start(f32[80,128]{1,0:T(8,128)S(1)} %add_add_fusion.mine_ref), channel_id=1, source_target_pairs={{0,17},{1,16},{2,19},{3,18},{4,21},{5,20},{6,23},{7,22},{8,25},{9,... | collective-permute-start | bytes 122888 | tf_op jit(solution)/shard_map/ppermute | solution.py:372

commit v10 on v9

--- a/solution.py
+++ b/solution.py
@@ -89,11 +89,10 @@
     return jnp.where(value < 0, -root, root)
 
 
-def filter_kernel(raw_ref, before_ref, table_ref, out_ref, extended_ref):
+def filter_kernel(raw_ref, table_ref, out_ref, extended_ref):
     own, samples = raw_ref.shape
-    receivers, _, width = out_ref.shape
-    part = width - 128
-    extended_ref[:, :RIM] = before_ref[...]
+    receivers, _, part = out_ref.shape
+    extended_ref[:, :RIM] = jnp.zeros((own, RIM), extended_ref.dtype)
     extended_ref[:, RIM:] = raw_ref[...]
     blocks = samples // STEP
     windows = jnp.concatenate(
@@ -101,36 +100,63 @@
     )
     bands = table_ref.shape[0] // 128
     share = part // 128
-    peaks = []
     for pair in range(bands // 2):
         both = dot_nt(windows, table_ref[256 * pair : 256 * pair + 256, :])
         for b in range(2):
-            largest = jnp.max(jnp.abs(both[:, 128 * b : 128 * b + 128]), axis=0, keepdims=True)
-            peaks.append(jnp.max(largest, axis=1, keepdims=True))
             for m in range(blocks):
                 place = (2 * pair + b) * (receivers // bands) + m // share
                 first = 128 * (m % share)
                 out_ref[place, :, first : first + 128] = both[
                     m * own : (m + 1) * own, 128 * b : 128 * b + 128
                 ]
+
+
+def message_kernel(filtered_ref, before_ref, table_ref, out_ref):
+    receivers, own, part = filtered_ref.shape
+    bands = table_ref.shape[0] // 128
+    shares = receivers // bands
+    firsts, peaks = [], []
+    for b in range(bands):
+        added = dot_nt(before_ref[...], table_ref[128 * b : 128 * b + 128, :RIM])
+        first = filtered_ref[shares * b, :, :128] + added
+        largest = jnp.max(jnp.abs(first), axis=0, keepdims=True)
+        for i in range(shares):
+            rest = filtered_ref[shares * b + i, :, 0 if i else 128 :]
+            rest = jnp.max(jnp.abs(rest), axis=0, keepdims=True)
+            for lane in range(0, rest.shape[1], 128):
+                largest = jnp.maximum(largest, rest[:, lane : lane + 128])
+        firsts.append(first)
+        peaks.append(jnp.max(largest, axis=1, keepdims=True))
     factors = powers_below(jnp.concatenate(peaks, axis=0) * 2.0**-6)
     scale = 1.0 / product(factors)
     for i in range(receivers):
-        b = i // (receivers // bands)
-        out_ref[i, :, :part] = squared(out_ref[i, :, :part] * scale[b : b + 1, :])
-        out_ref[i, :, part:] = on_lanes([factor[b : b + 1, :] for factor in factors], (own, 128))
+        b = i // shares
+        factor = scale[b : b + 1, :]
+        out_ref[i, :, :part] = squared(filtered_ref[i] * factor)
+        if i % shares == 0:
+            out_ref[i, :, :128] = squared(firsts[b] * factor)
+        out_ref[i, :, part:] = on_lanes([each[b : b + 1, :] for each in factors], (own, 128))
 
 
 def filtered(raw_strain, before, table, receivers):
     own, samples = raw_strain.shape
     part = table.shape[0] // 128 * (samples // 4) // receivers
-    return pl.pallas_call(
+    alone = pl.pallas_call(
         filter_kernel,
+        out_shape=jax.ShapeDtypeStruct((receivers, own, part), jnp.float32),
+        scratch_shapes=[pltpu.VMEM((own, samples + RIM), raw_strain.dtype)],
+        compiler_params=pltpu.CompilerParams(vmem_limit_bytes=VMEM_LIMIT),
+        cost_estimate=pl.CostEstimate(
+            flops=2 * 512 * 640 * 1024, bytes_accessed=4 << 20, transcendentals=0
+        ),
+        name="filtered",
+    )(raw_strain, table)
+    return pl.pallas_call(
+        message_kernel,
         out_shape=jax.ShapeDtypeStruct((receivers, own, part + 128), jnp.float32),
-        scratch_shapes=[pltpu.VMEM((own, samples + RIM), raw_strain.dtype)],
-        compiler_params=pltpu.CompilerParams(vmem_limit_bytes=VMEM_LIMIT),
-        name="filtered",
-    )(raw_strain, before, table)
+        compiler_params=pltpu.CompilerParams(vmem_limit_bytes=VMEM_LIMIT),
+        name="message",
+    )(alone, before, table)
 
 
 def gram_kernel(core_ref, message_ref, kept_ref, sent_ref, samples_ref, packed_ref):

time: 97.6 us -> 99.2 us (1.016)
  transfers between devices with their start and end apart: 11 -> 11, of which waited for: 8 -> 8; matrix products, arithmetic and copies ran while one was open for 1% -> 1% of each run, Pallas kernels for 0% -> 1%
where the time goes in v10:
time: 99.2 us; the launch traced here: 98.9 us
  waiting for transfers between devices  30.3 us (31%)
  starting transfers between devices  28.9 us (29%)
  blocking collectives  20.7 us (21%)
  Pallas kernels  14.6 us (15%)
  local copies, waits for them, and re-layouts  2.57 us (3%)
  other arithmetic  1.63 us (2%)
    all_to_all x1, blocking collectives, shards(): result = lax.all_to_all(result, 'chan', 0, 0, tiled=True)  20.7 us
    all_to_all x1, waiting for transfers between devices, shards(): lax.all_to_all(message, 'chan', 0, 0, tiled=True).astype(jnp.float32)  17.9 us
    ppermute x8, starting transfers between devices, swapped(): return lax.ppermute(block, axis, route)  15.6 us
    ppermute x8, waiting for transfers between devices, swapped(): return lax.ppermute(block, axis, route)  11.1 us
    pallas_call x1, Pallas kernels, denoised_band(): pl.pallas_call(refine_kernel, in_specs=[pl.BlockSpec(memory_space=pltpu.S...  8.45 us
    all_to_all x1, starting transfers between devices, shards(): lax.all_to_all(message, 'chan', 0, 0, tiled=True).astype(jnp.float32)  6.76 us
    ppermute x1, starting transfers between devices, shards(): lax.ppermute(rim_piece, 'tm', [(i, i + 1) for i in range(tm_count - 1)])  4.92 us
    pallas_call x1, Pallas kernels, restored(): pl.pallas_call(restore_kernel, grid=(steps,), in_specs=[pl.BlockSpec((sou...  2.03 us
  transfers between devices with their start and end apart: 11, of which 8 were waited for; matrix products, arithmetic and copies ran while one was open for 1% of the time, Pallas kernels for 1%

profile of v10, /device:TPU:1, one launch (start us, length us, event | category | flops | bytes accessed | tf_op | source)
XLA Modules:
  0.0 98.9 jit_solution(17034734914771075422)
XLA Ops:
  0.0 0.0 copy-start
  0.0 0.7 slice.3
  0.7 4.9 %collective-permute-start = (bf16[16,128]{1,0:T(8,128)(2,1)S(1)}, bf16[16,128]{1,0:T(8,128)(2,1)S(1)}, u32[]{:S(2)}, u32[]{:S(2)}) collective-permute-start(bf16[16,128]{1,0:T(8,128)(2,1)S(1)} %slice.3), channel_id=1, source_target_pairs={{0,1},{1,2},{2,3},{3,4},{4,5},{5,6},{6,7},{7,8},{8,9},{9,10},{10,1... | collective-permute-start | bytes 12296 | tf_op jit(solution)/shard_map/ppermute | solution.py:378
  5.7 0.7 copy.5.taps_ref
  6.4 0.2 filter_table.1.table_ref
  6.5 0.0 copy-start.1
  6.6 1.0 %copy-done.1 = bf16[16,16384]{1,0:T(8,128)(2,1)S(1)} copy-done((bf16[16,16384]{1,0:T(8,128)(2,1)S(1)}, bf16[16,16384]{1,0:T(8,128)(2,1)}, u32[]{:S(2)}) %copy-start.1) | copy-done | bytes 524312
  7.6 1.1 %filtered.1.filtered_ref = f32[16,16,2048]{2,1,0:T(8,128)S(1)} custom-call(bf16[16,16384]{1,0:T(8,128)(2,1)S(1)} %copy-done.1, bf16[1024,640]{1,0:T(8,128)(2,1)S(1)} %filter_table.1.table_ref), custom_call_target="tpu_custom_call" | custom-call | flops 671088640 | bytes 4194304 | tf_op jit(solution)/shard_map/filtered/pallas_call | solution.py:144
  8.7 0.0 collective-permute-done.before_ref
  8.7 0.9 message.1
  9.6 1.1 %convert_element_type.15 = f16[16,16,2176]{2,1,0:T(8,128)(2,1)} convert(f32[16,16,2176]{2,1,0:T(8,128)S(1)} %message.1) | non-fusion elementwise | flops 557056 | bytes 3342336 | tf_op jit(solution)/shard_map/convert_element_type | solution.py:381
  10.7 6.8 %all-to-all-start = ((f16[16,16,2176]{2,1,0:T(8,128)(2,1)}), f16[16,16,2176]{2,1,0:T(8,128)(2,1)S(1)}, u32[]{:S(2)}, u32[]{:S(2)}) async-start(f16[16,16,2176]{2,1,0:T(8,128)(2,1)} %convert_element_type.15), calls=%async_computation | async-start | bytes 2228224 | tf_op jit(solution)/shard_map/all_to_all | solution.py:382
  17.5 17.9 %all-to-all-done = f16[16,16,2176]{2,1,0:T(8,128)(2,1)S(1)} async-done(((f16[16,16,2176]{2,1,0:T(8,128)(2,1)}), f16[16,16,2176]{2,1,0:T(8,128)(2,1)S(1)}, u32[]{:S(2)}, u32[]{:S(2)}) %all-to-all-start) | async-done | bytes 1114144 | tf_op jit(solution)/shard_map/all_to_all | solution.py:382
  35.3 0.1 convert_element_type.16.message_ref
  35.5 2.0 %band_gram.1 = (f32[160,128]{1,0:T(8,128)S(1)}, f32[160,128]{1,0:T(8,128)S(1)}, f32[256,2048]{1,0:T(8,128)S(1)}) custom-call(s32[1]{0:T(128)} %bitcast.core_ref, f32[16,16,2176]{2,1,0:T(8,128)S(1)} %convert_element_type.16.message_ref), custom_call_target="tpu_custom_call" | custom-call | tf_op jit(solution)/shard_map/band_gram/pallas_call | solution.py:188
  37.5 0.1 collective-permute-start.1
  37.6 1.2 %collective-permute-done.1 = f32[160,128]{1,0:T(8,128)S(1)} collective-permute-done((f32[160,128]{1,0:T(8,128)S(1)}, f32[160,128]{1,0:T(8,128)S(1)}, u32[]{:S(2)}, u32[]{:S(2)}) %collective-permute-start.1) | collective-permute-done | bytes 81952 | tf_op jit(solution)/shard_map/ppermute | solution.py:20
  38.9 0.4 collective-permute-start.2
  39.2 2.6 %collective-permute-done.2 = f32[80,128]{1,0:T(8,128)S(1)} collective-permute-done((f32[80,128]{1,0:T(8,128)S(1)}, f32[80,128]{1,0:T(8,128)S(1)}, u32[]{:S(2)}, u32[]{:S(2)}) %collective-permute-start.2) | collective-permute-done | bytes 40992 | tf_op jit(solution)/shard_map/ppermute | solution.py:20
  41.8 1.9 %collective-permute-start.3 = (f32[80,128]{1,0:T(8,128)S(1)}, f32[80,128]{1,0:T(8,128)S(1)}, u32[]{:S(2)}, u32[]{:S(2)}) collective-permute-start(f32[80,128]{1,0:T(8,128)S(1)} %bitcast_add_fusion), channel_id=1, source_target_pairs={{0,2},{1,3},{2,0},{3,1},{4,6},{5,7},{6,4},{7,5},{8,10},{9,11},{10,... | collective-permute-start | bytes 122888 | tf_op jit(solution)/shard_map/ppermute | solution.py:20
  43.7 1.4 %collective-permute-done.3 = f32[80,128]{1,0:T(8,128)S(1)} collective-permute-done((f32[80,128]{1,0:T(8,128)S(1)}, f32[80,128]{1,0:T(8,128)S(1)}, u32[]{:S(2)}, u32[]{:S(2)}) %collective-permute-start.3) | collective-permute-done | bytes 40992 | tf_op jit(solution)/shard_map/ppermute | solution.py:20
  45.1 6.9 %collective-permute-start.4 = (f32[80,128]{1,0:T(8,128)S(1)}, f32[80,128]{1,0:T(8,128)S(1)}, u32[]{:S(2)}, u32[]{:S(2)}) collective-permute-start(f32[80,128]{1,0:T(8,128)S(1)} %add.44), channel_id=1, source_target_pairs={{0,8},{1,9},{2,10},{3,11},{4,12},{5,13},{6,14},{7,15},{8,0},{9,1},... | collective-permute-start | bytes 122888 | tf_op jit(solution)/shard_map/ppermute | solution.py:20
  52.0 1.6 %collective-permute-start.5 = (f32[80,128]{1,0:T(8,128)S(1)}, f32[80,128]{1,0:T(8,128)S(1)}, u32[]{:S(2)}, u32[]{:S(2)}) collective-permute-start(f32[80,128]{1,0:T(8,128)S(1)} %add.44), channel_id=1, source_target_pairs={{0,4},{1,5},{2,6},{3,7},{4,0},{5,1},{6,2},{7,3},{8,12},{9,13},{10,... | collective-permute-start | bytes 122888 | tf_op jit(solution)/shard_map/ppermute | solution.py:20
  53.6 0.0 collective-permute-start.6
  53.6 0.0 copy-done
  53.7 0.0 collective-permute-done.4
  53.7 2.4 %collective-permute-done.5 = f32[80,128]{1,0:T(8,128)S(1)} collective-permute-done((f32[80,128]{1,0:T(8,128)S(1)}, f32[80,128]{1,0:T(8,128)S(1)}, u32[]{:S(2)}, u32[]{:S(2)}) %collective-permute-start.5) | collective-permute-done | bytes 40992 | tf_op jit(solution)/shard_map/ppermute | solution.py:20
  56.1 2.5 %collective-permute-done.6 = f32[80,128]{1,0:T(8,128)S(1)} collective-permute-done((f32[80,128]{1,0:T(8,128)S(1)}, f32[80,128]{1,0:T(8,128)S(1)}, u32[]{:S(2)}, u32[]{:S(2)}) %collective-permute-start.6) | collective-permute-done | bytes 40992 | tf_op jit(solution)/shard_map/ppermute | solution.py:20
  58.6 4.6 %collective-permute-start.7 = (f32[80,128]{1,0:T(8,128)S(1)}, f32[80,128]{1,0:T(8,128)S(1)}, u32[]{:S(2)}, u32[]{:S(2)}) collective-permute-start(f32[80,128]{1,0:T(8,128)S(1)} %add_add_fusion.mine_ref), channel_id=1, source_target_pairs={{0,1},{1,0},{2,3},{3,2},{4,5},{5,4},{6,7},{7,6},{8,9},{9,8},{10,11... | collective-permute-start | bytes 122888 | tf_op jit(solution)/shard_map/ppermute | solution.py:20
  63.2 0.1 collective-permute-start.8
  63.3 1.6 %collective-permute-start.9 = (f32[80,128]{1,0:T(8,128)S(1)}, f32[80,128]{1,0:T(8,128)S(1)}, u32[]{:S(2)}, u32[]{:S(2)}) collective-permute-start(f32[80,128]{1,0:T(8,128)S(1)} %add_add_fusion.mine_ref), channel_id=1, source_target_pairs={{0,17},{1,16},{2,19},{3,18},{4,21},{5,20},{6,23},{7,22},{8,25},{9,... | collective-permute-start | bytes 122888 | tf_op jit(solution)/shard_map/ppermute | solution.py:398
  64.9 0.1 pad_add_fusion.place_ref
  65.0 0.1 copy.6
  65.1 0.0 collective-permute-done.7.core_ref
  65.1 1.0 collective-permute-done.8.chan_ref
  66.1 1.3 %collective-permute-done.9.both_ref = f32[80,128]{1,0:T(8,128)S(1)} collective-permute-done((f32[80,128]{1,0:T(8,128)S(1)}, f32[80,128]{1,0:T(8,128)S(1)}, u32[]{:S(2)}, u32[]{:S(2)}) %collective-permute-start.9) | collective-permute-done | bytes 40992 | tf_op jit(solution)/shard_map/ppermute | solution.py:398
  67.4 8.4 %denoised_band.1 = f32[256,2176]{1,0:T(8,128)S(1)} custom-call(s32[2]{0:T(128)S(1)} %pad_add_fusion.place_ref, f32[80,128]{1,0:T(8,128)S(1)} %add_add_fusion.mine_ref, f32[80,128]{1,0:T(8,128)S(1)} %collective-permute-done.7.core_ref, f32[80,128]{1,0:T(8,128)S(1)} %collective-permute-done.8.chan_ref, f32[80,128]{1,0:T(8,128)S(1)} %collective-permute-done.9.both_ref, ...), custom_call_target="tpu_custom_call" | custom-call | tf_op jit(solution)/shard_map/denoised_band/pallas_call | solution.py:334
  75.9 0.1 convert_element_type.17
  76.0 20.7 %all_to_all.10 = f16[16,16,2176]{2,1,0:T(8,128)(2,1)S(1)} all-to-all(f16[16,16,2176]{2,1,0:T(8,128)(2,1)S(1)} %bitcast.11), channel_id=1, replica_groups=mesh['chan'=16,'tm'=16] {'chan'}, dimensions={0} | all-to-all | bytes 2228224 | tf_op jit(solution)/shard_map/all_to_all | solution.py:404
  96.7 0.1 convert_element_type.19.message_ref
  96.8 2.0 %restored.1 = f32[8,16,4096]{2,1,0:T(8,128)} custom-call(f32[16,16,2176]{2,1,0:T(8,128)S(1)} %convert_element_type.19.message_ref), custom_call_target="tpu_custom_call" | custom-call | tf_op jit(solution)/shard_map/restored/pallas_call | solution.py:360
  (6 shorter events, 0.1 us)
Async XLA Ops:
  0.0 53.7 %copy-start = (f32[8,256,32]{1,2,0:T(8,128)S(1)}, f32[8,256,32]{1,2,0:T(8,128)}, u32[]{:S(2)}) copy-start(f32[8,256,32]{1,2,0:T(8,128)} %param.5) | copy-start | bytes 786436
  0.7 7.9 %collective-permute-start = (bf16[16,128]{1,0:T(8,128)(2,1)S(1)}, bf16[16,128]{1,0:T(8,128)(2,1)S(1)}, u32[]{:S(2)}, u32[]{:S(2)}) collective-permute-start(bf16[16,128]{1,0:T(8,128)(2,1)S(1)} %slice.3), channel_id=1, source_target_pairs={{0,1},{1,2},{2,3},{3,4},{4,5},{5,6},{6,7},{7,8},{8,9},{9,10},{10,1... | collective-permute-start | bytes 12296 | tf_op jit(solution)/shard_map/ppermute | solution.py:378
  6.5 1.0 %copy-start.1 = (bf16[16,16384]{1,0:T(8,128)(2,1)S(1)}, bf16[16,16384]{1,0:T(8,128)(2,1)}, u32[]{:S(2)}) copy-start(bf16[16,16384]{1,0:T(8,128)(2,1)} %raw_ref.1) | copy-start | bytes 1572868
  10.7 24.6 %all-to-all-start = ((f16[16,16,2176]{2,1,0:T(8,128)(2,1)}), f16[16,16,2176]{2,1,0:T(8,128)(2,1)S(1)}, u32[]{:S(2)}, u32[]{:S(2)}) async-start(f16[16,16,2176]{2,1,0:T(8,128)(2,1)} %convert_element_type.15), calls=%async_computation | async-start | bytes 2228224 | tf_op jit(solution)/shard_map/all_to_all | solution.py:382
  37.5 1.4 %collective-permute-start.1 = (f32[160,128]{1,0:T(8,128)S(1)}, f32[160,128]{1,0:T(8,128)S(1)}, u32[]{:S(2)}, u32[]{:S(2)}) collective-permute-start(f32[160,128]{1,0:T(8,128)S(1)} %get-tuple-element.9), channel_id=1, source_target_pairs={{0,1},{1,0},{2,3},{3,2},{4,5},{5,4},{6,7},{7,6},{8,9},{9,8},{10,11... | collective-permute-start | bytes 245768 | tf_op jit(solution)/shard_map/ppermute | solution.py:20
  38.9 2.9 %collective-permute-start.2 = (f32[80,128]{1,0:T(8,128)S(1)}, f32[80,128]{1,0:T(8,128)S(1)}, u32[]{:S(2)}, u32[]{:S(2)}) collective-permute-start(f32[80,128]{1,0:T(8,128)S(1)} %dynamic-slice_bitcast_fusion), channel_id=1, source_target_pairs={{0,16},{16,0},{32,48},{48,32},{64,80},{80,64},{96,112},{112,96},{1... | collective-permute-start | bytes 122888 | tf_op jit(solution)/shard_map/ppermute | solution.py:20
  41.8 3.3 %collective-permute-start.3 = (f32[80,128]{1,0:T(8,128)S(1)}, f32[80,128]{1,0:T(8,128)S(1)}, u32[]{:S(2)}, u32[]{:S(2)}) collective-permute-start(f32[80,128]{1,0:T(8,128)S(1)} %bitcast_add_fusion), channel_id=1, source_target_pairs={{0,2},{1,3},{2,0},{3,1},{4,6},{5,7},{6,4},{7,5},{8,10},{9,11},{10,... | collective-permute-start | bytes 122888 | tf_op jit(solution)/shard_map/ppermute | solution.py:20
  45.1 8.6 %collective-permute-start.4 = (f32[80,128]{1,0:T(8,128)S(1)}, f32[80,128]{1,0:T(8,128)S(1)}, u32[]{:S(2)}, u32[]{:S(2)}) collective-permute-start(f32[80,128]{1,0:T(8,128)S(1)} %add.44), channel_id=1, source_target_pairs={{0,8},{1,9},{2,10},{3,11},{4,12},{5,13},{6,14},{7,15},{8,0},{9,1},... | collective-permute-start | bytes 122888 | tf_op jit(solution)/shard_map/ppermute | solution.py:20
  52.0 4.0 %collective-permute-start.5 = (f32[80,128]{1,0:T(8,128)S(1)}, f32[80,128]{1,0:T(8,128)S(1)}, u32[]{:S(2)}, u32[]{:S(2)}) collective-permute-start(f32[80,128]{1,0:T(8,128)S(1)} %add.44), channel_id=1, source_target_pairs={{0,4},{1,5},{2,6},{3,7},{4,0},{5,1},{6,2},{7,3},{8,12},{9,13},{10,... | collective-permute-start | bytes 122888 | tf_op jit(solution)/shard_map/ppermute | solution.py:20
  53.6 5.0 %collective-permute-start.6 = (f32[80,128]{1,0:T(8,128)S(1)}, f32[80,128]{1,0:T(8,128)S(1)}, u32[]{:S(2)}, u32[]{:S(2)}) collective-permute-start(f32[80,128]{1,0:T(8,128)S(1)} %add.44), channel_id=1, source_target_pairs={{0,12},{1,13},{2,14},{3,15},{4,8},{5,9},{6,10},{7,11},{8,4},{9,5},... | collective-permute-start | bytes 122888 | tf_op jit(solution)/shard_map/ppermute | solution.py:20
  58.6 6.5 %collective-permute-start.7 = (f32[80,128]{1,0:T(8,128)S(1)}, f32[80,128]{1,0:T(8,128)S(1)}, u32[]{:S(2)}, u32[]{:S(2)}) collective-permute-start(f32[80,128]{1,0:T(8,128)S(1)} %add_add_fusion.mine_ref), channel_id=1, source_target_pairs={{0,1},{1,0},{2,3},{3,2},{4,5},{5,4},{6,7},{7,6},{8,9},{9,8},{10,11... | collective-permute-start | bytes 122888 | tf_op jit(solution)/shard_map/ppermute | solution.py:20
  63.2 2.9 %collective-permute-start.8 = (f32[80,128]{1,0:T(8,128)S(1)}, f32[80,128]{1,0:T(8,128)S(1)}, u32[]{:S(2)}, u32[]{:S(2)}) collective-permute-start(f32[80,128]{1,0:T(8,128)S(1)} %add_add_fusion.mine_ref), channel_id=1, source_target_pairs={{0,16},{16,0},{32,48},{48,32},{64,80},{80,64},{96,112},{112,96},{1... | collective-permute-start | bytes 122888 | tf_op jit(solution)/shard_map/ppermute | solution.py:20
  63.3 4.1 %collective-permute-start.9 = (f32[80,128]{1,0:T(8,128)S(1)}, f32[80,128]{1,0:T(8,128)S(1)}, u32[]{:S(2)}, u32[]{:S(2)}) collective-permute-start(f32[80,128]{1,0:T(8,128)S(1)} %add_add_fusion.mine_ref), channel_id=1, source_target_pairs={{0,17},{1,16},{2,19},{3,18},{4,21},{5,20},{6,23},{7,22},{8,25},{9,... | collective-permute-start | bytes 122888 | tf_op jit(solution)/shard_map/ppermute | solution.py:398

commit v11 on v9

--- a/solution.py
+++ b/solution.py
@@ -222,16 +222,16 @@
     unit = (rows == columns).astype(jnp.float32)
     both = jnp.concatenate([compact, unit], axis=1)
     below = lax.broadcasted_iota(jnp.int32, both.shape, 0)
-    for block in range(0, rank, 8):
+    for block in range(0, rank, 16):
         spread = [
-            jnp.broadcast_to(both[:, block + p : block + p + 1], both.shape) for p in range(8)
+            jnp.broadcast_to(both[:, block + p : block + p + 1], both.shape) for p in range(16)
         ]
-        for p in range(8):
+        for p in range(16):
             j = block + p
             column = spread[p]
             factor = jnp.where(below > j, column * (1.0 / column[j : j + 1, :]), 0.0)
             both = both - factor * both[j : j + 1, :]
-            for q in range(p + 1, 8):
+            for q in range(p + 1, 16):
                 spread[q] = spread[q] - factor * spread[q][j : j + 1, :]
     pivots = jnp.sum(unit * both[:, :rank], axis=1, keepdims=True)
     return both[:, rank:] / jnp.sqrt(pivots)

time: 97.6 us -> 97.1 us (level)
  no operation moved by 1% of the time
where the time goes in v11:
time: 97.1 us; the launch traced here: 96.8 us
  waiting for transfers between devices  29.5 us (30%)
  starting transfers between devices  29 us (30%)
  blocking collectives  20.3 us (21%)
  Pallas kernels  13.6 us (14%)
  local copies, waits for them, and re-layouts  2.57 us (3%)
  other arithmetic  1.63 us (2%)
    all_to_all x1, blocking collectives, shards(): result = lax.all_to_all(result, 'chan', 0, 0, tiled=True)  20.3 us
    all_to_all x1, waiting for transfers between devices, shards(): lax.all_to_all(message, 'chan', 0, 0, tiled=True).astype(jnp.float32)  17.9 us
    ppermute x8, starting transfers between devices, swapped(): return lax.ppermute(block, axis, route)  15.8 us
    ppermute x8, waiting for transfers between devices, swapped(): return lax.ppermute(block, axis, route)  10.3 us
    pallas_call x1, Pallas kernels, denoised_band(): pl.pallas_call(refine_kernel, in_specs=[pl.BlockSpec(memory_space=pltpu.S...  7.94 us
    all_to_all x1, starting transfers between devices, shards(): lax.all_to_all(message, 'chan', 0, 0, tiled=True).astype(jnp.float32)  6.75 us
    ppermute x1, starting transfers between devices, shards(): lax.ppermute(rim_piece, 'tm', [(i, i + 1) for i in range(tm_count - 1)])  4.92 us
    pallas_call x1, Pallas kernels, restored(): pl.pallas_call(restore_kernel, grid=(steps,), in_specs=[pl.BlockSpec((sou...  2.03 us
  transfers between devices with their start and end apart: 11, of which 8 were waited for; matrix products, arithmetic and copies ran while one was open for 1% of the time, Pallas kernels for 0%

profile of v11, /device:TPU:1, one launch (start us, length us, event | category | flops | bytes accessed | tf_op | source)
XLA Modules:
  0.0 96.8 jit_solution(15501026094067562568)
XLA Ops:
  0.0 0.0 copy-start
  0.0 0.7 slice.3
  0.7 4.9 %collective-permute-start = (bf16[16,128]{1,0:T(8,128)(2,1)S(1)}, bf16[16,128]{1,0:T(8,128)(2,1)S(1)}, u32[]{:S(2)}, u32[]{:S(2)}) collective-permute-start(bf16[16,128]{1,0:T(8,128)(2,1)S(1)} %slice.3), channel_id=1, source_target_pairs={{0,1},{1,2},{2,3},{3,4},{4,5},{5,6},{6,7},{7,8},{8,9},{9,10},{10,1... | collective-permute-start | bytes 12296 | tf_op jit(solution)/shard_map/ppermute | solution.py:352
  5.7 0.7 copy.5.taps_ref
  6.4 0.2 filter_table.1.table_ref
  6.5 0.0 collective-permute-done.before_ref
  6.6 0.0 copy-start.1
  6.6 1.0 %copy-done.1 = bf16[16,16384]{1,0:T(8,128)(2,1)S(1)} copy-done((bf16[16,16384]{1,0:T(8,128)(2,1)S(1)}, bf16[16,16384]{1,0:T(8,128)(2,1)}, u32[]{:S(2)}) %copy-start.1) | copy-done | bytes 524312
  7.6 1.5 %filtered.1 = f32[16,16,2176]{2,1,0:T(8,128)S(1)} custom-call(bf16[16,16384]{1,0:T(8,128)(2,1)S(1)} %copy-done.1, bf16[16,128]{1,0:T(8,128)(2,1)S(1)} %collective-permute-done.before_ref, bf16[1024,640]{1,0:T(8,128)(2,1)S(1)} %filter_table.1.table_ref), custom_call_target="tpu_custom_call" | custom-call | tf_op jit(solution)/shard_map/filtered/pallas_call | solution.py:127
  9.1 1.1 %convert_element_type.15 = f16[16,16,2176]{2,1,0:T(8,128)(2,1)} convert(f32[16,16,2176]{2,1,0:T(8,128)S(1)} %filtered.1) | non-fusion elementwise | flops 557056 | bytes 3342336 | tf_op jit(solution)/shard_map/convert_element_type | solution.py:355
  10.2 6.8 %all-to-all-start = ((f16[16,16,2176]{2,1,0:T(8,128)(2,1)}), f16[16,16,2176]{2,1,0:T(8,128)(2,1)S(1)}, u32[]{:S(2)}, u32[]{:S(2)}) async-start(f16[16,16,2176]{2,1,0:T(8,128)(2,1)} %convert_element_type.15), calls=%async_computation | async-start | bytes 2228224 | tf_op jit(solution)/shard_map/all_to_all | solution.py:356
  17.0 17.9 %all-to-all-done = f16[16,16,2176]{2,1,0:T(8,128)(2,1)S(1)} async-done(((f16[16,16,2176]{2,1,0:T(8,128)(2,1)}), f16[16,16,2176]{2,1,0:T(8,128)(2,1)S(1)}, u32[]{:S(2)}, u32[]{:S(2)}) %all-to-all-start) | async-done | bytes 1114144 | tf_op jit(solution)/shard_map/all_to_all | solution.py:356
  34.9 0.1 convert_element_type.16.message_ref
  35.0 2.0 %band_gram.1 = (f32[160,128]{1,0:T(8,128)S(1)}, f32[160,128]{1,0:T(8,128)S(1)}, f32[256,2048]{1,0:T(8,128)S(1)}) custom-call(s32[1]{0:T(128)} %bitcast.core_ref, f32[16,16,2176]{2,1,0:T(8,128)S(1)} %convert_element_type.16.message_ref), custom_call_target="tpu_custom_call" | custom-call | tf_op jit(solution)/shard_map/band_gram/pallas_call | solution.py:162
  37.0 0.1 collective-permute-start.1
  37.1 1.2 %collective-permute-done.1 = f32[160,128]{1,0:T(8,128)S(1)} collective-permute-done((f32[160,128]{1,0:T(8,128)S(1)}, f32[160,128]{1,0:T(8,128)S(1)}, u32[]{:S(2)}, u32[]{:S(2)}) %collective-permute-start.1) | collective-permute-done | bytes 81952 | tf_op jit(solution)/shard_map/ppermute | solution.py:20
  38.4 0.4 collective-permute-start.2
  38.8 2.6 %collective-permute-done.2 = f32[80,128]{1,0:T(8,128)S(1)} collective-permute-done((f32[80,128]{1,0:T(8,128)S(1)}, f32[80,128]{1,0:T(8,128)S(1)}, u32[]{:S(2)}, u32[]{:S(2)}) %collective-permute-start.2) | collective-permute-done | bytes 40992 | tf_op jit(solution)/shard_map/ppermute | solution.py:20
  41.3 3.0 %collective-permute-start.3 = (f32[80,128]{1,0:T(8,128)S(1)}, f32[80,128]{1,0:T(8,128)S(1)}, u32[]{:S(2)}, u32[]{:S(2)}) collective-permute-start(f32[80,128]{1,0:T(8,128)S(1)} %bitcast_add_fusion), channel_id=1, source_target_pairs={{0,2},{1,3},{2,0},{3,1},{4,6},{5,7},{6,4},{7,5},{8,10},{9,11},{10,... | collective-permute-start | bytes 122888 | tf_op jit(solution)/shard_map/ppermute | solution.py:20
  44.3 1.4 %collective-permute-done.3 = f32[80,128]{1,0:T(8,128)S(1)} collective-permute-done((f32[80,128]{1,0:T(8,128)S(1)}, f32[80,128]{1,0:T(8,128)S(1)}, u32[]{:S(2)}, u32[]{:S(2)}) %collective-permute-start.3) | collective-permute-done | bytes 40992 | tf_op jit(solution)/shard_map/ppermute | solution.py:20
  45.7 5.1 %collective-permute-start.4 = (f32[80,128]{1,0:T(8,128)S(1)}, f32[80,128]{1,0:T(8,128)S(1)}, u32[]{:S(2)}, u32[]{:S(2)}) collective-permute-start(f32[80,128]{1,0:T(8,128)S(1)} %add.44), channel_id=1, source_target_pairs={{0,8},{1,9},{2,10},{3,11},{4,12},{5,13},{6,14},{7,15},{8,0},{9,1},... | collective-permute-start | bytes 122888 | tf_op jit(solution)/shard_map/ppermute | solution.py:20
  50.8 1.5 %collective-permute-start.5 = (f32[80,128]{1,0:T(8,128)S(1)}, f32[80,128]{1,0:T(8,128)S(1)}, u32[]{:S(2)}, u32[]{:S(2)}) collective-permute-start(f32[80,128]{1,0:T(8,128)S(1)} %add.44), channel_id=1, source_target_pairs={{0,4},{1,5},{2,6},{3,7},{4,0},{5,1},{6,2},{7,3},{8,12},{9,13},{10,... | collective-permute-start | bytes 122888 | tf_op jit(solution)/shard_map/ppermute | solution.py:20
  52.3 1.3 %collective-permute-start.6 = (f32[80,128]{1,0:T(8,128)S(1)}, f32[80,128]{1,0:T(8,128)S(1)}, u32[]{:S(2)}, u32[]{:S(2)}) collective-permute-start(f32[80,128]{1,0:T(8,128)S(1)} %add.44), channel_id=1, source_target_pairs={{0,12},{1,13},{2,14},{3,15},{4,8},{5,9},{6,10},{7,11},{8,4},{9,5},... | collective-permute-start | bytes 122888 | tf_op jit(solution)/shard_map/ppermute | solution.py:20
  53.6 0.0 copy-done
  53.6 0.0 collective-permute-done.4
  53.6 1.2 %collective-permute-done.5 = f32[80,128]{1,0:T(8,128)S(1)} collective-permute-done((f32[80,128]{1,0:T(8,128)S(1)}, f32[80,128]{1,0:T(8,128)S(1)}, u32[]{:S(2)}, u32[]{:S(2)}) %collective-permute-start.5) | collective-permute-done | bytes 40992 | tf_op jit(solution)/shard_map/ppermute | solution.py:20
  54.9 2.9 %collective-permute-done.6 = f32[80,128]{1,0:T(8,128)S(1)} collective-permute-done((f32[80,128]{1,0:T(8,128)S(1)}, f32[80,128]{1,0:T(8,128)S(1)}, u32[]{:S(2)}, u32[]{:S(2)}) %collective-permute-start.6) | collective-permute-done | bytes 40992 | tf_op jit(solution)/shard_map/ppermute | solution.py:20
  57.8 4.2 %collective-permute-start.7 = (f32[80,128]{1,0:T(8,128)S(1)}, f32[80,128]{1,0:T(8,128)S(1)}, u32[]{:S(2)}, u32[]{:S(2)}) collective-permute-start(f32[80,128]{1,0:T(8,128)S(1)} %add_add_fusion.mine_ref), channel_id=1, source_target_pairs={{0,1},{1,0},{2,3},{3,2},{4,5},{5,4},{6,7},{7,6},{8,9},{9,8},{10,11... | collective-permute-start | bytes 122888 | tf_op jit(solution)/shard_map/ppermute | solution.py:20
  62.0 0.2 collective-permute-start.8
  62.2 1.5 %collective-permute-start.9 = (f32[80,128]{1,0:T(8,128)S(1)}, f32[80,128]{1,0:T(8,128)S(1)}, u32[]{:S(2)}, u32[]{:S(2)}) collective-permute-start(f32[80,128]{1,0:T(8,128)S(1)} %add_add_fusion.mine_ref), channel_id=1, source_target_pairs={{0,17},{1,16},{2,19},{3,18},{4,21},{5,20},{6,23},{7,22},{8,25},{9,... | collective-permute-start | bytes 122888 | tf_op jit(solution)/shard_map/ppermute | solution.py:372
  63.7 0.1 pad_add_fusion.place_ref
  63.8 0.1 copy.6
  63.9 0.0 collective-permute-done.7.core_ref
  63.9 1.0 collective-permute-done.8.chan_ref
  64.9 1.3 %collective-permute-done.9.both_ref = f32[80,128]{1,0:T(8,128)S(1)} collective-permute-done((f32[80,128]{1,0:T(8,128)S(1)}, f32[80,128]{1,0:T(8,128)S(1)}, u32[]{:S(2)}, u32[]{:S(2)}) %collective-permute-start.9) | collective-permute-done | bytes 40992 | tf_op jit(solution)/shard_map/ppermute | solution.py:372
  66.2 7.9 %denoised_band.1 = f32[256,2176]{1,0:T(8,128)S(1)} custom-call(s32[2]{0:T(128)S(1)} %pad_add_fusion.place_ref, f32[80,128]{1,0:T(8,128)S(1)} %add_add_fusion.mine_ref, f32[80,128]{1,0:T(8,128)S(1)} %collective-permute-done.7.core_ref, f32[80,128]{1,0:T(8,128)S(1)} %collective-permute-done.8.chan_ref, f32[80,128]{1,0:T(8,128)S(1)} %collective-permute-done.9.both_ref, ...), custom_call_target="tpu_custom_call" | custom-call | tf_op jit(solution)/shard_map/denoised_band/pallas_call | solution.py:308
  74.2 0.1 convert_element_type.17
  74.3 20.3 %all_to_all.10 = f16[16,16,2176]{2,1,0:T(8,128)(2,1)S(1)} all-to-all(f16[16,16,2176]{2,1,0:T(8,128)(2,1)S(1)} %bitcast.11), channel_id=1, replica_groups=mesh['chan'=16,'tm'=16] {'chan'}, dimensions={0} | all-to-all | bytes 2228224 | tf_op jit(solution)/shard_map/all_to_all | solution.py:378
  94.6 0.1 convert_element_type.19.message_ref
  94.8 2.0 %restored.1 = f32[8,16,4096]{2,1,0:T(8,128)} custom-call(f32[16,16,2176]{2,1,0:T(8,128)S(1)} %convert_element_type.19.message_ref), custom_call_target="tpu_custom_call" | custom-call | tf_op jit(solution)/shard_map/restored/pallas_call | solution.py:334
  (6 shorter events, 0.1 us)
Async XLA Ops:
  0.0 53.6 %copy-start = (f32[8,256,32]{1,2,0:T(8,128)S(1)}, f32[8,256,32]{1,2,0:T(8,128)}, u32[]{:S(2)}) copy-start(f32[8,256,32]{1,2,0:T(8,128)} %param.5) | copy-start | bytes 786436
  0.7 5.8 %collective-permute-start = (bf16[16,128]{1,0:T(8,128)(2,1)S(1)}, bf16[16,128]{1,0:T(8,128)(2,1)S(1)}, u32[]{:S(2)}, u32[]{:S(2)}) collective-permute-start(bf16[16,128]{1,0:T(8,128)(2,1)S(1)} %slice.3), channel_id=1, source_target_pairs={{0,1},{1,2},{2,3},{3,4},{4,5},{5,6},{6,7},{7,8},{8,9},{9,10},{10,1... | collective-permute-start | bytes 12296 | tf_op jit(solution)/shard_map/ppermute | solution.py:352
  6.6 1.0 %copy-start.1 = (bf16[16,16384]{1,0:T(8,128)(2,1)S(1)}, bf16[16,16384]{1,0:T(8,128)(2,1)}, u32[]{:S(2)}) copy-start(bf16[16,16384]{1,0:T(8,128)(2,1)} %raw_ref.1) | copy-start | bytes 1572868
  10.2 24.6 %all-to-all-start = ((f16[16,16,2176]{2,1,0:T(8,128)(2,1)}), f16[16,16,2176]{2,1,0:T(8,128)(2,1)S(1)}, u32[]{:S(2)}, u32[]{:S(2)}) async-start(f16[16,16,2176]{2,1,0:T(8,128)(2,1)} %convert_element_type.15), calls=%async_computation | async-start | bytes 2228224 | tf_op jit(solution)/shard_map/all_to_all | solution.py:356
  37.0 1.4 %collective-permute-start.1 = (f32[160,128]{1,0:T(8,128)S(1)}, f32[160,128]{1,0:T(8,128)S(1)}, u32[]{:S(2)}, u32[]{:S(2)}) collective-permute-start(f32[160,128]{1,0:T(8,128)S(1)} %get-tuple-element.9), channel_id=1, source_target_pairs={{0,1},{1,0},{2,3},{3,2},{4,5},{5,4},{6,7},{7,6},{8,9},{9,8},{10,11... | collective-permute-start | bytes 245768 | tf_op jit(solution)/shard_map/ppermute | solution.py:20
  38.4 2.9 %collective-permute-start.2 = (f32[80,128]{1,0:T(8,128)S(1)}, f32[80,128]{1,0:T(8,128)S(1)}, u32[]{:S(2)}, u32[]{:S(2)}) collective-permute-start(f32[80,128]{1,0:T(8,128)S(1)} %dynamic-slice_bitcast_fusion), channel_id=1, source_target_pairs={{0,16},{16,0},{32,48},{48,32},{64,80},{80,64},{96,112},{112,96},{1... | collective-permute-start | bytes 122888 | tf_op jit(solution)/shard_map/ppermute | solution.py:20
  41.3 4.4 %collective-permute-start.3 = (f32[80,128]{1,0:T(8,128)S(1)}, f32[80,128]{1,0:T(8,128)S(1)}, u32[]{:S(2)}, u32[]{:S(2)}) collective-permute-start(f32[80,128]{1,0:T(8,128)S(1)} %bitcast_add_fusion), channel_id=1, source_target_pairs={{0,2},{1,3},{2,0},{3,1},{4,6},{5,7},{6,4},{7,5},{8,10},{9,11},{10,... | collective-permute-start | bytes 122888 | tf_op jit(solution)/shard_map/ppermute | solution.py:20
  45.7 7.9 %collective-permute-start.4 = (f32[80,128]{1,0:T(8,128)S(1)}, f32[80,128]{1,0:T(8,128)S(1)}, u32[]{:S(2)}, u32[]{:S(2)}) collective-permute-start(f32[80,128]{1,0:T(8,128)S(1)} %add.44), channel_id=1, source_target_pairs={{0,8},{1,9},{2,10},{3,11},{4,12},{5,13},{6,14},{7,15},{8,0},{9,1},... | collective-permute-start | bytes 122888 | tf_op jit(solution)/shard_map/ppermute | solution.py:20
  50.8 4.0 %collective-permute-start.5 = (f32[80,128]{1,0:T(8,128)S(1)}, f32[80,128]{1,0:T(8,128)S(1)}, u32[]{:S(2)}, u32[]{:S(2)}) collective-permute-start(f32[80,128]{1,0:T(8,128)S(1)} %add.44), channel_id=1, source_target_pairs={{0,4},{1,5},{2,6},{3,7},{4,0},{5,1},{6,2},{7,3},{8,12},{9,13},{10,... | collective-permute-start | bytes 122888 | tf_op jit(solution)/shard_map/ppermute | solution.py:20
  52.3 5.5 %collective-permute-start.6 = (f32[80,128]{1,0:T(8,128)S(1)}, f32[80,128]{1,0:T(8,128)S(1)}, u32[]{:S(2)}, u32[]{:S(2)}) collective-permute-start(f32[80,128]{1,0:T(8,128)S(1)} %add.44), channel_id=1, source_target_pairs={{0,12},{1,13},{2,14},{3,15},{4,8},{5,9},{6,10},{7,11},{8,4},{9,5},... | collective-permute-start | bytes 122888 | tf_op jit(solution)/shard_map/ppermute | solution.py:20
  57.8 6.1 %collective-permute-start.7 = (f32[80,128]{1,0:T(8,128)S(1)}, f32[80,128]{1,0:T(8,128)S(1)}, u32[]{:S(2)}, u32[]{:S(2)}) collective-permute-start(f32[80,128]{1,0:T(8,128)S(1)} %add_add_fusion.mine_ref), channel_id=1, source_target_pairs={{0,1},{1,0},{2,3},{3,2},{4,5},{5,4},{6,7},{7,6},{8,9},{9,8},{10,11... | collective-permute-start | bytes 122888 | tf_op jit(solution)/shard_map/ppermute | solution.py:20
  62.0 2.9 %collective-permute-start.8 = (f32[80,128]{1,0:T(8,128)S(1)}, f32[80,128]{1,0:T(8,128)S(1)}, u32[]{:S(2)}, u32[]{:S(2)}) collective-permute-start(f32[80,128]{1,0:T(8,128)S(1)} %add_add_fusion.mine_ref), channel_id=1, source_target_pairs={{0,16},{16,0},{32,48},{48,32},{64,80},{80,64},{96,112},{112,96},{1... | collective-permute-start | bytes 122888 | tf_op jit(solution)/shard_map/ppermute | solution.py:20
  62.2 4.0 %collective-permute-start.9 = (f32[80,128]{1,0:T(8,128)S(1)}, f32[80,128]{1,0:T(8,128)S(1)}, u32[]{:S(2)}, u32[]{:S(2)}) collective-permute-start(f32[80,128]{1,0:T(8,128)S(1)} %add_add_fusion.mine_ref), channel_id=1, source_target_pairs={{0,17},{1,16},{2,19},{3,18},{4,21},{5,20},{6,23},{7,22},{8,25},{9,... | collective-permute-start | bytes 122888 | tf_op jit(solution)/shard_map/ppermute | solution.py:372

commit v12 on v9

--- a/solution.py
+++ b/solution.py
@@ -365,12 +365,9 @@
 
     everyone = range(chan_count * tm_count)
     across = [(i, i ^ (tm_count + 1)) for i in everyone]
-    four = (
-        quarter,
-        swapped(quarter, "tm", 1),
-        swapped(quarter, "chan", 1),
-        lax.ppermute(quarter, ("chan", "tm"), across),
-    )
+    both = lax.ppermute(quarter, ("chan", "tm"), across)
+    beside = swapped(quarter, "chan", 1)
+    four = (quarter, swapped(quarter, "tm", 1), beside, both)
     start = lax.dynamic_index_in_dim(start_basis, place // 2, 0, False)
     result = denoised_band(jnp.stack([core, half]), four, start, decimated)
 

time: 97.6 us -> 97.6 us (level)
  no operation moved by 1% of the time
where the time goes in v12:
time: 97.6 us; the launch traced here: 97.3 us
  waiting for transfers between devices  29.5 us (30%)
  starting transfers between devices  29 us (30%)
  blocking collectives  20.3 us (21%)
  Pallas kernels  14.1 us (14%)
  local copies, waits for them, and re-layouts  2.57 us (3%)
  other arithmetic  1.63 us (2%)
    all_to_all x1, blocking collectives, shards(): result = lax.all_to_all(result, 'chan', 0, 0, tiled=True)  20.3 us
    all_to_all x1, waiting for transfers between devices, shards(): lax.all_to_all(message, 'chan', 0, 0, tiled=True).astype(jnp.float32)  17.9 us
    ppermute x8, starting transfers between devices, swapped(): return lax.ppermute(block, axis, route)  15.8 us
    ppermute x8, waiting for transfers between devices, swapped(): return lax.ppermute(block, axis, route)  10.3 us
    pallas_call x1, Pallas kernels, denoised_band(): pl.pallas_call(refine_kernel, in_specs=[pl.BlockSpec(memory_space=pltpu.S...  8.45 us
    all_to_all x1, starting transfers between devices, shards(): lax.all_to_all(message, 'chan', 0, 0, tiled=True).astype(jnp.float32)  6.75 us
    ppermute x1, starting transfers between devices, shards(): lax.ppermute(rim_piece, 'tm', [(i, i + 1) for i in range(tm_count - 1)])  4.92 us
    pallas_call x1, Pallas kernels, restored(): pl.pallas_call(restore_kernel, grid=(steps,), in_specs=[pl.BlockSpec((sou...  2.03 us
  transfers between devices with their start and end apart: 11, of which 8 were waited for; matrix products, arithmetic and copies ran while one was open for 1% of the time, Pallas kernels for 0%

profile of v12, /device:TPU:1, one launch (start us, length us, event | category | flops | bytes accessed | tf_op | source)
XLA Modules:
  0.0 97.3 jit_solution(17314629413640959404)
XLA Ops:
  0.0 0.0 copy-start
  0.0 0.7 slice.3
  0.7 4.9 %collective-permute-start = (bf16[16,128]{1,0:T(8,128)(2,1)S(1)}, bf16[16,128]{1,0:T(8,128)(2,1)S(1)}, u32[]{:S(2)}, u32[]{:S(2)}) collective-permute-start(bf16[16,128]{1,0:T(8,128)(2,1)S(1)} %slice.3), channel_id=1, source_target_pairs={{0,1},{1,2},{2,3},{3,4},{4,5},{5,6},{6,7},{7,8},{8,9},{9,10},{10,1... | collective-permute-start | bytes 12296 | tf_op jit(solution)/shard_map/ppermute | solution.py:352
  5.7 0.7 copy.5.taps_ref
  6.4 0.2 filter_table.1.table_ref
  6.5 0.0 collective-permute-done.before_ref
  6.6 0.0 copy-start.1
  6.6 1.0 %copy-done.1 = bf16[16,16384]{1,0:T(8,128)(2,1)S(1)} copy-done((bf16[16,16384]{1,0:T(8,128)(2,1)S(1)}, bf16[16,16384]{1,0:T(8,128)(2,1)}, u32[]{:S(2)}) %copy-start.1) | copy-done | bytes 524312
  7.6 1.5 %filtered.1 = f32[16,16,2176]{2,1,0:T(8,128)S(1)} custom-call(bf16[16,16384]{1,0:T(8,128)(2,1)S(1)} %copy-done.1, bf16[16,128]{1,0:T(8,128)(2,1)S(1)} %collective-permute-done.before_ref, bf16[1024,640]{1,0:T(8,128)(2,1)S(1)} %filter_table.1.table_ref), custom_call_target="tpu_custom_call" | custom-call | tf_op jit(solution)/shard_map/filtered/pallas_call | solution.py:127
  9.1 1.1 %convert_element_type.15 = f16[16,16,2176]{2,1,0:T(8,128)(2,1)} convert(f32[16,16,2176]{2,1,0:T(8,128)S(1)} %filtered.1) | non-fusion elementwise | flops 557056 | bytes 3342336 | tf_op jit(solution)/shard_map/convert_element_type | solution.py:355
  10.2 6.8 %all-to-all-start = ((f16[16,16,2176]{2,1,0:T(8,128)(2,1)}), f16[16,16,2176]{2,1,0:T(8,128)(2,1)S(1)}, u32[]{:S(2)}, u32[]{:S(2)}) async-start(f16[16,16,2176]{2,1,0:T(8,128)(2,1)} %convert_element_type.15), calls=%async_computation | async-start | bytes 2228224 | tf_op jit(solution)/shard_map/all_to_all | solution.py:356
  17.0 17.9 %all-to-all-done = f16[16,16,2176]{2,1,0:T(8,128)(2,1)S(1)} async-done(((f16[16,16,2176]{2,1,0:T(8,128)(2,1)}), f16[16,16,2176]{2,1,0:T(8,128)(2,1)S(1)}, u32[]{:S(2)}, u32[]{:S(2)}) %all-to-all-start) | async-done | bytes 1114144 | tf_op jit(solution)/shard_map/all_to_all | solution.py:356
  34.9 0.1 convert_element_type.16.message_ref
  35.0 2.0 %band_gram.1 = (f32[160,128]{1,0:T(8,128)S(1)}, f32[160,128]{1,0:T(8,128)S(1)}, f32[256,2048]{1,0:T(8,128)S(1)}) custom-call(s32[1]{0:T(128)} %bitcast.core_ref, f32[16,16,2176]{2,1,0:T(8,128)S(1)} %convert_element_type.16.message_ref), custom_call_target="tpu_custom_call" | custom-call | tf_op jit(solution)/shard_map/band_gram/pallas_call | solution.py:162
  37.0 0.1 collective-permute-start.1
  37.1 1.2 %collective-permute-done.1 = f32[160,128]{1,0:T(8,128)S(1)} collective-permute-done((f32[160,128]{1,0:T(8,128)S(1)}, f32[160,128]{1,0:T(8,128)S(1)}, u32[]{:S(2)}, u32[]{:S(2)}) %collective-permute-start.1) | collective-permute-done | bytes 81952 | tf_op jit(solution)/shard_map/ppermute | solution.py:20
  38.4 0.4 collective-permute-start.2
  38.8 2.6 %collective-permute-done.2 = f32[80,128]{1,0:T(8,128)S(1)} collective-permute-done((f32[80,128]{1,0:T(8,128)S(1)}, f32[80,128]{1,0:T(8,128)S(1)}, u32[]{:S(2)}, u32[]{:S(2)}) %collective-permute-start.2) | collective-permute-done | bytes 40992 | tf_op jit(solution)/shard_map/ppermute | solution.py:20
  41.3 3.0 %collective-permute-start.3 = (f32[80,128]{1,0:T(8,128)S(1)}, f32[80,128]{1,0:T(8,128)S(1)}, u32[]{:S(2)}, u32[]{:S(2)}) collective-permute-start(f32[80,128]{1,0:T(8,128)S(1)} %bitcast_add_fusion), channel_id=1, source_target_pairs={{0,2},{1,3},{2,0},{3,1},{4,6},{5,7},{6,4},{7,5},{8,10},{9,11},{10,... | collective-permute-start | bytes 122888 | tf_op jit(solution)/shard_map/ppermute | solution.py:20
  44.3 1.4 %collective-permute-done.3 = f32[80,128]{1,0:T(8,128)S(1)} collective-permute-done((f32[80,128]{1,0:T(8,128)S(1)}, f32[80,128]{1,0:T(8,128)S(1)}, u32[]{:S(2)}, u32[]{:S(2)}) %collective-permute-start.3) | collective-permute-done | bytes 40992 | tf_op jit(solution)/shard_map/ppermute | solution.py:20
  45.7 5.1 %collective-permute-start.4 = (f32[80,128]{1,0:T(8,128)S(1)}, f32[80,128]{1,0:T(8,128)S(1)}, u32[]{:S(2)}, u32[]{:S(2)}) collective-permute-start(f32[80,128]{1,0:T(8,128)S(1)} %add.44), channel_id=1, source_target_pairs={{0,8},{1,9},{2,10},{3,11},{4,12},{5,13},{6,14},{7,15},{8,0},{9,1},... | collective-permute-start | bytes 122888 | tf_op jit(solution)/shard_map/ppermute | solution.py:20
  50.8 1.5 %collective-permute-start.5 = (f32[80,128]{1,0:T(8,128)S(1)}, f32[80,128]{1,0:T(8,128)S(1)}, u32[]{:S(2)}, u32[]{:S(2)}) collective-permute-start(f32[80,128]{1,0:T(8,128)S(1)} %add.44), channel_id=1, source_target_pairs={{0,4},{1,5},{2,6},{3,7},{4,0},{5,1},{6,2},{7,3},{8,12},{9,13},{10,... | collective-permute-start | bytes 122888 | tf_op jit(solution)/shard_map/ppermute | solution.py:20
  52.3 1.3 %collective-permute-start.6 = (f32[80,128]{1,0:T(8,128)S(1)}, f32[80,128]{1,0:T(8,128)S(1)}, u32[]{:S(2)}, u32[]{:S(2)}) collective-permute-start(f32[80,128]{1,0:T(8,128)S(1)} %add.44), channel_id=1, source_target_pairs={{0,12},{1,13},{2,14},{3,15},{4,8},{5,9},{6,10},{7,11},{8,4},{9,5},... | collective-permute-start | bytes 122888 | tf_op jit(solution)/shard_map/ppermute | solution.py:20
  53.6 0.0 copy-done
  53.6 0.0 collective-permute-done.4
  53.6 1.2 %collective-permute-done.5 = f32[80,128]{1,0:T(8,128)S(1)} collective-permute-done((f32[80,128]{1,0:T(8,128)S(1)}, f32[80,128]{1,0:T(8,128)S(1)}, u32[]{:S(2)}, u32[]{:S(2)}) %collective-permute-start.5) | collective-permute-done | bytes 40992 | tf_op jit(solution)/shard_map/ppermute | solution.py:20
  54.9 2.9 %collective-permute-done.6 = f32[80,128]{1,0:T(8,128)S(1)} collective-permute-done((f32[80,128]{1,0:T(8,128)S(1)}, f32[80,128]{1,0:T(8,128)S(1)}, u32[]{:S(2)}, u32[]{:S(2)}) %collective-permute-start.6) | collective-permute-done | bytes 40992 | tf_op jit(solution)/shard_map/ppermute | solution.py:20
  57.8 4.2 %collective-permute-start.7 = (f32[80,128]{1,0:T(8,128)S(1)}, f32[80,128]{1,0:T(8,128)S(1)}, u32[]{:S(2)}, u32[]{:S(2)}) collective-permute-start(f32[80,128]{1,0:T(8,128)S(1)} %add_add_fusion.mine_ref), channel_id=1, source_target_pairs={{0,1},{1,0},{2,3},{3,2},{4,5},{5,4},{6,7},{7,6},{8,9},{9,8},{10,11... | collective-permute-start | bytes 122888 | tf_op jit(solution)/shard_map/ppermute | solution.py:20
  62.0 0.2 collective-permute-start.8
  62.2 1.5 %collective-permute-start.9 = (f32[80,128]{1,0:T(8,128)S(1)}, f32[80,128]{1,0:T(8,128)S(1)}, u32[]{:S(2)}, u32[]{:S(2)}) collective-permute-start(f32[80,128]{1,0:T(8,128)S(1)} %add_add_fusion.mine_ref), channel_id=1, source_target_pairs={{0,17},{1,16},{2,19},{3,18},{4,21},{5,20},{6,23},{7,22},{8,25},{9,... | collective-permute-start | bytes 122888 | tf_op jit(solution)/shard_map/ppermute | solution.py:368
  63.7 0.1 pad_add_fusion.place_ref
  63.8 0.1 copy.6
  63.9 0.0 collective-permute-done.7.core_ref
  63.9 1.0 collective-permute-done.8.chan_ref
  64.9 1.3 %collective-permute-done.9.both_ref = f32[80,128]{1,0:T(8,128)S(1)} collective-permute-done((f32[80,128]{1,0:T(8,128)S(1)}, f32[80,128]{1,0:T(8,128)S(1)}, u32[]{:S(2)}, u32[]{:S(2)}) %collective-permute-start.9) | collective-permute-done | bytes 40992 | tf_op jit(solution)/shard_map/ppermute | solution.py:368
  66.2 8.5 %denoised_band.1 = f32[256,2176]{1,0:T(8,128)S(1)} custom-call(s32[2]{0:T(128)S(1)} %pad_add_fusion.place_ref, f32[80,128]{1,0:T(8,128)S(1)} %add_add_fusion.mine_ref, f32[80,128]{1,0:T(8,128)S(1)} %collective-permute-done.7.core_ref, f32[80,128]{1,0:T(8,128)S(1)} %collective-permute-done.8.chan_ref, f32[80,128]{1,0:T(8,128)S(1)} %collective-permute-done.9.both_ref, ...), custom_call_target="tpu_custom_call" | custom-call | tf_op jit(solution)/shard_map/denoised_band/pallas_call | solution.py:308
  74.7 0.1 convert_element_type.17
  74.8 20.3 %all_to_all.10 = f16[16,16,2176]{2,1,0:T(8,128)(2,1)S(1)} all-to-all(f16[16,16,2176]{2,1,0:T(8,128)(2,1)S(1)} %bitcast.11), channel_id=1, replica_groups=mesh['chan'=16,'tm'=16] {'chan'}, dimensions={0} | all-to-all | bytes 2228224 | tf_op jit(solution)/shard_map/all_to_all | solution.py:375
  95.1 0.1 convert_element_type.19.message_ref
  95.3 2.0 %restored.1 = f32[8,16,4096]{2,1,0:T(8,128)} custom-call(f32[16,16,2176]{2,1,0:T(8,128)S(1)} %convert_element_type.19.message_ref), custom_call_target="tpu_custom_call" | custom-call | tf_op jit(solution)/shard_map/restored/pallas_call | solution.py:334
  (6 shorter events, 0.1 us)
Async XLA Ops:
  0.0 53.6 %copy-start = (f32[8,256,32]{1,2,0:T(8,128)S(1)}, f32[8,256,32]{1,2,0:T(8,128)}, u32[]{:S(2)}) copy-start(f32[8,256,32]{1,2,0:T(8,128)} %param.5) | copy-start | bytes 786436
  0.7 5.8 %collective-permute-start = (bf16[16,128]{1,0:T(8,128)(2,1)S(1)}, bf16[16,128]{1,0:T(8,128)(2,1)S(1)}, u32[]{:S(2)}, u32[]{:S(2)}) collective-permute-start(bf16[16,128]{1,0:T(8,128)(2,1)S(1)} %slice.3), channel_id=1, source_target_pairs={{0,1},{1,2},{2,3},{3,4},{4,5},{5,6},{6,7},{7,8},{8,9},{9,10},{10,1... | collective-permute-start | bytes 12296 | tf_op jit(solution)/shard_map/ppermute | solution.py:352
  6.6 1.0 %copy-start.1 = (bf16[16,16384]{1,0:T(8,128)(2,1)S(1)}, bf16[16,16384]{1,0:T(8,128)(2,1)}, u32[]{:S(2)}) copy-start(bf16[16,16384]{1,0:T(8,128)(2,1)} %raw_ref.1) | copy-start | bytes 1572868
  10.2 24.6 %all-to-all-start = ((f16[16,16,2176]{2,1,0:T(8,128)(2,1)}), f16[16,16,2176]{2,1,0:T(8,128)(2,1)S(1)}, u32[]{:S(2)}, u32[]{:S(2)}) async-start(f16[16,16,2176]{2,1,0:T(8,128)(2,1)} %convert_element_type.15), calls=%async_computation | async-start | bytes 2228224 | tf_op jit(solution)/shard_map/all_to_all | solution.py:356
  37.0 1.4 %collective-permute-start.1 = (f32[160,128]{1,0:T(8,128)S(1)}, f32[160,128]{1,0:T(8,128)S(1)}, u32[]{:S(2)}, u32[]{:S(2)}) collective-permute-start(f32[160,128]{1,0:T(8,128)S(1)} %get-tuple-element.9), channel_id=1, source_target_pairs={{0,1},{1,0},{2,3},{3,2},{4,5},{5,4},{6,7},{7,6},{8,9},{9,8},{10,11... | collective-permute-start | bytes 245768 | tf_op jit(solution)/shard_map/ppermute | solution.py:20
  38.4 2.9 %collective-permute-start.2 = (f32[80,128]{1,0:T(8,128)S(1)}, f32[80,128]{1,0:T(8,128)S(1)}, u32[]{:S(2)}, u32[]{:S(2)}) collective-permute-start(f32[80,128]{1,0:T(8,128)S(1)} %dynamic-slice_bitcast_fusion), channel_id=1, source_target_pairs={{0,16},{16,0},{32,48},{48,32},{64,80},{80,64},{96,112},{112,96},{1... | collective-permute-start | bytes 122888 | tf_op jit(solution)/shard_map/ppermute | solution.py:20
  41.3 4.4 %collective-permute-start.3 = (f32[80,128]{1,0:T(8,128)S(1)}, f32[80,128]{1,0:T(8,128)S(1)}, u32[]{:S(2)}, u32[]{:S(2)}) collective-permute-start(f32[80,128]{1,0:T(8,128)S(1)} %bitcast_add_fusion), channel_id=1, source_target_pairs={{0,2},{1,3},{2,0},{3,1},{4,6},{5,7},{6,4},{7,5},{8,10},{9,11},{10,... | collective-permute-start | bytes 122888 | tf_op jit(solution)/shard_map/ppermute | solution.py:20
  45.7 7.9 %collective-permute-start.4 = (f32[80,128]{1,0:T(8,128)S(1)}, f32[80,128]{1,0:T(8,128)S(1)}, u32[]{:S(2)}, u32[]{:S(2)}) collective-permute-start(f32[80,128]{1,0:T(8,128)S(1)} %add.44), channel_id=1, source_target_pairs={{0,8},{1,9},{2,10},{3,11},{4,12},{5,13},{6,14},{7,15},{8,0},{9,1},... | collective-permute-start | bytes 122888 | tf_op jit(solution)/shard_map/ppermute | solution.py:20
  50.8 4.0 %collective-permute-start.5 = (f32[80,128]{1,0:T(8,128)S(1)}, f32[80,128]{1,0:T(8,128)S(1)}, u32[]{:S(2)}, u32[]{:S(2)}) collective-permute-start(f32[80,128]{1,0:T(8,128)S(1)} %add.44), channel_id=1, source_target_pairs={{0,4},{1,5},{2,6},{3,7},{4,0},{5,1},{6,2},{7,3},{8,12},{9,13},{10,... | collective-permute-start | bytes 122888 | tf_op jit(solution)/shard_map/ppermute | solution.py:20
  52.3 5.5 %collective-permute-start.6 = (f32[80,128]{1,0:T(8,128)S(1)}, f32[80,128]{1,0:T(8,128)S(1)}, u32[]{:S(2)}, u32[]{:S(2)}) collective-permute-start(f32[80,128]{1,0:T(8,128)S(1)} %add.44), channel_id=1, source_target_pairs={{0,12},{1,13},{2,14},{3,15},{4,8},{5,9},{6,10},{7,11},{8,4},{9,5},... | collective-permute-start | bytes 122888 | tf_op jit(solution)/shard_map/ppermute | solution.py:20
  57.8 6.1 %collective-permute-start.7 = (f32[80,128]{1,0:T(8,128)S(1)}, f32[80,128]{1,0:T(8,128)S(1)}, u32[]{:S(2)}, u32[]{:S(2)}) collective-permute-start(f32[80,128]{1,0:T(8,128)S(1)} %add_add_fusion.mine_ref), channel_id=1, source_target_pairs={{0,1},{1,0},{2,3},{3,2},{4,5},{5,4},{6,7},{7,6},{8,9},{9,8},{10,11... | collective-permute-start | bytes 122888 | tf_op jit(solution)/shard_map/ppermute | solution.py:20
  62.0 2.9 %collective-permute-start.8 = (f32[80,128]{1,0:T(8,128)S(1)}, f32[80,128]{1,0:T(8,128)S(1)}, u32[]{:S(2)}, u32[]{:S(2)}) collective-permute-start(f32[80,128]{1,0:T(8,128)S(1)} %add_add_fusion.mine_ref), channel_id=1, source_target_pairs={{0,16},{16,0},{32,48},{48,32},{64,80},{80,64},{96,112},{112,96},{1... | collective-permute-start | bytes 122888 | tf_op jit(solution)/shard_map/ppermute | solution.py:20
  62.2 4.0 %collective-permute-start.9 = (f32[80,128]{1,0:T(8,128)S(1)}, f32[80,128]{1,0:T(8,128)S(1)}, u32[]{:S(2)}, u32[]{:S(2)}) collective-permute-start(f32[80,128]{1,0:T(8,128)S(1)} %add_add_fusion.mine_ref), channel_id=1, source_target_pairs={{0,17},{1,16},{2,19},{3,18},{4,21},{5,20},{6,23},{7,22},{8,25},{9,... | collective-permute-start | bytes 122888 | tf_op jit(solution)/shard_map/ppermute | solution.py:368
